TPU v7x, 128 devices: a whole 4x4x4 slice. The times are simulated.
128 devices in a mesh: expert: 32 (over z, x, core), head: 4 (over y).
Axes of the slice: x: 4, y: 4, z: 4, core: 2. Of those that a mesh axis runs over, the one named last changes fastest.
Arguments:
- tokens: bfloat16 [32768, 1024], P(('expert', 'head')), may hold values from -6 to 6
- cotangent: bfloat16 [32768, 1024], P(('expert', 'head')), may hold values from -6 to 6
- routes: int32 [32768, 8], P(('expert', 'head')), may hold values from 0 to 31, all different within a row; in each aligned block of 256 rows (0 to 255, 256 to 511, ...) at most 96 rows name the same one
- lengths: int32 [32, 8], P('expert'), may hold values from 1 to 896, as said below
- gain_attn: float32 [1024], replicated, may hold values from 0.5 to 1.5
- w_query: bfloat16 [1024, 1024], P(None, 'head'), may hold values from -0.1875 to 0.1875
- w_key: bfloat16 [1024, 512], P(None, 'head'), may hold values from -0.1875 to 0.1875
- w_value: bfloat16 [1024, 512], P(None, 'head'), may hold values from -0.1875 to 0.1875
- w_output: bfloat16 [1024, 1024], P('head'), may hold values from -1.5 to 1.5
- gain_mix: float32 [1024], replicated, may hold values from 0.5 to 1.5
- w_router: float32 [1024, 32], replicated, may hold values from -0.09375 to 0.09375
- gate_weight: bfloat16 [32, 1024, 512], P('expert'), may hold values from -0.1875 to 0.1875
- up_weight: bfloat16 [32, 1024, 512], P('expert'), may hold values from -0.1875 to 0.1875
- down_weight: bfloat16 [32, 512, 1024], P('expert'), may hold values from -1.5 to 1.5
Outputs:
- output: bfloat16 [32768, 1024], P(('expert', 'head'))
- grad_tokens: float32 [32768, 1024], P(('expert', 'head'))
- grad_gain_attn: float32 [1024], replicated
- grad_w_query: float32 [1024, 1024], P(None, 'head')
- grad_w_key: float32 [1024, 512], P(None, 'head')
- grad_w_value: float32 [1024, 512], P(None, 'head')
- grad_w_output: float32 [1024, 1024], P('head')
- grad_gain_mix: float32 [1024], replicated
- grad_w_router: float32 [1024, 32], replicated
- grad_w_gate: float32 [32, 1024, 512], P('expert')
- grad_w_up: float32 [32, 1024, 512], P('expert')
- grad_w_down: float32 [32, 512, 1024], P('expert')
Inputs may be any that keep to these rules, and one draw needn't show every extreme that they name: `routes`: each row names 8 different experts. Among the 256 rows of one device no expert is named by more than 96 rows, a bound that some block reaches of them. Row g lists the lengths of the 8 sequences packed in order into the 1024 tokens of group g; they sum to 1024, and one of them has length 896.
All inputs are finite; a program needn't handle non-finite values.
Results may differ from a plain program's by a relative error of at most 0.03.
Values may be sent and summed in bfloat16 or wider, within the bound.
No kernel may reach another device: no remote copies, remote signals or barrier semaphores. Data moves between devices by JAX's collectives and lax.ppermute only.
A program may use at most 256 MiB of HBM per device.

v0:
```python
import jax
import jax.numpy as jnp
from jax import lax
from jax.sharding import PartitionSpec as P

HEAD_DIM = 64


eps_norm = 1e-06
rope_base = 10000.0
mask_fill = -1000000000.0


def laid_out(tiles, dim):
    tiles = jnp.moveaxis(tiles, 0, dim)
    shape = tiles.shape
    return tiles.reshape(*shape[:dim], shape[dim] * shape[dim + 1], *shape[dim + 2 :])


def sent_to_all(array, axis):
    length = lax.axis_size(axis)
    return lax.all_to_all(
        jnp.broadcast_to(array[None], (length, *array.shape)), axis, 0, 0, tiled=True
    )


def gather_directly(array, axis, dim):
    return laid_out(sent_to_all(array, axis), dim)


def cut_along(array, dim, length):
    shape = array.shape
    tiles = array.reshape(*shape[:dim], length, shape[dim] // length, *shape[dim + 1 :])
    return jnp.moveaxis(tiles, dim, 0)


def sum_at_owner(array, axis, dim):
    tiles = cut_along(array, dim, lax.axis_size(axis))
    arrived = lax.all_to_all(tiles, axis, split_axis=0, concat_axis=0, tiled=True)
    return arrived.astype(jnp.float32).sum(axis=0)


def rms_scale(values, gain_vec):
    return (
        values * lax.rsqrt(jnp.mean(values * values, axis=-1, keepdims=True) + eps_norm) * gain_vec
    )


def rotate(values, position):
    half_dim = values.shape[-1] // 2
    frequency = rope_base ** (-2.0 * jnp.arange(half_dim, dtype=jnp.float32) / values.shape[-1])
    angles = position.astype(jnp.float32)[:, None] * frequency[None, :]
    cosine = jnp.cos(angles)[:, None, :]
    sine_vals = jnp.sin(angles)[:, None, :]
    front_half = values[..., :half_dim]
    back_half = values[..., half_dim:]
    return jnp.concatenate(
        [front_half * cosine - back_half * sine_vals, back_half * cosine + front_half * sine_vals],
        axis=-1,
    )


def doc_layout(seq_lengths, group_rows):
    seq_ends = jnp.cumsum(seq_lengths, dtype=jnp.int32)
    starts = seq_ends - seq_lengths
    row_index = jnp.arange(group_rows, dtype=jnp.int32)
    segment = jnp.sum(
        (row_index[:, None] >= seq_ends[None, :]).astype(jnp.int32), axis=1, dtype=jnp.int32
    )
    in_seq = segment[:, None] == jnp.arange(seq_lengths.shape[0], dtype=jnp.int32)[None, :]
    beginning = jnp.sum(jnp.where(in_seq, starts[None, :], 0), axis=1, dtype=jnp.int32)
    return (segment, row_index - beginning, row_index)


def body(
    tokens,
    cotangent,
    routes,
    lengths,
    gain_attn,
    w_query,
    w_key,
    w_value,
    w_output,
    gain_mix,
    w_router,
    gate_weight,
    up_weight,
    down_weight,
):
    row_count, model_width = tokens.shape
    pick_count = routes.shape[1]
    head_count = lax.axis_size("head")
    owner_count = lax.axis_size("expert")
    group_rows = row_count * head_count
    query_heads = w_query.shape[1] // HEAD_DIM
    key_heads = w_key.shape[1] // HEAD_DIM
    repeat_count = query_heads // key_heads
    score_scale = HEAD_DIM ** (-0.5)
    local_experts = gate_weight.shape[0]
    expert_count = local_experts * owner_count
    capacity = min(row_count, 3 * row_count * pick_count // (2 * expert_count))
    segment, position, row_index = doc_layout(lengths[0], group_rows)
    allowed = (segment[:, None] == segment[None, :]) & (row_index[None, :] <= row_index[:, None])
    resid = tokens.astype(jnp.float32)
    normed_first = rms_scale(resid, gain_attn).astype(jnp.bfloat16)
    full_rows = gather_directly(normed_first, "head", 0)
    query_raw = jnp.dot(full_rows, w_query, preferred_element_type=jnp.float32).reshape(
        group_rows, query_heads, HEAD_DIM
    )
    key_raw = jnp.dot(full_rows, w_key, preferred_element_type=jnp.float32).reshape(
        group_rows, key_heads, HEAD_DIM
    )
    value_low = (
        jnp.dot(full_rows, w_value, preferred_element_type=jnp.float32)
        .astype(jnp.bfloat16)
        .reshape(group_rows, key_heads, HEAD_DIM)
    )
    query_low = (
        rotate(query_raw, position)
        .astype(jnp.bfloat16)
        .reshape(group_rows, key_heads, repeat_count, HEAD_DIM)
    )
    key_low = rotate(key_raw, position).astype(jnp.bfloat16)

    def masked_scores():
        product = (
            jnp.einsum("gkrd,skd->krgs", query_low, key_low, preferred_element_type=jnp.float32)
            * score_scale
        )
        return jnp.where(allowed, product, mask_fill)

    scores = masked_scores()
    row_peak = jnp.max(scores, axis=-1, keepdims=True)
    lifted = jnp.exp(scores - row_peak)
    row_total = jnp.sum(lifted, axis=-1, keepdims=True)
    log_total = row_peak + jnp.log(row_total)
    weights_low = (lifted / row_total).astype(jnp.bfloat16)
    mixed_low = (
        jnp.einsum("krgs,skd->gkrd", weights_low, value_low, preferred_element_type=jnp.float32)
        .reshape(group_rows, query_heads * HEAD_DIM)
        .astype(jnp.bfloat16)
    )
    attn_out = sum_at_owner(
        jnp.dot(mixed_low, w_output, preferred_element_type=jnp.float32).astype(jnp.bfloat16),
        "head",
        0,
    )
    hidden_first = resid + attn_out
    normed_second = rms_scale(hidden_first, gain_mix)
    logits = jnp.dot(normed_second, w_router)
    gates = jax.nn.softmax(jnp.take_along_axis(logits, routes, axis=1), axis=1)
    flat_routes = routes.reshape(-1)
    chosen = (flat_routes[:, None] == jnp.arange(expert_count, dtype=jnp.int32)[None, :]).astype(
        jnp.int32
    )
    rank_in = jnp.sum(
        (jnp.cumsum(chosen, axis=0, dtype=jnp.int32) - 1) * chosen, axis=1, dtype=jnp.int32
    )
    slot_index = flat_routes * capacity + rank_in
    source_row = jnp.arange(row_count * pick_count, dtype=jnp.int32) // pick_count
    holder = (
        jnp.full((expert_count * capacity,), row_count, jnp.int32).at[slot_index].set(source_row)
    )
    gate_slot = (
        jnp.zeros((expert_count * capacity,), jnp.float32).at[slot_index].set(gates.reshape(-1))
    )
    padded_in = jnp.concatenate(
        [normed_second.astype(jnp.bfloat16), jnp.zeros((1, model_width), jnp.bfloat16)], axis=0
    )
    outgoing = padded_in[holder].reshape(expert_count, capacity, model_width)
    arrived_tokens = lax.all_to_all(outgoing, "expert", split_axis=0, concat_axis=1, tiled=True)
    gate_portion = jnp.einsum(
        "tzs,tsp->tzp", arrived_tokens, gate_weight, preferred_element_type=jnp.float32
    )
    up_portion = jnp.einsum(
        "tzs,tsp->tzp", arrived_tokens, up_weight, preferred_element_type=jnp.float32
    )
    active_reduced = (jax.nn.silu(gate_portion) * up_portion).astype(jnp.bfloat16)
    produced = jnp.einsum(
        "cks,csz->ckz", active_reduced, down_weight, preferred_element_type=jnp.float32
    ).astype(jnp.bfloat16)
    returned = lax.all_to_all(produced, "expert", split_axis=1, concat_axis=0, tiled=True)
    back_rows = returned.reshape(expert_count * capacity, model_width)[slot_index].reshape(
        row_count, pick_count, model_width
    )
    mixture = jnp.sum(gates[:, :, None] * back_rows, axis=1)
    output = (hidden_first + mixture).astype(jnp.bfloat16)
    grad_out = cotangent.astype(jnp.float32)
    grad_gates = jnp.sum(back_rows * grad_out[:, None, :], axis=2)
    padded_grad = jnp.concatenate([grad_out, jnp.zeros((1, model_width), jnp.float32)], axis=0)
    grad_slots = (
        (padded_grad[holder] * gate_slot[:, None])
        .astype(jnp.bfloat16)
        .reshape(expert_count, capacity, model_width)
    )
    arrived_gradient = lax.all_to_all(grad_slots, "expert", split_axis=0, concat_axis=1, tiled=True)
    inputs_gathered, gate_at, up_at, active_value_at = (
        arrived_tokens,
        gate_portion,
        up_portion,
        active_reduced,
    )
    silu_at, silu_pull = jax.vjp(jax.nn.silu, gate_at)
    grad_active = jnp.einsum(
        "vas,ves->vae", arrived_gradient, down_weight, preferred_element_type=jnp.float32
    )
    grad_w_down = jnp.einsum(
        "zim,ziy->zmy", active_value_at, arrived_gradient, preferred_element_type=jnp.float32
    )
    up_preact_gradient = (grad_active * silu_at).astype(jnp.bfloat16)
    gate_preact_gradient = silu_pull(grad_active * up_at)[0].astype(jnp.bfloat16)
    grad_w_gate = jnp.einsum(
        "jns,jny->jsy", inputs_gathered, gate_preact_gradient, preferred_element_type=jnp.float32
    )
    grad_w_up = jnp.einsum(
        "jns,jny->jsy", inputs_gathered, up_preact_gradient, preferred_element_type=jnp.float32
    )
    grad_inputs = (
        jnp.einsum(
            "wkn,wsn->wks", gate_preact_gradient, gate_weight, preferred_element_type=jnp.float32
        )
        + jnp.einsum(
            "wkn,wsn->wks", up_preact_gradient, up_weight, preferred_element_type=jnp.float32
        )
    ).astype(jnp.bfloat16)
    grad_back = lax.all_to_all(grad_inputs, "expert", split_axis=1, concat_axis=0, tiled=True)
    grad_normed2 = jnp.sum(
        grad_back.reshape(expert_count * capacity, model_width)[slot_index].reshape(
            row_count, pick_count, model_width
        ),
        axis=1,
        dtype=jnp.float32,
    )
    grad_picked = gates * (grad_gates - jnp.sum(gates * grad_gates, axis=1, keepdims=True))
    grad_logits = jnp.sum(
        grad_picked[:, :, None]
        * chosen.reshape(row_count, pick_count, expert_count).astype(jnp.float32),
        axis=1,
    )
    grad_router_part = jnp.einsum("td,te->de", normed_second, grad_logits)
    grad_normed2 = grad_normed2 + jnp.einsum("te,de->td", grad_logits, w_router)
    _, second_pull = jax.vjp(rms_scale, hidden_first, gain_mix)
    grad_from_norm, grad_gain_mix_part = second_pull(grad_normed2)
    grad_hidden = grad_out + grad_from_norm
    grad_full = gather_directly(grad_hidden.astype(jnp.bfloat16), "head", 0)
    grad_w_output = jnp.einsum(
        "gm,gd->md", mixed_low, grad_full, preferred_element_type=jnp.float32
    )
    grad_mixed = (
        jnp.einsum("gd,md->gm", grad_full, w_output, preferred_element_type=jnp.float32)
        .astype(jnp.bfloat16)
        .reshape(group_rows, key_heads, repeat_count, HEAD_DIM)
    )
    attn_weights = jnp.exp(masked_scores() - log_total)
    grad_weights = jnp.einsum(
        "gkrd,skd->krgs", grad_mixed, value_low, preferred_element_type=jnp.float32
    )
    grad_value = jnp.einsum(
        "krgs,gkrd->skd",
        attn_weights.astype(jnp.bfloat16),
        grad_mixed,
        preferred_element_type=jnp.float32,
    )
    inner = jnp.sum(attn_weights * grad_weights, axis=-1, keepdims=True)
    grad_scores = (attn_weights * (grad_weights - inner)).astype(jnp.bfloat16)
    grad_query_rot = (
        jnp.einsum("krgs,skd->gkrd", grad_scores, key_low, preferred_element_type=jnp.float32)
        * score_scale
    )
    grad_key_rot = (
        jnp.einsum("krgs,gkrd->skd", grad_scores, query_low, preferred_element_type=jnp.float32)
        * score_scale
    )
    grad_query = (
        rotate(grad_query_rot.reshape(group_rows, query_heads, HEAD_DIM), -position)
        .reshape(group_rows, -1)
        .astype(jnp.bfloat16)
    )
    grad_key = rotate(grad_key_rot, -position).reshape(group_rows, -1).astype(jnp.bfloat16)
    grad_value_low = grad_value.reshape(group_rows, -1).astype(jnp.bfloat16)
    grad_w_query = jnp.einsum(
        "gd,gm->dm", full_rows, grad_query, preferred_element_type=jnp.float32
    )
    grad_w_key = jnp.einsum("gd,gm->dm", full_rows, grad_key, preferred_element_type=jnp.float32)
    grad_w_value = jnp.einsum(
        "gd,gm->dm", full_rows, grad_value_low, preferred_element_type=jnp.float32
    )
    total_term = jnp.einsum("gm,dm->gd", grad_query, w_query, preferred_element_type=jnp.float32)
    total_term = total_term + jnp.einsum(
        "gm,dm->gd", grad_key, w_key, preferred_element_type=jnp.float32
    )
    grad_normed1 = sum_at_owner(
        (
            total_term
            + jnp.einsum("gm,dm->gd", grad_value_low, w_value, preferred_element_type=jnp.float32)
        ).astype(jnp.bfloat16),
        "head",
        0,
    )
    _, first_pull = jax.vjp(rms_scale, resid, gain_attn)
    grad_from_first, grad_gain_attn_part = first_pull(grad_normed1)
    grad_tokens = grad_hidden + grad_from_first
    head_summed = (
        lax.psum(grad_w_gate.astype(jnp.bfloat16), "head").astype(jnp.float32),
        lax.psum(grad_w_up.astype(jnp.bfloat16), "head").astype(jnp.float32),
        lax.psum(grad_w_down.astype(jnp.bfloat16), "head").astype(jnp.float32),
        lax.psum(grad_router_part.astype(jnp.bfloat16), "head").astype(jnp.float32),
        lax.psum(grad_gain_attn_part.astype(jnp.bfloat16), "head").astype(jnp.float32),
        lax.psum(grad_gain_mix_part.astype(jnp.bfloat16), "head").astype(jnp.float32),
    )
    group_summed = (
        lax.psum(grad_w_query.astype(jnp.bfloat16), "expert").astype(jnp.float32),
        lax.psum(grad_w_key.astype(jnp.bfloat16), "expert").astype(jnp.float32),
        lax.psum(grad_w_value.astype(jnp.bfloat16), "expert").astype(jnp.float32),
        lax.psum(grad_w_output.astype(jnp.bfloat16), "expert").astype(jnp.float32),
        lax.psum(head_summed[3].astype(jnp.bfloat16), "expert").astype(jnp.float32),
        lax.psum(head_summed[4].astype(jnp.bfloat16), "expert").astype(jnp.float32),
        lax.psum(head_summed[5].astype(jnp.bfloat16), "expert").astype(jnp.float32),
    )
    return (
        output,
        grad_tokens,
        group_summed[5],
        group_summed[0],
        group_summed[1],
        group_summed[2],
        group_summed[3],
        group_summed[6],
        group_summed[4],
        head_summed[0],
        head_summed[1],
        head_summed[2],
    )


def solution(mesh):
    in_specs = (
        P(("expert", "head"), None),
        P(("expert", "head"), None),
        P(("expert", "head"), None),
        P("expert", None),
        P(),
        P(None, "head"),
        P(None, "head"),
        P(None, "head"),
        P("head", None),
        P(),
        P(),
        P("expert", None, None),
        P("expert", None, None),
        P("expert", None, None),
    )
    out_specs = (
        P(("expert", "head"), None),
        P(("expert", "head"), None),
        P(),
        P(None, "head"),
        P(None, "head"),
        P(None, "head"),
        P("head", None),
        P(),
        P(),
        P("expert", None, None),
        P("expert", None, None),
        P("expert", None, None),
    )
    return jax.shard_map(body, mesh=mesh, in_specs=in_specs, out_specs=out_specs, check_vma=False)
```

profile of v0, /device:TPU:4, one launch (start us, length us, event | category | flops | bytes accessed | tf_op | source)
XLA Modules:
  0.0 897.0 jit_solution(3409679828043066715)
XLA Ops:
  25.8 17.5 %all-to-all-done = bf16[4,256,1024]{2,1,0:T(8,128)(2,1)S(1)} async-done(((bf16[4,256,1024]{2,1,0:T(8,128)(2,1)}), bf16[4,256,1024]{2,1,0:T(8,128)(2,1)S(1)}, u32[]{:S(2)}, u32[]{:S(2)}) %all-to-all-start) | async-done | bytes 2097184 | tf_op jit(solution)/shard_map/all_to_all | solution.py:22
  78.7 9.1 %reduce-window.11 = s32[32,16,128]{2,1,0:T(8,128)S(1)} reduce-window(s32[32,16,128]{2,1,0:T(8,128)S(1)} %fusion.55, s32[]{:T(128)} %constant.41.clone.1), window={size=1x1x128 pad=0_0x0_0x127_0}, to_apply=%region_10.11 | reduce-window | flops 8323072 | bytes 524292 | tf_op jit(solution)/shard_map/reduce-window.1
  106.5 14.0 %gather_fusion = bf16[3072,1024]{1,0:T(8,128)(2,1)} fusion(bf16[257,1024]{1,0:T(8,128)(2,1)S(1)} %concatenate.29, s32[3072]{0:T(1024)S(1)} %fusion.56), kind=kCustom, calls=%fused_computation | custom fusion | bytes 12595200 | tf_op jit(solution)/shard_map/gather | solution.py:171
  120.5 8.5 all-to-all-start.2
  130.4 14.2 %gather_fusion.2 = f32[3072,1024]{1,0:T(8,128)} fusion(f32[257,1024]{1,0:T(8,128)S(1)} %concatenate.30, s32[3072]{0:T(1024)S(1)} %fusion.56), kind=kCustom, calls=%fused_computation.2 | custom fusion | bytes 25178112 | tf_op jit(solution)/shard_map/gather | solution.py:193
  144.9 16.8 %gather_fusion.4 = f32[2048]{0:T(1024)S(1)} fusion(f32[256,32]{0,1:T(8,128)S(1)} %fusion.48, s32[2048]{0:T(1024)S(1)} %reshape.550), kind=kCustom, calls=%fused_computation.4 | custom fusion | bytes 32768 | tf_op jit(solution)/shard_map/jit(take_along_axis)/gather | solution.py:152
  178.4 24.0 %all-to-all-done.2 = bf16[32,96,1024]{2,1,0:T(8,128)(2,1)} async-done(((bf16[32,96,1024]{2,1,0:T(8,128)(2,1)}), bf16[32,96,1024]{2,1,0:T(8,128)(2,1)}, u32[]{:S(2)}, u32[]{:S(2)}) %all-to-all-start.2) | async-done | bytes 6291488 | tf_op jit(solution)/shard_map/all_to_all | solution.py:172
  202.4 9.9 %all-to-all-start.4 = ((bf16[32,96,1024]{2,1,0:T(8,128)(2,1)}), bf16[32,96,1024]{2,1,0:T(8,128)(2,1)}, u32[]{:S(2)}, u32[]{:S(2)}) async-start(bf16[32,96,1024]{2,1,0:T(8,128)(2,1)} %multiply_convert_fusion), calls=%async_computation.4 | async-start | bytes 12582912 | tf_op jit(solution)/shard_map/all_to_all | solution.py:197
  212.4 9.2 %fusion.41 = f32[3072,512]{1,0:T(8,128)} fusion(bf16[3072,1024]{1,0:T(8,128)(2,1)} %bitcast.29, bf16[1,1024,512]{2,1,0:T(8,128)(2,1)} %param.26), kind=kOutput, calls=%fused_computation.87 | convolution fusion | flops 3221225472 | bytes 13631488 | tf_op jit(solution)/shard_map/tzs,tsp->tzp/dot_general | solution.py:176
  229.7 56.0 %all-to-all-done.4 = bf16[32,96,1024]{2,1,0:T(8,128)(2,1)} async-done(((bf16[32,96,1024]{2,1,0:T(8,128)(2,1)}), bf16[32,96,1024]{2,1,0:T(8,128)(2,1)}, u32[]{:S(2)}, u32[]{:S(2)}) %all-to-all-start.4) | async-done | bytes 6291488 | tf_op jit(solution)/shard_map/all_to_all | solution.py:197
  285.7 12.3 %multiply_convert_fusion.1 = (bf16[3072,512]{1,0:T(8,128)(2,1)}, bf16[3072,512]{1,0:T(8,128)(2,1)}, bf16[3072,512]{1,0:T(8,128)(2,1)S(1)}) fusion(f32[3072,512]{1,0:T(8,128)} %fusion.45, f32[3072,512]{1,0:T(8,128)} %fusion.41, bf16[3072,1024]{1,0:T(8,128)(2,1)} %bitcast.36, bf16[1,512,1024]{2,1,0:T(8,128)(2,1)S(1)} %copy-done), kind=kOutput, calls=%fused_computation.35 | convolution fusion | flops 3246391296 | bytes 29360128 | tf_op jit(solution)/shard_map/vas,ves->vae/dot_general | solution.py:205
  301.7 42.8 %copy.165 = bf16[1,3072,1024]{2,0,1:T(2,128)(2,1)} copy(bf16[1,3072,1024]{2,1,0:T(8,128)(2,1)S(1)} %convert_bitcast_fusion) | data formatting | bytes 12582912 | tf_op jit(solution)/shard_map/convert_element_type | solution.py:182
  344.9 37.9 %reduce.5 = bf16[3072,1024]{1,0:T(8,128)(2,1)} reduce(bf16[3072,1,1024]{2,1,0:T(2,128)(2,1)} %bitcast.206, bf16[]{:T(256)} %broadcast.353), dimensions={1}, to_apply=%bitcast.190.reduce_sub_computation | reduce | bytes 12582914
  382.8 12.9 %reshape.588 = bf16[32,2,49152]{2,1,0:T(2,128)(2,1)} reshape(bf16[3072,1024]{1,0:T(8,128)(2,1)} %reduce.5) | data formatting | bytes 12582912
  395.7 9.2 %all-to-all-start.3 = ((bf16[32,2,49152]{2,1,0:T(2,128)(2,1)}), bf16[32,2,49152]{2,1,0:T(2,128)(2,1)}, u32[]{:S(2)}, u32[]{:S(2)}) async-start(bf16[32,2,49152]{2,1,0:T(2,128)(2,1)} %reshape.588), calls=%async_computation.3 | async-start | bytes 12582912 | tf_op jit(solution)/shard_map/all_to_all | solution.py:183
  419.8 42.6 %copy.164 = bf16[1,3072,1024]{2,0,1:T(2,128)(2,1)} copy(bf16[1,3072,1024]{2,1,0:T(8,128)(2,1)S(1)} %fusion.14) | data formatting | bytes 12582912 | tf_op jit(solution)/shard_map/convert_element_type | solution.py:226
  462.5 37.8 %reduce.4 = bf16[3072,1024]{1,0:T(8,128)(2,1)} reduce(bf16[3072,1,1024]{2,1,0:T(2,128)(2,1)} %bitcast.207, bf16[]{:T(256)} %broadcast.353), dimensions={1}, to_apply=%bitcast.189.reduce_sub_computation | reduce | bytes 12582914
  500.2 12.9 %reshape.590 = bf16[32,2,49152]{2,1,0:T(2,128)(2,1)} reshape(bf16[3072,1024]{1,0:T(8,128)(2,1)} %reduce.4) | data formatting | bytes 12582912
  529.5 21.7 %reshape.589 = bf16[3072,1,1024]{2,1,0:T(2,128)(2,1)} reshape(bf16[32,2,49152]{2,1,0:T(2,128)(2,1)} %all-to-all-done.3) | data formatting | bytes 12582912
  551.2 9.8 %copy.163 = bf16[1,3072,1024]{2,1,0:T(8,128)(2,1)} copy(bf16[1,3072,1024]{2,0,1:T(2,128)(2,1)} %bitcast.204) | data formatting | bytes 12582912
  560.9 14.6 %gather_fusion.1 = bf16[2048,1024]{1,0:T(8,128)(2,1)} fusion(bf16[3072,1024]{1,0:T(8,128)(2,1)} %bitcast.197, s32[2048]{0:T(1024)S(1)} %broadcast_clamp_fusion), kind=kCustom, calls=%fused_computation.1 | custom fusion | bytes 8396800 | tf_op jit(solution)/shard_map/gather | solution.py:184
  581.7 12.8 %all-to-all-done.5 = bf16[32,2,49152]{2,1,0:T(2,128)(2,1)} async-done(((bf16[32,2,49152]{2,1,0:T(2,128)(2,1)}), bf16[32,2,49152]{2,1,0:T(2,128)(2,1)}, u32[]{:S(2)}, u32[]{:S(2)}) %all-to-all-start.5) | async-done | bytes 6291488 | tf_op jit(solution)/shard_map/all_to_all | solution.py:227
  594.5 22.0 %reshape.591 = bf16[3072,1,1024]{2,1,0:T(2,128)(2,1)} reshape(bf16[32,2,49152]{2,1,0:T(2,128)(2,1)} %all-to-all-done.5) | data formatting | bytes 12582912
  616.6 9.8 %copy.162 = bf16[1,3072,1024]{2,1,0:T(8,128)(2,1)} copy(bf16[1,3072,1024]{2,0,1:T(2,128)(2,1)} %bitcast.205) | data formatting | bytes 12582912
  626.4 14.7 %gather_fusion.3 = bf16[2048,1024]{1,0:T(8,128)(2,1)} fusion(bf16[3072,1024]{1,0:T(8,128)(2,1)} %bitcast.196, s32[2048]{0:T(1024)S(1)} %broadcast_clamp_fusion), kind=kCustom, calls=%fused_computation.3 | custom fusion | bytes 8396800 | tf_op jit(solution)/shard_map/gather | solution.py:229
  670.3 8.6 all-to-all-done.6
  681.1 15.3 %fusion = (f32[2,2,1024]{2,1,0:T(2,128)S(1)}, f32[2,1024,1024,2]{2,1,3,0:T(8,128)}) fusion(f32[2,2,1024,1024]{2,3,1,0:T(8,128)} %get-tuple-element.55, f32[2,2,1024]{2,1,0:T(2,128)S(1)} %log_add_fusion, bf16[1024,2,64,1]{0,2,3,1:T(8,128)(2,1)S(1)} %bitcast.224, bf16[1024,2,2,64]{0,3,2,1:T(8,128)(2,1)S(1)} %bitcast.217), kind=kOutput, calls=%fused_computation.9 | convolution fusion | flops 549449728 | bytes 34373632 | tf_op jit(solution)/shard_map/gkrd,skd->krgs/dot_general | solution.py:256
  697.6 11.0 %fusion.2 = bf16[2,2,1024,1024]{2,3,1,0:T(8,128)(2,1)} fusion(f32[2,1024,1024,2]{2,1,3,0:T(8,128)} %get-tuple-element.58, f32[2,2,1024,1024]{2,3,1,0:T(8,128)S(1)} %bitcast.195, f32[2,2,1024]{2,1,0:T(2,128)S(1)} %get-tuple-element.57, f32[2,2,1024]{2,1,0:T(2,128)S(1)} %log_add_fusion), kind=kLoop, calls=%fused_computation.11 | loop fusion | flops 16777216 | bytes 41975808 | tf_op jit(solution)/shard_map/convert_element_type | solution.py:266
  746.8 24.9 %all-to-all-done.7 = bf16[4,256,1024]{2,1,0:T(8,128)(2,1)} async-done(((bf16[4,256,1024]{2,1,0:T(8,128)(2,1)}), bf16[4,256,1024]{2,1,0:T(8,128)(2,1)}, u32[]{:S(2)}, u32[]{:S(2)}) %all-to-all-start.7) | async-done | bytes 2097184 | tf_op jit(solution)/shard_map/all_to_all | solution.py:39
  776.5 9.0 %all-reduce.4 = (bf16[1024]{0:T(1024)(128)(2,1)S(1)}, bf16[1024]{0:T(1024)(128)(2,1)S(1)}) all-reduce(bf16[1024]{0:T(1024)(128)(2,1)S(1)} %get-tuple-element.16, bf16[1024]{0:T(1024)(128)(2,1)S(1)} %get-tuple-element.14), channel_id=1, replica_groups=mesh['expert'=32,'head'=4] {'head'}, use_global_device_ids=true, to_apply=%region_25.26 | all-reduce | flops 2048 | bytes 8192 | tf_op jit(solution)/shard_map/psum | solution.py:309
  785.6 55.4 %all-reduce.2 = (bf16[1024]{0:T(1024)(128)(2,1)S(1)}, bf16[1024]{0:T(1024)(128)(2,1)S(1)}) all-reduce(bf16[1024]{0:T(1024)(128)(2,1)S(1)} %get-tuple-element.25, bf16[1024]{0:T(1024)(128)(2,1)S(1)} %get-tuple-element.26), channel_id=1, replica_groups=mesh['expert'=32,'head'=4] {'expert'}, use_global_device_ids=true, to_apply=%region_26.27 | all-reduce | flops 2048 | bytes 8192 | tf_op jit(solution)/shard_map/psum | solution.py:318
  850.3 30.3 %all-reduce.9.cloned.1.call-done = (bf16[1024,256]{1,0:T(8,128)(2,1)}, bf16[1024,128]{1,0:T(8,128)(2,1)}, bf16[1024,128]{1,0:T(8,128)(2,1)}, bf16[256,1024]{1,0:T(8,128)(2,1)}, bf16[1024,32]{0,1:T(8,128)(2,1)}) async-done(((bf16[1024,256]{1,0:T(8,128)(2,1)}, bf16[1024,128]{1,0:T(8,128)(2,1)}, bf16[1024,128]{1,0:T(8,128)(2,1)}, bf16[256,1024]{1,0:T(8,128)(2,1)}, bf16[1024,32]{0,1:T(8,128)(2,1)}), ...) | async-done | bytes 1638416 | tf_op jit(solution)/shard_map/psum | solution.py:313
  (259 shorter events, 234.4 us)
Async XLA Ops:
  7.2 278.5 %copy-start = (bf16[1,512,1024]{2,1,0:T(8,128)(2,1)S(1)}, bf16[1,512,1024]{2,1,0:T(8,128)(2,1)}, u32[]{:S(2)}) copy-start(bf16[1,512,1024]{2,1,0:T(8,128)(2,1)} %param.27) | copy-start | bytes 3145732
  12.5 30.8 %all-to-all-start = ((bf16[4,256,1024]{2,1,0:T(8,128)(2,1)}), bf16[4,256,1024]{2,1,0:T(8,128)(2,1)S(1)}, u32[]{:S(2)}, u32[]{:S(2)}) async-start(bf16[4,256,1024]{2,1,0:T(8,128)(2,1)} %broadcast_in_dim.41), calls=%async_computation | async-start | bytes 4194304 | tf_op jit(solution)/shard_map/all_to_all | solution.py:22
  48.3 15.6 %copy-start.20 = (bf16[1024,128]{0,1:T(8,128)(2,1)}, bf16[1024,128]{0,1:T(8,128)(2,1)S(1)}, u32[]{:S(2)}) copy-start(bf16[1024,128]{0,1:T(8,128)(2,1)S(1)} %convolution_convert_fusion.9) | copy-start | bytes 786436
  71.4 34.5 %copy-start.6 = (bf16[256,1024]{1,0:T(8,128)(2,1)S(1)}, bf16[256,1024]{1,0:T(8,128)(2,1)}, u32[]{:S(2)}) copy-start(bf16[256,1024]{1,0:T(8,128)(2,1)} %param.14) | copy-start | bytes 1572868
  73.5 32.7 %copy-start.43 = (f32[1024]{0:T(1024)S(1)}, f32[1024]{0:T(1024)}, u32[]{:S(2)}) copy-start(f32[1024]{0:T(1024)} %param.23) | copy-start | bytes 12292
  73.5 30.3 %all-to-all-start.1 = ((bf16[4,256,1024]{2,1,0:T(8,128)(2,1)}), bf16[4,256,1024]{2,1,0:T(8,128)(2,1)}, u32[]{:S(2)}, u32[]{:S(2)}) async-start(bf16[4,256,1024]{2,1,0:T(8,128)(2,1)} %bitcast.210), calls=%async_computation.1 | async-start | bytes 4194304 | tf_op jit(solution)/shard_map/all_to_all | solution.py:39
  106.2 38.3 %copy-start.4 = (f32[256,1024]{1,0:T(8,128)}, f32[256,1024]{1,0:T(8,128)S(1)}, u32[]{:S(2)}) copy-start(f32[256,1024]{1,0:T(8,128)S(1)} %get-tuple-element.32) | copy-start | bytes 3145732
  106.3 38.3 %copy-start.49 = (f32[256]{0:T(256)}, f32[256]{0:T(256)S(1)}, u32[]{:S(2)}) copy-start(f32[256]{0:T(256)S(1)} %fusion.68) | copy-start | bytes 3076
  120.5 81.9 %all-to-all-start.2 = ((bf16[32,96,1024]{2,1,0:T(8,128)(2,1)}), bf16[32,96,1024]{2,1,0:T(8,128)(2,1)}, u32[]{:S(2)}, u32[]{:S(2)}) async-start(bf16[32,96,1024]{2,1,0:T(8,128)(2,1)} %bitcast.209), calls=%async_computation.2 | async-start | bytes 12582912 | tf_op jit(solution)/shard_map/all_to_all | solution.py:172
  202.4 83.3 %all-to-all-start.4 = ((bf16[32,96,1024]{2,1,0:T(8,128)(2,1)}), bf16[32,96,1024]{2,1,0:T(8,128)(2,1)}, u32[]{:S(2)}, u32[]{:S(2)}) async-start(bf16[32,96,1024]{2,1,0:T(8,128)(2,1)} %multiply_convert_fusion), calls=%async_computation.4 | async-start | bytes 12582912 | tf_op jit(solution)/shard_map/all_to_all | solution.py:197
  395.7 117.4 %all-to-all-start.3 = ((bf16[32,2,49152]{2,1,0:T(2,128)(2,1)}), bf16[32,2,49152]{2,1,0:T(2,128)(2,1)}, u32[]{:S(2)}, u32[]{:S(2)}) async-start(bf16[32,2,49152]{2,1,0:T(2,128)(2,1)} %reshape.588), calls=%async_computation.3 | async-start | bytes 12582912 | tf_op jit(solution)/shard_map/all_to_all | solution.py:183
  513.1 81.4 %all-to-all-start.5 = ((bf16[32,2,49152]{2,1,0:T(2,128)(2,1)}), bf16[32,2,49152]{2,1,0:T(2,128)(2,1)}, u32[]{:S(2)}, u32[]{:S(2)}) async-start(bf16[32,2,49152]{2,1,0:T(2,128)(2,1)} %reshape.590), calls=%async_computation.5 | async-start | bytes 12582912 | tf_op jit(solution)/shard_map/all_to_all | solution.py:227
  626.4 20.1 %copy-start.5 = (f32[256,1024]{1,0:T(8,128)S(1)}, f32[256,1024]{1,0:T(8,128)}, u32[]{:S(2)}) copy-start(f32[256,1024]{1,0:T(8,128)} %copy-done.4) | copy-start | bytes 3145732
  626.4 20.1 %copy-start.41 = (f32[1024,32]{0,1:T(8,128)S(1)}, f32[1024,32]{0,1:T(8,128)}, u32[]{:S(2)}) copy-start(f32[1024,32]{0,1:T(8,128)} %param.24) | copy-start | bytes 393220
  626.4 20.2 %copy-start.44 = (f32[1024]{0:T(1024)S(1)}, f32[1024]{0:T(1024)}, u32[]{:S(2)}) copy-start(f32[1024]{0:T(1024)} %param.23) | copy-start | bytes 12292
  626.4 20.2 %copy-start.50 = (f32[256]{0:T(256)S(1)}, f32[256]{0:T(256)}, u32[]{:S(2)}) copy-start(f32[256]{0:T(256)} %copy-done.49) | copy-start | bytes 3076
  650.0 28.9 %all-to-all-start.6 = ((bf16[4,256,1024]{2,1,0:T(8,128)(2,1)}), bf16[4,256,1024]{2,1,0:T(8,128)(2,1)S(1)}, u32[]{:S(2)}, u32[]{:S(2)}) async-start(bf16[4,256,1024]{2,1,0:T(8,128)(2,1)} %broadcast_in_dim.53), calls=%async_computation.6 | async-start | bytes 4194304 | tf_op jit(solution)/shard_map/all_to_all | solution.py:22
  653.6 121.2 %all-reduce.11.cloned.1.call-start = ((), (), s32[]{:S(2)}) async-start(), calls=%async_computation.9 | async-start | bytes 6422528 | tf_op jit(solution)/shard_map/psum | solution.py:308
  678.9 17.5 %copy-start.16 = (bf16[4,256,1024]{2,1,0:T(8,128)(2,1)}, bf16[4,256,1024]{2,1,0:T(8,128)(2,1)S(1)}, u32[]{:S(2)}) copy-start(bf16[4,256,1024]{2,1,0:T(8,128)(2,1)S(1)} %all-to-all-done.6) | copy-start | bytes 6291460
  681.0 15.3 %slice-start = ((s8[16777216]{0:T(1024)(128)(4,1)}), s8[4194304]{0:T(1024)(128)(4,1)S(1)}, s32[]{:S(2)}) async-start(s8[16777216]{0:T(1024)(128)(4,1)} %bitcast.194), calls=%async_computation.10 | async-start | bytes 8388608
  681.1 15.3 %slice-start.1 = ((s8[16777216]{0:T(1024)(128)(4,1)}), s8[4194304]{0:T(1024)(128)(4,1)S(1)}, s32[]{:S(2)}) async-start(s8[16777216]{0:T(1024)(128)(4,1)} %bitcast.194), calls=%async_computation.11 | async-start | bytes 8388608
  681.1 15.3 %slice-start.2 = ((s8[16777216]{0:T(1024)(128)(4,1)}), s8[4194304]{0:T(1024)(128)(4,1)S(1)}, s32[]{:S(2)}) async-start(s8[16777216]{0:T(1024)(128)(4,1)} %bitcast.194), calls=%async_computation.12 | async-start | bytes 8388608
  681.1 16.5 %slice-start.3 = ((s8[16777216]{0:T(1024)(128)(4,1)}), s8[4194304]{0:T(1024)(128)(4,1)S(1)}, s32[]{:S(2)}) async-start(s8[16777216]{0:T(1024)(128)(4,1)} %bitcast.194), calls=%async_computation.13 | async-start | bytes 8388608
  735.0 36.7 %all-to-all-start.7 = ((bf16[4,256,1024]{2,1,0:T(8,128)(2,1)}), bf16[4,256,1024]{2,1,0:T(8,128)(2,1)}, u32[]{:S(2)}, u32[]{:S(2)}) async-start(bf16[4,256,1024]{2,1,0:T(8,128)(2,1)} %bitcast.211), calls=%async_computation.7 | async-start | bytes 4194304 | tf_op jit(solution)/shard_map/all_to_all | solution.py:39
  739.5 141.1 %all-reduce.9.cloned.1.call-start = ((), (), s32[]{:S(2)}) async-start(), calls=%async_computation.8 | async-start | bytes 3276800 | tf_op jit(solution)/shard_map/psum | solution.py:313
  743.7 31.1 %copy-start.51 = (f32[1024]{0:T(1024)S(1)}, f32[1024]{0:T(1024)}, u32[]{:S(2)}) copy-start(f32[1024]{0:T(1024)} %param.18) | copy-start | bytes 12292
  743.7 31.1 %copy-start.54 = (f32[256]{0:T(256)S(1)}, f32[256]{0:T(256)}, u32[]{:S(2)}) copy-start(f32[256]{0:T(256)} %copy-done.53) | copy-start | bytes 3076
  745.2 96.9 %copy-start.56 = (f32[256]{0:T(256)S(1)}, f32[256]{0:T(256)}, u32[]{:S(2)}) copy-start(f32[256]{0:T(256)} %copy-done.55) | copy-start | bytes 3076
  746.8 95.4 %copy-start.7 = (bf16[256,1024]{1,0:T(8,128)(2,1)S(1)}, bf16[256,1024]{1,0:T(8,128)(2,1)}, u32[]{:S(2)}) copy-start(bf16[256,1024]{1,0:T(8,128)(2,1)} %param.14) | copy-start | bytes 1572868
  746.8 95.4 %copy-start.9 = (f32[256,1024]{1,0:T(8,128)S(1)}, f32[256,1024]{1,0:T(8,128)}, u32[]{:S(2)}) copy-start(f32[256,1024]{1,0:T(8,128)} %copy-done.8) | copy-start | bytes 3145732
  746.8 95.4 %copy-start.11 = (bf16[256,1024]{1,0:T(8,128)(2,1)S(1)}, bf16[256,1024]{1,0:T(8,128)(2,1)}, u32[]{:S(2)}) copy-start(bf16[256,1024]{1,0:T(8,128)(2,1)} %param.15) | copy-start | bytes 1572868
  845.5 44.3 %copy-start.1 = (bf16[1,512,1024]{2,1,0:T(8,128)(2,1)S(1)}, bf16[1,512,1024]{2,1,0:T(8,128)(2,1)}, u32[]{:S(2)}) copy-start(bf16[1,512,1024]{2,1,0:T(8,128)(2,1)} %param.27) | copy-start | bytes 3145732
  (46 other events, 310.1 us)
Sparse Core Ops, SparseCore 0:
  670.4 85.2 all-reduce.10
  774.9 105.6 all-reduce.8
where the time goes:
time: 909 us; the launch traced here: 897 us
  local copies, waits for them, and re-layouts  279 us (31%)
  waiting for transfers between devices  181 us (20%)
  other arithmetic  158 us (17%)
  matrix products  145 us (16%)
  blocking collectives  64.4 us (7%)
  starting transfers between devices  53.5 us (6%)
  between operations  15.5 us (2%)
    unnamed x146, local copies, waits for them, and re-layouts  96.9 us
    unnamed x3, other arithmetic  75.6 us
    all_to_all x1, waiting for transfers between devices, body(): lax.all_to_all(grad_slots, 'expert', split_axis=0, concat_axis=1, tiled=T...  56 us
    psum x1, blocking collectives, body(): lax.psum(head_summed[4].astype(jnp.bfloat16), 'expert').astype(jnp.float32)  55.4 us
    convert_element_type x1, local copies, waits for them, and re-layouts, body(): produced = jnp.einsum('cks,csz->ckz', active_reduced, down_weight, prefer...  42.8 us
    convert_element_type x1, local copies, waits for them, and re-layouts, body(): grad_inputs = (jnp.einsum('wkn,wsn->wks', gate_preact_gradient, gate_weig...  42.6 us
    all_to_all x2, waiting for transfers between devices, sum_at_owner(): lax.all_to_all(tiles, axis, split_axis=0, concat_axis=0, tiled=True)  32 us
    psum x1, waiting for transfers between devices, body(): lax.psum(grad_w_query.astype(jnp.bfloat16), 'expert').astype(jnp.float32)  30.3 us
  transfers between devices with their start and end apart: 10, of which 8 were waited for; matrix products, arithmetic and copies ran while one was open for 39% of the time, Pallas kernels for 0%

commit v1 on v0

v1 whole, which is shorter than its diff:
```python
import jax
import jax.numpy as jnp
from jax import lax
from jax.sharding import PartitionSpec as P

HEAD_DIM = 64


eps_norm = 1e-06
rope_base = 10000.0
mask_fill = -1000000000.0


def all_rows(array, axis):
    length = lax.axis_size(axis)
    sent = jnp.broadcast_to(array[None], (length, *array.shape))
    arrived = lax.all_to_all(sent, axis, 0, 0, tiled=True)
    return arrived.reshape(length * array.shape[0], *array.shape[1:])


def swap(array, axis):
    return lax.all_to_all(array, axis, 0, 0, tiled=True)


def sum_at_owner(array, axis):
    length = lax.axis_size(axis)
    arrived = swap(array.reshape(length, array.shape[0] // length, *array.shape[1:]), axis)
    return arrived.astype(jnp.float32).sum(axis=0)


def rms_scale(values, gain_vec):
    return (
        values * lax.rsqrt(jnp.mean(values * values, axis=-1, keepdims=True) + eps_norm) * gain_vec
    )


def rotate(values, cosine, sine_vals):
    half_dim = values.shape[-1] // 2
    front_half = values[..., :half_dim]
    back_half = values[..., half_dim:]
    return jnp.concatenate(
        [front_half * cosine - back_half * sine_vals, back_half * cosine + front_half * sine_vals],
        axis=-1,
    )


def doc_layout(seq_lengths, group_rows):
    seq_ends = jnp.cumsum(seq_lengths, dtype=jnp.int32)
    row_index = jnp.arange(group_rows, dtype=jnp.int32)
    beginning = jnp.max(
        jnp.where(row_index[:, None] >= seq_ends[None, :], seq_ends[None, :], 0), axis=1
    )
    return beginning, row_index


def wide(spec, left, right):
    return jnp.einsum(spec, left, right, preferred_element_type=jnp.float32)


def body(
    tokens,
    cotangent,
    routes,
    lengths,
    gain_attn,
    w_query,
    w_key,
    w_value,
    w_output,
    gain_mix,
    w_router,
    gate_weight,
    up_weight,
    down_weight,
):
    bf16 = jnp.bfloat16
    row_count, model_width = tokens.shape
    pick_count = routes.shape[1]
    head_count = lax.axis_size("head")
    expert_count = lax.axis_size("expert")
    group_rows = row_count * head_count
    query_heads = w_query.shape[1] // HEAD_DIM
    key_heads = w_key.shape[1] // HEAD_DIM
    repeat_count = query_heads // key_heads
    score_scale = HEAD_DIM ** (-0.5)
    capacity = min(row_count, 3 * row_count * pick_count // (2 * expert_count))
    gate_mat, up_mat, down_mat = gate_weight[0], up_weight[0], down_weight[0]

    chosen = jnp.any(
        routes[:, :, None] == jnp.arange(expert_count, dtype=jnp.int32)[None, None, :], axis=1
    )
    earlier = jnp.arange(row_count)[:, None] > jnp.arange(row_count)[None, :]
    rank_in = jnp.dot(earlier.astype(bf16), chosen.astype(bf16), preferred_element_type=jnp.float32)
    slot_of = jnp.where(chosen, rank_in, -1.0).T
    picks = slot_of[:, None, :] == jnp.arange(capacity, dtype=jnp.float32)[None, :, None]
    picks_low = picks.astype(bf16).reshape(expert_count * capacity, row_count)

    def dispatch(rows):
        taken = jnp.dot(picks_low, rows, preferred_element_type=jnp.float32).astype(bf16)
        return swap(taken.reshape(expert_count, capacity, model_width), "expert")

    def collect(slots):
        return lax.dot_general(
            picks_low,
            slots.reshape(expert_count * capacity, model_width),
            (((0,), (0,)), ((), ())),
            preferred_element_type=jnp.float32,
        )

    grad_arrived = dispatch(cotangent)

    beginning, row_index = doc_layout(lengths[0], group_rows)
    position = row_index - beginning
    allowed = (row_index[None, :] >= beginning[:, None]) & (
        row_index[None, :] <= row_index[:, None]
    )
    half_dim = HEAD_DIM // 2
    frequency = rope_base ** (-2.0 * jnp.arange(half_dim, dtype=jnp.float32) / HEAD_DIM)
    angles = position.astype(jnp.float32)[:, None] * frequency[None, :]
    cosine = jnp.cos(angles)[:, None, :]
    sine_vals = jnp.sin(angles)[:, None, :]

    resid_full = all_rows(tokens, "head").astype(jnp.float32)
    full_rows = rms_scale(resid_full, gain_attn).astype(bf16)
    query_raw = jnp.dot(full_rows, w_query, preferred_element_type=jnp.float32).reshape(
        group_rows, query_heads, HEAD_DIM
    )
    key_raw = jnp.dot(full_rows, w_key, preferred_element_type=jnp.float32).reshape(
        group_rows, key_heads, HEAD_DIM
    )
    value_low = (
        jnp.dot(full_rows, w_value, preferred_element_type=jnp.float32)
        .astype(bf16)
        .reshape(group_rows, key_heads, HEAD_DIM)
    )
    query_low = (
        rotate(query_raw, cosine, sine_vals)
        .astype(bf16)
        .reshape(group_rows, key_heads, repeat_count, HEAD_DIM)
    )
    key_low = rotate(key_raw, cosine, sine_vals).astype(bf16)

    def masked_scores():
        product = wide("gkrd,skd->krgs", query_low, key_low) * score_scale
        return jnp.where(allowed, product, mask_fill)

    scores = masked_scores()
    row_peak = jnp.max(scores, axis=-1, keepdims=True)
    lifted = jnp.exp(scores - row_peak)
    row_total = jnp.sum(lifted, axis=-1, keepdims=True)
    log_total = row_peak + jnp.log(row_total)
    weights_low = (lifted / row_total).astype(bf16)
    mixed_low = (
        wide("krgs,skd->gkrd", weights_low, value_low)
        .reshape(group_rows, query_heads * HEAD_DIM)
        .astype(bf16)
    )
    attn_out = sum_at_owner(
        jnp.dot(mixed_low, w_output, preferred_element_type=jnp.float32).astype(bf16), "head"
    )
    resid = tokens.astype(jnp.float32)
    hidden_first = resid + attn_out
    normed_second = rms_scale(hidden_first, gain_mix)
    inputs_arrived = dispatch(normed_second.astype(bf16))
    logits = jnp.dot(normed_second, w_router)
    peak = jnp.max(jnp.where(chosen, logits, -jnp.inf), axis=1, keepdims=True)
    raised = jnp.where(chosen, jnp.exp(jnp.minimum(logits - peak, 0.0)), 0.0)
    share = raised / jnp.sum(raised, axis=1, keepdims=True)
    gate_slot = jnp.sum(jnp.where(picks, share.T[:, None, :], 0.0), axis=2)
    gate_arrived = swap(gate_slot, "expert").reshape(expert_count * capacity, 1)

    rows_in = inputs_arrived.reshape(expert_count * capacity, model_width)
    rows_grad = grad_arrived.reshape(expert_count * capacity, model_width)
    gate_pre = jnp.dot(rows_in, gate_mat, preferred_element_type=jnp.float32)
    up_pre = jnp.dot(rows_in, up_mat, preferred_element_type=jnp.float32)
    silu_at, silu_pull = jax.vjp(jax.nn.silu, gate_pre)
    active = (silu_at * up_pre).astype(bf16)
    produced = jnp.dot(active, down_mat, preferred_element_type=jnp.float32).astype(bf16)
    wide_grad = rows_grad.astype(jnp.float32)
    gate_grad_slot = jnp.sum(wide_grad * produced.astype(jnp.float32), axis=1)
    grad_produced = (wide_grad * gate_arrived).astype(bf16)
    grad_active = wide("zy,my->zm", grad_produced, down_mat)
    grad_up_pre = (grad_active * silu_at).astype(bf16)
    grad_gate_pre = silu_pull(grad_active * up_pre)[0].astype(bf16)
    grad_inputs = (
        wide("kn,sn->ks", grad_gate_pre, gate_mat) + wide("kn,sn->ks", grad_up_pre, up_mat)
    ).astype(bf16)
    gate_grad_back = swap(gate_grad_slot.reshape(expert_count, capacity), "expert")
    grad_back = swap(grad_inputs.reshape(expert_count, capacity, model_width), "expert")
    grad_w_down = wide("zm,zy->my", active, grad_produced)
    grad_w_gate = wide("ns,ny->sy", rows_in, grad_gate_pre)
    grad_w_up = wide("ns,ny->sy", rows_in, grad_up_pre)

    grad_share = jnp.sum(jnp.where(picks, gate_grad_back[:, :, None], 0.0), axis=1).T
    grad_logits = share * (grad_share - jnp.sum(share * grad_share, axis=1, keepdims=True))
    grad_router_part = wide("td,te->de", normed_second, grad_logits)
    grad_normed2 = collect(grad_back) + wide("te,de->td", grad_logits, w_router)
    _, second_pull = jax.vjp(rms_scale, hidden_first, gain_mix)
    grad_from_norm, grad_gain_mix_part = second_pull(grad_normed2)
    grad_hidden = cotangent.astype(jnp.float32) + grad_from_norm
    grad_full = all_rows(grad_hidden.astype(bf16), "head")

    produced_held, _ = lax.optimization_barrier((produced, grad_back))
    returned = swap(produced_held.reshape(expert_count, capacity, model_width), "expert")

    grad_w_output = wide("gm,gd->md", mixed_low, grad_full)
    grad_mixed = (
        wide("gd,md->gm", grad_full, w_output)
        .astype(bf16)
        .reshape(group_rows, key_heads, repeat_count, HEAD_DIM)
    )
    attn_weights = jnp.exp(masked_scores() - log_total)
    grad_weights = wide("gkrd,skd->krgs", grad_mixed, value_low)
    grad_value = wide("krgs,gkrd->skd", attn_weights.astype(bf16), grad_mixed)
    inner = jnp.sum(attn_weights * grad_weights, axis=-1, keepdims=True)
    grad_scores = (attn_weights * (grad_weights - inner)).astype(bf16)
    grad_query_rot = wide("krgs,skd->gkrd", grad_scores, key_low) * score_scale
    grad_key_rot = wide("krgs,gkrd->skd", grad_scores, query_low) * score_scale
    grad_query = (
        rotate(grad_query_rot.reshape(group_rows, query_heads, HEAD_DIM), cosine, -sine_vals)
        .reshape(group_rows, -1)
        .astype(bf16)
    )
    grad_key = rotate(grad_key_rot, cosine, -sine_vals).reshape(group_rows, -1).astype(bf16)
    grad_value_low = grad_value.reshape(group_rows, -1).astype(bf16)
    total_term = wide("gm,dm->gd", grad_query, w_query)
    total_term = total_term + wide("gm,dm->gd", grad_key, w_key)
    total_term = total_term + wide("gm,dm->gd", grad_value_low, w_value)
    grad_normed1 = sum_at_owner(total_term.astype(bf16), "head")
    grad_w_query = wide("gd,gm->dm", full_rows, grad_query)
    grad_w_key = wide("gd,gm->dm", full_rows, grad_key)
    grad_w_value = wide("gd,gm->dm", full_rows, grad_value_low)
    _, first_pull = jax.vjp(rms_scale, resid, gain_attn)
    grad_from_first, grad_gain_attn_part = first_pull(grad_normed1)
    grad_tokens = grad_hidden + grad_from_first
    gated = (picks_low.reshape(expert_count, capacity, row_count) * share.T[:, None, :]).astype(
        bf16
    )
    mixture = lax.dot_general(
        gated.reshape(expert_count * capacity, row_count),
        returned.reshape(expert_count * capacity, model_width),
        (((0,), (0,)), ((), ())),
        preferred_element_type=jnp.float32,
    )
    output = (hidden_first + mixture).astype(bf16)

    def summed(part, axis):
        return lax.psum(part.astype(bf16), axis).astype(jnp.float32)

    return (
        output,
        grad_tokens,
        summed(grad_gain_attn_part, ("expert", "head")),
        summed(grad_w_query, "expert"),
        summed(grad_w_key, "expert"),
        summed(grad_w_value, "expert"),
        summed(grad_w_output, "expert"),
        summed(grad_gain_mix_part, ("expert", "head")),
        summed(grad_router_part, ("expert", "head")),
        summed(grad_w_gate, "head")[None],
        summed(grad_w_up, "head")[None],
        summed(grad_w_down, "head")[None],
    )


def solution(mesh):
    rows = P(("expert", "head"), None)
    per_expert = P("expert", None, None)
    columns = P(None, "head")
    in_specs = (
        rows,
        rows,
        rows,
        P("expert", None),
        P(),
        columns,
        columns,
        columns,
        P("head", None),
        P(),
        P(),
        per_expert,
        per_expert,
        per_expert,
    )
    out_specs = (
        rows,
        rows,
        P(),
        columns,
        columns,
        columns,
        P("head", None),
        P(),
        P(),
        per_expert,
        per_expert,
        per_expert,
    )
    return jax.shard_map(body, mesh=mesh, in_specs=in_specs, out_specs=out_specs, check_vma=False)
```

time: 909 us -> 999 us (1.099)
  waiting for transfers between devices: 181 us -> 587 us
  local copies, waits for them, and re-layouts: 279 us -> 30.2 us
  other arithmetic: 158 us -> 57.3 us
  matrix products: 145 us -> 158 us
  blocking collectives: 64.4 us -> 75.8 us
    psum x2 -> x3, waiting for transfers between devices: 30.3 us -> 310 us  [summed(): return lax.psum(part.astype(bf16), axis).astype(jnp.float32)]
    all_to_all x8 -> x9, waiting for transfers between devices: 151 us -> 277 us  [the longest x7 231 us: swap(): return lax.all_to_all(array, axis, 0, 0, tiled=True)]
    unnamed x146 -> x117, local copies, waits for them, and re-layouts: 96.9 us -> 6.29 us
    convert_element_type x2 -> x1, local copies, waits for them, and re-layouts: 85.4 us -> 9.52 us  [body(): wide_grad = rows_grad.astype(jnp.float32)]
    unnamed x3 -> x1, other arithmetic: 75.6 us -> 0.01 us
    gather x9 -> x0, local copies, waits for them, and re-layouts: 74.6 us -> none  [the longest x5 17.2 us: body(): gates = jax.nn.softmax(jnp.take_along_axis(logits, routes, axis=1), axis=1)]
    scatter x2 -> x0, local copies, waits for them, and re-layouts: 16.1 us -> none  [the longest x1 8.06 us: body(): jnp.full((expert_count * capacity,), row_count, jnp.int32).at[slot_index]]
    dot_general x26 -> x31, matrix products: 139 us -> 154 us  [the longest x22 107 us: wide(): return jnp.einsum(spec, left, right, preferred_element_type=jnp.float32)]
  transfers between devices with their start and end apart: 10 -> 12, of which waited for: 8 -> 11; matrix products, arithmetic and copies ran while one was open for 39% -> 10% of each run, Pallas kernels for 0% -> 0%
where the time goes in v1:
time: 999 us; the launch traced here: 986 us
  waiting for transfers between devices  587 us (59%)
  matrix products  158 us (16%)
  blocking collectives  75.8 us (8%)
  starting transfers between devices  62.6 us (6%)
  other arithmetic  57.3 us (6%)
  local copies, waits for them, and re-layouts  30.2 us (3%)
  between operations  14.8 us (1%)
    psum x3, waiting for transfers between devices, summed(): return lax.psum(part.astype(bf16), axis).astype(jnp.float32)  310 us
    all_to_all x7, waiting for transfers between devices, swap(): return lax.all_to_all(array, axis, 0, 0, tiled=True)  231 us
    dot_general x22, matrix products, wide(): return jnp.einsum(spec, left, right, preferred_element_type=jnp.float32)  107 us
    psum x1, blocking collectives, summed(): return lax.psum(part.astype(bf16), axis).astype(jnp.float32)  65 us
    all_to_all x7, starting transfers between devices, swap(): return lax.all_to_all(array, axis, 0, 0, tiled=True)  52.8 us
    all_to_all x2, waiting for transfers between devices, all_rows(): arrived = lax.all_to_all(sent, axis, 0, 0, tiled=True)  45.8 us
  transfers between devices with their start and end apart: 12, of which 11 were waited for; matrix products, arithmetic and copies ran while one was open for 10% of the time, Pallas kernels for 0%

profile of v1, /device:TPU:4, one launch (start us, length us, event | category | flops | bytes accessed | tf_op | source)
XLA Modules:
  0.0 986.4 jit_solution(10173657598221586243)
XLA Ops:
  20.3 20.4 %all-to-all-done = bf16[4,256,1024]{2,1,0:T(8,128)(2,1)S(1)} async-done(((bf16[4,256,1024]{2,1,0:T(8,128)(2,1)}), bf16[4,256,1024]{2,1,0:T(8,128)(2,1)S(1)}, u32[]{:S(2)}, u32[]{:S(2)}) %all-to-all-start) | async-done | bytes 2097184 | tf_op jit(solution)/shard_map/all_to_all | solution.py:17
  45.2 7.5 fusion.85
  52.7 8.0 fusion.3
  60.8 7.5 fusion.32
  81.6 18.2 %all-to-all-done.1 = bf16[4,256,1024]{2,1,0:T(8,128)(2,1)S(1)} async-done(((bf16[4,256,1024]{2,1,0:T(8,128)(2,1)}), bf16[4,256,1024]{2,1,0:T(8,128)(2,1)S(1)}, u32[]{:S(2)}, u32[]{:S(2)}) %all-to-all-start.1) | async-done | bytes 2097184 | tf_op jit(solution)/shard_map/all_to_all | solution.py:22
  101.1 8.6 all-to-all-start.3
  117.3 65.9 %all-to-all-done.3 = bf16[32,96,1024]{2,1,0:T(8,128)(2,1)} async-done(((bf16[32,96,1024]{2,1,0:T(8,128)(2,1)}), bf16[32,96,1024]{2,1,0:T(8,128)(2,1)}, u32[]{:S(2)}, u32[]{:S(2)}) %all-to-all-start.3) | async-done | bytes 6291488 | tf_op jit(solution)/shard_map/all_to_all | solution.py:22
  183.2 9.4 all-to-all-start.2
  193.0 9.5 copy.57
  202.5 63.5 %all-to-all-done.2 = bf16[32,96,1024]{2,1,0:T(8,128)(2,1)} async-done(((bf16[32,96,1024]{2,1,0:T(8,128)(2,1)}), bf16[32,96,1024]{2,1,0:T(8,128)(2,1)}, u32[]{:S(2)}, u32[]{:S(2)}) %all-to-all-start.2) | async-done | bytes 6291488 | tf_op jit(solution)/shard_map/all_to_all | solution.py:22
  272.0 11.1 %multiply_convert_fusion.4 = (bf16[3072,512]{1,0:T(8,128)(2,1)S(1)}, f32[3072,512]{1,0:T(8,128)}) fusion(f32[3072,512]{1,0:T(8,128)S(1)} %fusion.55, bf16[3072,1024]{1,0:T(8,128)(2,1)} %bitcast.25, bf16[1,1024,512]{2,1,0:T(8,128)(2,1)S(1)} %copy-done.46), kind=kOutput, calls=%fused_computation.25 | convolution fusion | flops 3230662656 | bytes 23068672 | tf_op jit(solution)/shard_map/dot_general | solution.py:175
  283.1 9.4 multiply_reduce_fusion
  293.2 8.3 all-to-all-start.7
  308.2 10.9 %all_to_all.58 = f32[32,1,96]{2,1,0:T(1,128)S(1)} all-to-all(f32[32,1,96]{2,1,0:T(1,128)S(1)} %bitcast.225), channel_id=1, replica_groups=mesh['expert'=32,'head'=4] {'expert'}, dimensions={0} | all-to-all | bytes 24576 | tf_op jit(solution)/shard_map/all_to_all | solution.py:22
  323.6 9.3 multiply_convert_fusion.3
  336.5 7.7 add_convert_fusion
  344.1 6.9 all-to-all-start.5
  351.1 73.4 %all-to-all-done.5 = bf16[32,96,1024]{2,1,0:T(8,128)(2,1)} async-done(((bf16[32,96,1024]{2,1,0:T(8,128)(2,1)}), bf16[32,96,1024]{2,1,0:T(8,128)(2,1)}, u32[]{:S(2)}, u32[]{:S(2)}) %all-to-all-start.5) | async-done | bytes 6291488 | tf_op jit(solution)/shard_map/all_to_all | solution.py:22
  436.4 25.4 %all-to-all-done.8 = bf16[4,256,1024]{2,1,0:T(8,128)(2,1)} async-done(((bf16[4,256,1024]{2,1,0:T(8,128)(2,1)}), bf16[4,256,1024]{2,1,0:T(8,128)(2,1)}, u32[]{:S(2)}, u32[]{:S(2)}) %all-to-all-start.8) | async-done | bytes 2097184 | tf_op jit(solution)/shard_map/all_to_all | solution.py:17
  464.2 8.6 fusion.38
  472.9 13.0 %fusion = (f32[2,2,1024]{2,1,0:T(2,128)S(1)}, f32[2,1024,1024,2]{2,1,3,0:T(8,128)}) fusion(f32[2,2,1024,1024]{2,3,1,0:T(8,128)} %get-tuple-element.48, f32[2,2,1024]{2,1,0:T(2,128)S(1)} %log_add_fusion, bf16[1024,2,64,1]{0,2,3,1:T(8,128)(2,1)S(1)} %bitcast.214, bf16[1024,2,2,64]{0,3,2,1:T(8,128)(2,1)S(1)} %bitcast.210), kind=kOutput, calls=%fused_computation.2 | convolution fusion | flops 549449728 | bytes 34373632 | tf_op jit(solution)/shard_map/gkrd,skd->krgs/dot_general | solution.py:57
  486.2 10.9 %fusion.2 = bf16[2,2,1024,1024]{2,3,1,0:T(8,128)(2,1)} fusion(f32[2,1024,1024,2]{2,1,3,0:T(8,128)} %get-tuple-element.57, f32[2,2,1024,1024]{2,3,1,0:T(8,128)S(1)} %bitcast.191, f32[2,2,1024]{2,1,0:T(2,128)S(1)} %get-tuple-element.56, f32[2,2,1024]{2,1,0:T(2,128)S(1)} %log_add_fusion), kind=kLoop, calls=%fused_computation.4 | loop fusion | flops 16777216 | bytes 41975808 | tf_op jit(solution)/shard_map/convert_element_type | solution.py:216
  497.1 6.2 fusion.37
  516.1 8.3 fusion.27
  524.4 8.7 copy.56
  538.0 11.0 %all-to-all-start.6 = ((bf16[32,96,1024]{2,1,0:T(8,128)(2,1)}), bf16[32,96,1024]{2,1,0:T(8,128)(2,1)}, u32[]{:S(2)}, u32[]{:S(2)}) async-start(bf16[32,96,1024]{2,1,0:T(8,128)(2,1)} %bitcast.199), calls=%async_computation.6 | async-start | bytes 12582912 | tf_op jit(solution)/shard_map/all_to_all | solution.py:22
  549.1 8.3 fusion.26
  557.4 7.2 fusion.25
  575.8 128.7 %all-reduce.7.cloned.1.call-done = bf16[1024,32]{0,1:T(8,128)(2,1)} async-done(((bf16[1024,32]{0,1:T(8,128)(2,1)}), bf16[1024,32]{0,1:T(8,128)(2,1)}) %all-reduce.7.cloned.1.call-update) | async-done | bytes 65552 | tf_op jit(solution)/shard_map/psum | solution.py:248
  706.0 78.2 %all-reduce.11.cloned.1.call-done = (bf16[1,1024,512]{2,1,0:T(8,128)(2,1)}, bf16[1,1024,512]{2,1,0:T(8,128)(2,1)}, bf16[1,512,1024]{2,1,0:T(8,128)(2,1)}) async-done(((bf16[1,1024,512]{2,1,0:T(8,128)(2,1)}, bf16[1,1024,512]{2,1,0:T(8,128)(2,1)}, bf16[1,512,1024]{2,1,0:T(8,128)(2,1)}), (bf16[1,1024,512]{2,1,0:T(8,128)(2,1)}, bf16[1,1024,512]{2,1,0:T(8,128)(2,1)}, ...) | async-done | bytes 3145744 | tf_op jit(solution)/shard_map/psum | solution.py:248
  791.5 103.3 %all-reduce.9.cloned.1.call-done = (bf16[1024,256]{1,0:T(8,128)(2,1)}, bf16[1024,128]{1,0:T(8,128)(2,1)}, bf16[1024,128]{1,0:T(8,128)(2,1)}, bf16[256,1024]{1,0:T(8,128)(2,1)}) async-done(((bf16[1024,256]{1,0:T(8,128)(2,1)}, bf16[1024,128]{1,0:T(8,128)(2,1)}, bf16[1024,128]{1,0:T(8,128)(2,1)}, bf16[256,1024]{1,0:T(8,128)(2,1)}), (bf16[1024,256]{1,0:T(8,128)(2,1)}, bf16[1024,128]{1,0:T(8,128)(2,1)}, ...) | async-done | bytes 1572880 | tf_op jit(solution)/shard_map/psum | solution.py:248
  905.0 65.0 %all-reduce = (bf16[1024]{0:T(1024)(128)(2,1)S(1)}, bf16[1024]{0:T(1024)(128)(2,1)S(1)}) all-reduce(bf16[1024]{0:T(1024)(128)(2,1)S(1)} %get-tuple-element.16, bf16[1024]{0:T(1024)(128)(2,1)S(1)} %get-tuple-element.14), channel_id=1, replica_groups=mesh['expert'=32,'head'=4] {'expert','head'}, use_global_device_ids=true, to_apply=%region_20.21 | all-reduce | flops 2048 | bytes 8192 | tf_op jit(solution)/shard_map/psum | solution.py:248
  (206 shorter events, 133.4 us)
Async XLA Ops:
  7.2 275.9 %copy-start = (bf16[1,512,1024]{2,1,0:T(8,128)(2,1)S(1)}, bf16[1,512,1024]{2,1,0:T(8,128)(2,1)}, u32[]{:S(2)}) copy-start(bf16[1,512,1024]{2,1,0:T(8,128)(2,1)} %param.27) | copy-start | bytes 3145732
  7.2 10.1 %copy-start.48 = (s32[1,8]{1,0:T(1,128)S(1)}, s32[1,8]{1,0:T(1,128)}, u32[]{:S(2)}) copy-start(s32[1,8]{1,0:T(1,128)} %param.17) | copy-start | bytes 100
  7.2 34.0 %copy-start.41 = (f32[1024]{0:T(1024)S(1)}, f32[1024]{0:T(1024)}, u32[]{:S(2)}) copy-start(f32[1024]{0:T(1024)} %param.18) | copy-start | bytes 12292
  10.0 30.8 %all-to-all-start = ((bf16[4,256,1024]{2,1,0:T(8,128)(2,1)}), bf16[4,256,1024]{2,1,0:T(8,128)(2,1)S(1)}, u32[]{:S(2)}, u32[]{:S(2)}) async-start(bf16[4,256,1024]{2,1,0:T(8,128)(2,1)} %broadcast_in_dim.73), calls=%async_computation | async-start | bytes 4194304 | tf_op jit(solution)/shard_map/all_to_all | solution.py:17
  18.8 24.8 %copy-start.13 = (f32[1024,32]{0,1:T(8,128)}, f32[1024,32]{0,1:T(8,128)S(1)}, u32[]{:S(2)}) copy-start(f32[1024,32]{0,1:T(8,128)S(1)} %get-tuple-element.44) | copy-start | bytes 393220
  45.2 15.5 %copy-start.17 = (bf16[1024,128]{0,1:T(8,128)(2,1)}, bf16[1024,128]{0,1:T(8,128)(2,1)S(1)}, u32[]{:S(2)}) copy-start(bf16[1024,128]{0,1:T(8,128)(2,1)S(1)} %convolution_convert_fusion.11) | copy-start | bytes 786436
  70.4 29.4 %all-to-all-start.1 = ((bf16[4,256,1024]{2,1,0:T(8,128)(2,1)}), bf16[4,256,1024]{2,1,0:T(8,128)(2,1)S(1)}, u32[]{:S(2)}, u32[]{:S(2)}) async-start(bf16[4,256,1024]{2,1,0:T(8,128)(2,1)} %bitcast.200), calls=%async_computation.1 | async-start | bytes 4194304 | tf_op jit(solution)/shard_map/all_to_all | solution.py:22
  101.1 10.8 %copy-start.7 = (bf16[256,1024]{1,0:T(8,128)(2,1)S(1)}, bf16[256,1024]{1,0:T(8,128)(2,1)}, u32[]{:S(2)}) copy-start(bf16[256,1024]{1,0:T(8,128)(2,1)} %param.14) | copy-start | bytes 1572868
  101.1 11.6 %copy-start.11 = (pred[3072,256]{1,0:T(32,128)(4,1)S(1)}, pred[3072,256]{1,0:T(32,128)(4,1)}, u32[]{:S(2)}) copy-start(pred[3072,256]{1,0:T(32,128)(4,1)} %copy-done.10) | copy-start | bytes 2359300
  101.1 11.6 %copy-start.40 = (f32[1024]{0:T(1024)S(1)}, f32[1024]{0:T(1024)}, u32[]{:S(2)}) copy-start(f32[1024]{0:T(1024)} %param.23) | copy-start | bytes 12292
  101.1 82.1 %all-to-all-start.3 = ((bf16[32,96,1024]{2,1,0:T(8,128)(2,1)}), bf16[32,96,1024]{2,1,0:T(8,128)(2,1)}, u32[]{:S(2)}, u32[]{:S(2)}) async-start(bf16[32,96,1024]{2,1,0:T(8,128)(2,1)} %bitcast.198), calls=%async_computation.3 | async-start | bytes 12582912 | tf_op jit(solution)/shard_map/all_to_all | solution.py:22
  183.2 82.8 %all-to-all-start.2 = ((bf16[32,96,1024]{2,1,0:T(8,128)(2,1)}), bf16[32,96,1024]{2,1,0:T(8,128)(2,1)}, u32[]{:S(2)}, u32[]{:S(2)}) async-start(bf16[32,96,1024]{2,1,0:T(8,128)(2,1)} %bitcast.197), calls=%async_computation.2 | async-start | bytes 12582912 | tf_op jit(solution)/shard_map/all_to_all | solution.py:22
  272.0 11.2 %copy-start.51 = (f32[3072,512]{1,0:T(8,128)}, f32[3072,512]{1,0:T(8,128)S(1)}, u32[]{:S(2)}) copy-start(f32[3072,512]{1,0:T(8,128)S(1)} %fusion.55) | copy-start | bytes 18874372
  293.2 13.6 %all-to-all-start.7 = ((f32[32,1,96]{2,1,0:T(1,128)}), f32[32,1,96]{2,1,0:T(1,128)S(1)}, u32[]{:S(2)}, u32[]{:S(2)}) async-start(f32[32,1,96]{2,1,0:T(1,128)} %all_to_all.44), calls=%async_computation.7 | async-start | bytes 32768 | tf_op jit(solution)/shard_map/all_to_all | solution.py:22
  344.1 80.4 %all-to-all-start.5 = ((bf16[32,96,1024]{2,1,0:T(8,128)(2,1)}), bf16[32,96,1024]{2,1,0:T(8,128)(2,1)}, u32[]{:S(2)}, u32[]{:S(2)}) async-start(bf16[32,96,1024]{2,1,0:T(8,128)(2,1)} %bitcast.202), calls=%async_computation.5 | async-start | bytes 12582912 | tf_op jit(solution)/shard_map/all_to_all | solution.py:22
  351.1 78.7 %copy-start.12 = (bf16[256,1024]{1,0:T(8,128)(2,1)S(1)}, bf16[256,1024]{1,0:T(8,128)(2,1)}, u32[]{:S(2)}) copy-start(bf16[256,1024]{1,0:T(8,128)(2,1)} %param.15) | copy-start | bytes 1572868
  429.2 32.7 %copy-start.36 = (bf16[256,1024]{1,0:T(8,128)(2,1)S(1)}, bf16[256,1024]{1,0:T(8,128)(2,1)}, u32[]{:S(2)}) copy-start(bf16[256,1024]{1,0:T(8,128)(2,1)} %param.22) | copy-start | bytes 1572868
  429.7 34.4 %copy-start.6 = (f32[256,1024]{1,0:T(8,128)}, f32[256,1024]{1,0:T(8,128)S(1)}, u32[]{:S(2)}) copy-start(f32[256,1024]{1,0:T(8,128)S(1)} %get-tuple-element.55) | copy-start | bytes 3145732
  431.7 30.1 %all-to-all-start.8 = ((bf16[4,256,1024]{2,1,0:T(8,128)(2,1)}), bf16[4,256,1024]{2,1,0:T(8,128)(2,1)}, u32[]{:S(2)}, u32[]{:S(2)}) async-start(bf16[4,256,1024]{2,1,0:T(8,128)(2,1)} %broadcast_in_dim.130), calls=%async_computation.8 | async-start | bytes 4194304 | tf_op jit(solution)/shard_map/all_to_all | solution.py:17
  464.2 21.6 %slice-start = ((s8[16777216]{0:T(1024)(128)(4,1)}), s8[4194304]{0:T(1024)(128)(4,1)S(1)}, s32[]{:S(2)}) async-start(s8[16777216]{0:T(1024)(128)(4,1)} %bitcast.190), calls=%async_computation.13 | async-start | bytes 8388608
  464.2 21.6 %slice-start.1 = ((s8[16777216]{0:T(1024)(128)(4,1)}), s8[4194304]{0:T(1024)(128)(4,1)S(1)}, s32[]{:S(2)}) async-start(s8[16777216]{0:T(1024)(128)(4,1)} %bitcast.190), calls=%async_computation.14 | async-start | bytes 8388608
  472.8 13.0 %slice-start.2 = ((s8[16777216]{0:T(1024)(128)(4,1)}), s8[4194304]{0:T(1024)(128)(4,1)S(1)}, s32[]{:S(2)}) async-start(s8[16777216]{0:T(1024)(128)(4,1)} %bitcast.190), calls=%async_computation.15 | async-start | bytes 8388608
  472.8 13.4 %slice-start.3 = ((s8[16777216]{0:T(1024)(128)(4,1)}), s8[4194304]{0:T(1024)(128)(4,1)S(1)}, s32[]{:S(2)}) async-start(s8[16777216]{0:T(1024)(128)(4,1)} %bitcast.190), calls=%async_computation.16 | async-start | bytes 8388608
  486.2 10.9 %copy-start.23 = (bf16[1024,4,32]{0,2,1:T(8,128)(2,1)S(1)}, bf16[1024,4,32]{0,2,1:T(8,128)(2,1)}, u32[]{:S(2)}) copy-start(bf16[1024,4,32]{0,2,1:T(8,128)(2,1)} %copy-done.22) | copy-start | bytes 786436
  486.2 10.9 %copy-start.25 = (bf16[1024,4,32]{0,2,1:T(8,128)(2,1)S(1)}, bf16[1024,4,32]{0,2,1:T(8,128)(2,1)}, u32[]{:S(2)}) copy-start(bf16[1024,4,32]{0,2,1:T(8,128)(2,1)} %copy-done.24) | copy-start | bytes 786436
  508.9 29.1 %all-to-all-start.9 = ((bf16[4,256,1024]{2,1,0:T(8,128)(2,1)}), bf16[4,256,1024]{2,1,0:T(8,128)(2,1)}, u32[]{:S(2)}, u32[]{:S(2)}) async-start(bf16[4,256,1024]{2,1,0:T(8,128)(2,1)} %bitcast.201), calls=%async_computation.9 | async-start | bytes 4194304 | tf_op jit(solution)/shard_map/all_to_all | solution.py:22
  513.4 191.1 %all-reduce.7.cloned.1.call-start = ((), (), s32[]{:S(2)}) async-start(), calls=%async_computation.10 | async-start | bytes 131072 | tf_op jit(solution)/shard_map/psum | solution.py:248
  538.0 436.3 %all-to-all-start.6 = ((bf16[32,96,1024]{2,1,0:T(8,128)(2,1)}), bf16[32,96,1024]{2,1,0:T(8,128)(2,1)}, u32[]{:S(2)}, u32[]{:S(2)}) async-start(bf16[32,96,1024]{2,1,0:T(8,128)(2,1)} %bitcast.199), calls=%async_computation.6 | async-start | bytes 12582912 | tf_op jit(solution)/shard_map/all_to_all | solution.py:22
  549.0 235.2 %all-reduce.11.cloned.1.call-start = ((), (), s32[]{:S(2)}) async-start(), calls=%async_computation.12 | async-start | bytes 6291456 | tf_op jit(solution)/shard_map/psum | solution.py:248
  564.6 330.1 %all-reduce.9.cloned.1.call-start = ((), (), s32[]{:S(2)}) async-start(), calls=%async_computation.11 | async-start | bytes 3145728 | tf_op jit(solution)/shard_map/psum | solution.py:248
  789.9 114.7 %copy-start.8 = (bf16[256,1024]{1,0:T(8,128)(2,1)S(1)}, bf16[256,1024]{1,0:T(8,128)(2,1)}, u32[]{:S(2)}) copy-start(bf16[256,1024]{1,0:T(8,128)(2,1)} %param.14) | copy-start | bytes 1572868
  789.9 114.7 %copy-start.42 = (f32[1024]{0:T(1024)S(1)}, f32[1024]{0:T(1024)}, u32[]{:S(2)}) copy-start(f32[1024]{0:T(1024)} %param.18) | copy-start | bytes 12292
  (37 other events, 198.4 us)
Sparse Core Ops, SparseCore 0:
  519.6 184.8 all-reduce.6
  708.3 75.7 all-reduce.10
  788.9 105.8 all-reduce.8

commit v2 on v1

v2 whole, which is shorter than its diff:
```python
import functools

import jax
import jax.numpy as jnp
from jax import lax
from jax.experimental import pallas as pl
from jax.experimental.pallas import tpu as pltpu
from jax.sharding import PartitionSpec as P

HEAD_DIM = 64
SIDE = 4
LANES = 128
MIB = 1024 * 1024

eps_norm = 1e-06
rope_base = 10000.0
mask_fill = -1000000000.0

bf16 = jnp.bfloat16
f32 = jnp.float32


def dot(left, right):
    return lax.dot_general(left, right, (((1,), (0,)), ((), ())), preferred_element_type=f32)


def dot_rows(left, right):
    return lax.dot_general(left, right, (((1,), (1,)), ((), ())), preferred_element_type=f32)


def dot_cols(left, right):
    return lax.dot_general(left, right, (((0,), (0,)), ((), ())), preferred_element_type=f32)


def call(kernel, out_shapes, args, specs=None, grid=None, out_specs=None, scratch=(), flops=0, vmem=60, aliases=None):
    moved = sum(a.size * a.dtype.itemsize for a in args)
    moved += sum(s.size * s.dtype.itemsize for s in out_shapes)
    whole = pl.BlockSpec(memory_space=pltpu.VMEM)
    settings = {} if grid is None else {"grid": grid}
    return pl.pallas_call(
        kernel,
        out_shape=out_shapes,
        in_specs=specs or [whole] * len(args),
        out_specs=out_specs or [whole] * len(out_shapes),
        scratch_shapes=list(scratch),
        input_output_aliases=aliases or {},
        compiler_params=pltpu.CompilerParams(vmem_limit_bytes=vmem * MIB),
        cost_estimate=pl.CostEstimate(flops=flops, bytes_accessed=moved, transcendentals=0),
        **settings,
    )(*args)


def array(shape, dtype):
    return jax.ShapeDtypeStruct(shape, dtype)


CHIPS = ("z", "x")
PLANE = ("z", "x", "core")


def line_shift(values, step):
    pairs = [(i, (i + step) % SIDE) for i in range(SIDE)]
    return lax.ppermute(values, "head", pairs)


def plane_shift(first, values, step):
    pairs = []
    for i in range(2 * SIDE * SIDE):
        z, x, core = i // (2 * SIDE), i // 2 % SIDE, i % 2
        if (core == 0) == first:
            z = (z + step) % SIDE
        else:
            x = (x + step) % SIDE
        pairs.append((i, (z * SIDE + x) * 2 + core))
    return lax.ppermute(values, PLANE, pairs)


shift_u = functools.partial(plane_shift, True)
shift_w = functools.partial(plane_shift, False)


def swap_core(values):
    return lax.ppermute(values, "core", [(0, 1), (1, 0)])


def after(values, *earlier):
    return lax.optimization_barrier((values, *earlier))[0]


def ring_gather(block, shift, *between):
    half = block.shape[0] // 32 * 16
    from_before, from_after = shift(block, 1), shift(block, -1)
    if between:
        from_before, from_after, *_ = lax.optimization_barrier((from_before, from_after, *between))
    far_lo, far_hi = shift(from_before[:half], 1), shift(from_after[half:], -1)
    return block, from_after, far_lo, far_hi, from_before


def direct_swap(parts, shift):
    return [parts[0], shift(parts[3], -1), shift(parts[2], 2), shift(parts[1], 1)]


def ring_sum(parts, shift):
    before_high, after_low = shift(parts[1][1], 1), shift(parts[3][0], -1)
    low_in, high_in = shift(parts[2][0], 1), shift(parts[2][1], -1)
    up = (parts[1][0].astype(f32) + low_in.astype(f32)).astype(bf16)
    down = (parts[3][1].astype(f32) + high_in.astype(f32)).astype(bf16)
    before_low, after_high = shift(up, 1), shift(down, -1)
    return (before_low, before_high), (after_low, after_high)


def swap_all(values, axes):
    return lax.all_to_all(values, axes, 0, 0, tiled=True)


def all_blocks(block, axes):
    count = lax.axis_size(axes)
    return swap_all(jnp.broadcast_to(block[None], (count, *block.shape)), axes)


def rope(values, cosine, sine_signed):
    lane = lax.broadcasted_iota(jnp.int32, cosine.shape, 1)
    front = lane % HEAD_DIM < HEAD_DIM // 2
    out = []
    for at in range(0, values.shape[1], LANES):
        part = values[:, at : at + LANES]
        partner = jnp.where(
            front,
            pltpu.roll(part, LANES - HEAD_DIM // 2, 1),
            pltpu.roll(part, HEAD_DIM // 2, 1),
        )
        out.append(part * cosine + partner * sine_signed)
    return jnp.concatenate(out, axis=1)


def place(at, distance, rows):
    return pl.ds(pl.multiple_of((at[3] + distance) % SIDE * rows, rows), rows)


def attend_kernel(
    at, own, from_after, far_lo, far_hi, from_before, gain, weights, cosine, sine, starts,
    normed_out, query_out, key_out, value_out, mixed_out, log_out, mixed_0, mixed_1, mixed_2, mixed_3,
    rows_in, normed, query, key, value, mixed, log_total, sems,
):
    rows = own.shape[0]
    width = query.shape[1]
    kept = (normed, query, key, value, mixed, log_total)
    outs = (normed_out, query_out, key_out, value_out, mixed_out, log_out)

    def keep(i, n):
        here = pl.ds(i * rows, rows)
        return pltpu.make_async_copy(kept[n].at[here, :], outs[n].at[here, :], sems.at[i, n])

    rows_in[place(at, 0, rows), :] = own[...]
    rows_in[place(at, 1, rows), :] = from_after[...]
    rows_in[place(at, 3, rows), :] = from_before[...]
    half = rows // 2
    far = (at[3] + 2) % SIDE * rows
    rows_in[pl.ds(pl.multiple_of(far, half), half), :] = far_lo[...]
    rows_in[pl.ds(pl.multiple_of(far + half, half), half), :] = far_hi[...]
    head_of = lax.broadcasted_iota(jnp.int32, (rows, width), 1) // HEAD_DIM
    lane = lax.broadcasted_iota(jnp.int32, (rows, LANES), 1)
    for i in range(SIDE):
        here = slice(i * rows, (i + 1) * rows)
        extent = (i + 1) * rows
        x = rows_in[here, :].astype(f32)
        scale = lax.rsqrt(jnp.mean(x * x, axis=1, keepdims=True) + eps_norm)
        low = (x * scale * gain[...]).astype(bf16)
        normed[here, :] = low
        raw = dot(low, weights[...])
        q = rope(raw[:, :width], cosine[here, :], sine[here, :]).astype(bf16)
        q = q * jnp.asarray(HEAD_DIM**-0.5, bf16)
        query[here, :] = q
        key[here, :] = rope(raw[:, width : 2 * width], cosine[here, :], sine[here, :]).astype(bf16)
        value[here, :] = raw[:, 2 * width :].astype(bf16)
        column = lax.broadcasted_iota(jnp.int32, (rows, extent), 1)
        row = i * rows + lax.broadcasted_iota(jnp.int32, (rows, extent), 0)
        bias = jnp.where((column >= starts[here, :]) & (column <= row), 0.0, mask_fill)
        total = jnp.zeros((rows, width), f32)
        logs = jnp.zeros((rows, LANES), f32)
        for h in range(width // HEAD_DIM):
            q_h = jnp.where(head_of == h, q, jnp.zeros_like(q))
            scores = dot_rows(q_h, key[:extent, :]) + bias
            peak = jnp.max(scores, axis=1, keepdims=True)
            lifted = jnp.exp(scores - peak)
            summed = jnp.sum(lifted, axis=1, keepdims=True)
            probs = (lifted * (1.0 / summed)).astype(bf16)
            total = jnp.where(head_of == h, dot(probs, value[:extent, :]), total)
            logs = jnp.where(lane == h, peak + jnp.log(summed), logs)
        mixed[here, :] = total.astype(bf16)
        log_total[here, :] = logs
        for n in range(len(kept)):
            keep(i, n).start()
    for d, out in enumerate((mixed_0, mixed_1, mixed_2, mixed_3)):
        out[...] = mixed[place(at, d, rows), :]
    for i in range(SIDE):
        for n in range(len(kept)):
            keep(i, n).wait()


def attend_back_kernel(
    at, part_0, part_1, part_2a, part_2b, part_3, w_output, query, key, value, mixed, log_total, starts, cosine, sine,
    grads, out_0, out_1, out_2, out_3, grad_in, grad_query,
):
    rows, width = out_0.shape[0], query.shape[1]
    length = rows * SIDE
    heads = width // HEAD_DIM
    for d, part in ((0, part_0), (1, part_1), (3, part_3)):
        grad_in[place(at, d, rows), :] = dot_rows(part[:rows, :], w_output[...]).astype(bf16)
    cut = part_2a.shape[0]
    far = (at[3] + 2) % SIDE * rows
    low = pl.ds(pl.multiple_of(far, 16), cut)
    grad_in[low, :] = dot_rows(part_2a[...], w_output[...]).astype(bf16)
    high = pl.ds(pl.multiple_of(far + cut, 16), rows - cut)
    grad_in[high, :] = dot_rows(part_2b[: rows - cut, :], w_output[...]).astype(bf16)
    both = grad_in[...].astype(f32) * mixed[...].astype(f32)
    both_hi = both.astype(bf16)
    both_lo = (both - both_hi.astype(f32)).astype(bf16)
    marks = lax.broadcasted_iota(jnp.int32, (8, width), 1) // HEAD_DIM
    marks = (marks == lax.broadcasted_iota(jnp.int32, (8, width), 0)).astype(bf16)
    inner = dot_rows(marks, both_hi) + dot_rows(marks, both_lo)
    logs = jnp.transpose(log_total[...])
    head_of = lax.broadcasted_iota(jnp.int32, (rows, width), 1) // HEAD_DIM
    lane = lax.broadcasted_iota(jnp.int32, (rows, LANES), 1)
    for j in range(SIDE):
        here = slice(j * rows, (j + 1) * rows)
        first = j * rows
        extent = length - first
        key_at = first + lax.broadcasted_iota(jnp.int32, (rows, extent), 0)
        query_at = first + lax.broadcasted_iota(jnp.int32, (rows, extent), 1)
        allowed = (key_at >= starts[:, first:]) & (key_at <= query_at)
        bias = jnp.where(allowed, 0.0, mask_fill)
        k_here, v_here = key[here, :], value[here, :]
        q_there, g_there = query[first:, :], grad_in[first:, :]
        grad_k = jnp.zeros((rows, width), f32)
        grad_v = jnp.zeros((rows, width), f32)
        grad_q = None
        for h in range(heads):
            mine = head_of == h
            k_h = jnp.where(mine, k_here, jnp.zeros_like(k_here))
            v_h = jnp.where(mine, v_here, jnp.zeros_like(v_here))
            probs = jnp.exp(dot_rows(k_h, q_there) + bias - logs[h : h + 1, first:])
            slopes = probs * (dot_rows(v_h, g_there) - inner[h : h + 1, first:])
            probs_low, slopes_low = probs.astype(bf16), slopes.astype(bf16)
            grad_v = jnp.where(mine, dot(probs_low, g_there), grad_v)
            grad_k = jnp.where(mine, dot(slopes_low, q_there), grad_k)
            term = dot_cols(slopes_low, k_h)
            grad_q = term if grad_q is None else grad_q + term
        if j == 0:
            grad_query[...] = grad_q
        else:
            grad_query[first:, :] = grad_query[first:, :] + grad_q
        compact = []
        for values, turn in ((grad_k, True), (grad_v, False)):
            halves = []
            for lane_at in (0, LANES):
                part = values[:, lane_at : lane_at + LANES]
                part = part + pltpu.roll(part, HEAD_DIM, 1)
                halves.append(rope(part, cosine[here, :], -sine[here, :]) if turn else part)
            compact.append(jnp.where(lane < HEAD_DIM, halves[0], halves[1]).astype(bf16))
        grads[here, width : width + LANES] = compact[0]
        grads[here, width + LANES :] = compact[1]
        turned_q = rope(grad_query[here, :], cosine[here, :], -sine[here, :])
        grads[here, :width] = (turned_q * HEAD_DIM**-0.5).astype(bf16)
    for d, out in enumerate((out_0, out_1, out_2, out_3)):
        out[...] = grads[place(at, d, rows), :]


def join_kernel(
    at, mixed_0, mixed_1, mixed_2, mixed_3, weights, tokens, gain, hidden_out, inputs_out,
):
    hidden = tokens[...].astype(f32)
    for d, part in enumerate((mixed_0, mixed_1, mixed_2, mixed_3)):
        hidden = hidden + dot(part[...], weights[(at[3] + d) % SIDE])
    scale = lax.rsqrt(jnp.mean(hidden * hidden, axis=1, keepdims=True) + eps_norm)
    hidden_out[...] = hidden
    inputs_out[...] = (hidden * scale * gain[...]).astype(bf16)


def expert_kernel(capacity, distance, at, x_a, x_b, g_all, router, *refs):
    own, sib = refs[:3], refs[3:6]
    (grad_lo, grad_hi, share_out, mix_all, rows_out, grads_out, active_out, slopes_out,
     x_blocks, g_blocks, w_gate, w_up, w_down, share, slots, gate_rows, g_rows, marks, grad_slots, mix_slots,
     grad_blocks, mix_blocks, x_sem, g_sem, w_sem, mix_sem, grad_sem) = refs[6 if distance == 0 else 7 :]
    step = pl.program_id(0)
    rows = x_a.shape[0]
    picks = 8
    experts = share_out.shape[0]
    taken = g_blocks.shape[1]
    z, x, core = at[0], at[1], at[2]
    me = (z * SIDE + x) * 2 + core
    ids = (me, me + 1 - 2 * core)
    first_core = core == 0
    u, w = jnp.where(first_core, z, x), jnp.where(first_core, x, z)
    x_from = (x_a, *[x_b.at[pl.ds(b * rows, rows), :] for b in range(SIDE - 1)])

    def source(b):
        there, away = (u + b) % SIDE, (w + distance) % SIDE
        return jnp.where(first_core, there * SIDE + away, away * SIDE + there)

    def x_copy(b):
        return pltpu.make_async_copy(x_from[b], x_blocks.at[b], x_sem.at[b])

    def g_copy(b):
        there = pl.ds(pl.multiple_of(source(b) * taken, taken), taken)
        return pltpu.make_async_copy(g_all.at[there, :], g_blocks.at[b], g_sem.at[b])

    def w_copy(e, n):
        there = (w_gate, w_up, w_down)[n].at[e]
        return pltpu.make_async_copy((own, sib)[e][n].at[0], there, w_sem.at[e, n])

    def mix_copy(b):
        there = pl.ds(pl.multiple_of(source(b) * rows, rows), rows)
        return pltpu.make_async_copy(mix_blocks.at[b], mix_all.at[there, :], mix_sem.at[b])

    def grad_copy(b):
        out = grad_lo if b < SIDE // 2 else grad_hi
        there = pl.ds(b % (SIDE // 2) * taken, taken)
        return pltpu.make_async_copy(grad_blocks.at[b], out.at[there, :], grad_sem.at[b])

    @pl.when(step == 0)
    def _():
        for b in range(SIDE):
            x_copy(b).start()
            g_copy(b).start()
        for e in range(2):
            for n in range(3):
                w_copy(e, n).start()
        gate_rows[...] = jnp.zeros_like(gate_rows)
        expert = lax.broadcasted_iota(jnp.int32, (experts, rows), 0)
        token = lax.broadcasted_iota(jnp.int32, (rows, rows), 0)
        earlier = token < lax.broadcasted_iota(jnp.int32, (rows, rows), 1)
        earlier = earlier.astype(f32).astype(bf16)
        for b in range(SIDE):
            here = slice(b * rows, (b + 1) * rows)
            x_copy(b).wait()
            g_copy(b).wait()
            named = g_blocks[b, rows : rows + picks, :rows].astype(f32).astype(jnp.int32)
            used = jnp.zeros((experts, rows), f32)
            for p in range(picks):
                used = jnp.where(named[p : p + 1, :] == expert, 1.0, used)
            rank = jnp.where(used > 0, dot(used.astype(bf16), earlier), -1.0)
            logits = jnp.transpose(dot(x_blocks[b], router[...]))[:experts, :]
            peak = jnp.max(jnp.where(used > 0, logits, mask_fill), axis=0, keepdims=True)
            raised = jnp.where(used > 0, jnp.exp(jnp.minimum(logits - peak, 0.0)), 0.0)
            ratio = raised / jnp.sum(raised, axis=0, keepdims=True)
            if b == 0:
                share_out[...] = ratio
            for e in range(2):
                mine = expert == ids[e]
                share[e : e + 1, here] = jnp.sum(jnp.where(mine, ratio, 0.0), axis=0, keepdims=True)
                slots[e : e + 1, here] = jnp.sum(jnp.where(mine, rank, 0.0), axis=0, keepdims=True)
        for n in range(3):
            w_copy(0, n).wait()

    @pl.when(step == 1)
    def _():
        for n in range(3):
            w_copy(1, n).wait()

    slot_index = lax.broadcasted_iota(jnp.int32, (capacity, rows), 0).astype(f32)
    shares, slots_here = share[pl.ds(step, 1), :], slots[pl.ds(step, 1), :]
    target = pl.ds(pl.multiple_of(step * capacity, capacity), capacity)
    expert_row = lax.broadcasted_iota(jnp.int32, (experts, rows), 0)
    expert_row = expert_row == jnp.where(step == 0, ids[0], ids[1])
    gates, masks = [], []
    for b in range(SIDE):
        here = slice(b * rows, (b + 1) * rows)
        there = slice(b * capacity, (b + 1) * capacity)
        mask = slot_index == slots_here[:, here]
        masks.append(mask)
        mark = mask.astype(f32).astype(bf16)
        marks[b, target, :] = mark
        rows_out[0, there, :] = dot(mark, x_blocks[b]).astype(bf16)
        g_rows[there, :] = dot(mark, g_blocks[b, :rows, :]).astype(bf16)
        gates.append(jnp.sum(jnp.where(mask, shares[:, here], 0.0), axis=1, keepdims=True))
    gate = jnp.concatenate(gates, axis=0)
    x = rows_out[0]
    gate_pre = dot(x, w_gate[step])
    up_pre = dot(x, w_up[step])
    sigmoid = 1.0 / (1.0 + jnp.exp(-gate_pre))
    silu = gate_pre * sigmoid
    active = (silu * up_pre).astype(bf16)
    active_out[0] = active
    produced = dot(active, w_down[step]).astype(bf16).astype(f32)
    wide_g = g_rows[...].astype(f32)
    products = jnp.sum(wide_g * produced, axis=1, keepdims=True)
    grad_produced = (gate * wide_g).astype(bf16)
    grads_out[0] = grad_produced
    mix = (gate * produced).astype(bf16)
    grad_active = dot_rows(grad_produced, w_down[step])
    grad_up = (grad_active * silu).astype(bf16)
    slope = sigmoid * (1.0 + gate_pre * (1.0 - sigmoid))
    grad_gate = (grad_active * up_pre * slope).astype(bf16)
    width = grad_gate.shape[1]
    slopes_out[0, :, :width] = grad_gate
    slopes_out[0, :, width:] = grad_up
    grad_x = (dot_rows(grad_gate, w_gate[step]) + dot_rows(grad_up, w_up[step])).astype(bf16)
    for b in range(SIDE):
        there = slice(b * capacity, (b + 1) * capacity)
        grad_slots[b, target, :] = grad_x[there, :]
        mix_slots[b, target, :] = mix[there, :]
        row = jnp.sum(jnp.where(masks[b], products[there, :], 0.0), axis=0, keepdims=True)
        gate_rows[b] = jnp.where(expert_row, row, gate_rows[b])

    @pl.when(step == 1)
    def _():
        for b in range(SIDE):
            grad_blocks[b, :rows, :] = dot_cols(marks[b], grad_slots[b]).astype(bf16)
            full = gate_rows[b]
            high = full.astype(bf16)
            low = (full - high.astype(f32)).astype(bf16)
            parts = [part[i : i + 16, :] for part in (high, low) for i in range(0, experts, 16)]
            tail = jnp.concatenate(parts, axis=1)
            grad_blocks[b, rows:, : tail.shape[1]] = tail
            if tail.shape[1] < grad_blocks.shape[2]:
                grad_blocks[b, rows:, tail.shape[1] :] = jnp.zeros_like(
                    grad_blocks[b, rows:, tail.shape[1] :]
                )
            grad_copy(b).start()
            mix_blocks[b] = dot_cols(marks[b], mix_slots[b]).astype(bf16)
            mix_copy(b).start()
        for b in range(SIDE):
            grad_copy(b).wait()
            mix_copy(b).wait()


def expert_weights_kernel(*refs):
    out = refs[-1]
    groups = [refs[4 * i : 4 * i + 4] for i in range(SIDE)]
    for name in range(2):
        total = None
        for rows_in, grads, active, slopes in groups:
            term = dot_cols(rows_in[0], slopes[0]) if name == 0 else dot_cols(active[0], grads[0])
            total = term if total is None else total + term
        at = 0 if name == 0 else out.shape[1]
        out[at : at + total.shape[0], :] = total.astype(bf16)


def fold_kernel(own_lo, own_hi, before_lo, before_hi, after_lo, after_hi, *outs):
    rows = outs[0].shape[0]
    for i, out in enumerate(outs):
        part = slice(i % 2 * rows, (i % 2 + 1) * rows)
        refs = (own_lo, before_lo, after_lo) if i < 2 else (own_hi, before_hi, after_hi)
        out[...] = sum(ref[part, :].astype(f32) for ref in refs).astype(bf16)


def turn_kernel(
    term_0, term_1, term_2, term_3, shares, router, inputs, hidden_in, gain, cotangent, grad_hidden_out, out,
):
    experts, rows = shares.shape
    total = sum(ref[...].astype(f32) for ref in (term_0, term_1, term_2, term_3))
    tail = [total[rows:, i * rows : (i + 1) * rows] for i in range(experts // 8)]
    count = len(tail) // 2
    grad_share = jnp.concatenate([tail[i] + tail[i + count] for i in range(count)], axis=0)
    share = shares[...]
    grad_logits = share * (grad_share - jnp.sum(share * grad_share, axis=0, keepdims=True))
    grad_logits = grad_logits.astype(bf16)
    out[rows : rows + experts, :] = dot(grad_logits, inputs[...]).astype(bf16)
    grad = total[:rows, :] + dot_cols(grad_logits, router[...])
    hidden = hidden_in[...]
    scale = lax.rsqrt(jnp.mean(hidden * hidden, axis=1, keepdims=True) + eps_norm)
    gain_row = jnp.sum(grad * hidden * scale, axis=0, keepdims=True)
    row = lax.broadcasted_iota(jnp.int32, (16, grad.shape[1]), 0)
    out[rows + experts :, :] = jnp.where(row == 0, gain_row, 0.0).astype(bf16)
    grad = grad * gain[...]
    inner = jnp.mean(grad * hidden, axis=1, keepdims=True)
    grad = cotangent[...].astype(f32) + scale * grad - hidden * (scale * scale * scale * inner)
    grad_hidden_out[...] = grad
    out[:rows, :] = grad.astype(bf16)


def finish_kernel(at, g_0, g_1, g_2, g_3, weights, tokens, gain, grad_hidden, out):
    grad = dot_rows(g_0[...], weights[at[3]])
    for d, part in ((1, g_1), (2, g_2), (3, g_3)):
        grad = grad + dot_rows(part[...], weights[(at[3] + d) % SIDE])
    grad = grad * gain[...]
    x = tokens[...].astype(f32)
    scale = lax.rsqrt(jnp.mean(x * x, axis=1, keepdims=True) + eps_norm)
    inner = jnp.mean(grad * x, axis=1, keepdims=True)
    out[...] = grad_hidden[...] + scale * grad - x * (scale * scale * scale * inner)


def pack_kernel(
    at, normed, grads, mixed, part_0, part_1, part_2a, part_2b, part_3, w_own, gain, out, smalls,
):
    count, _, half = out.shape
    rows = mixed.shape[0] // SIDE
    cut = part_2a.shape[0]
    inner = dot_cols(normed[...], grads[...])
    outer = jnp.zeros((mixed.shape[1], normed.shape[1]), f32)
    for d, part in ((0, part_0), (1, part_1), (3, part_3)):
        outer = outer + dot_cols(mixed[place(at, d, rows), :], part[:rows, :])
        smalls[(at[3] + d) % SIDE] = part[rows:, :].astype(f32)
    far = (at[3] + 2) % SIDE * rows
    low = pl.ds(pl.multiple_of(far, 16), cut)
    outer = outer + dot_cols(mixed[low, :], part_2a[...])
    high = pl.ds(pl.multiple_of(far + cut, 16), rows - cut)
    outer = outer + dot_cols(mixed[high, :], part_2b[: rows - cut, :])
    smalls[(at[3] + 2) % SIDE] = part_2b[rows - cut :, :].astype(f32)
    small = smalls[0] + smalls[1] + smalls[2] + smalls[3]
    along = inner * w_own[...].astype(f32)
    along_hi = along.astype(bf16)
    along_lo = (along - along_hi.astype(f32)).astype(bf16)
    ones = jnp.ones((8, along.shape[1]), bf16)
    gain_1 = (dot_rows(ones, along_hi) + dot_rows(ones, along_lo)) / gain[...]
    gain_1, gain_2 = gain_1[0:1, :], small[count : count + 1, :]
    row = lax.broadcasted_iota(jnp.int32, (16, half), 0)
    gains = jnp.zeros((16, half), f32)
    for i, part in enumerate((gain_2[:, :half], gain_2[:, half:], gain_1[:, :half], gain_1[:, half:])):
        gains = jnp.where(row == 2 + i, part, gains)
    inner, outer = inner.astype(bf16), outer.astype(bf16)
    tall, short = inner.shape[0] // count, outer.shape[0] // count
    for c in range(count):
        out[c, :tall, :] = inner[c * tall : (c + 1) * tall, :]
        part = outer[c * short : (c + 1) * short, :].astype(f32)
        part = jnp.concatenate([part[:, :half], part[:, half:]], axis=0)
        out[c, tall : tall + 2 * short, :] = part.astype(bf16)
        last = jnp.where(row == 0, small[c : c + 1, :half], gains)
        last = jnp.where(row == 1, small[c : c + 1, half:], last)
        out[c, tall + 2 * short :, :] = last.astype(bf16)


def share_kernel(parts, out, last):
    total = parts[0].astype(f32)
    for i in range(1, parts.shape[0]):
        total = total + parts[i].astype(f32)
    last[...] = total[-16:, :]
    low = total.astype(bf16)
    for i in range(out.shape[0]):
        out[i] = low


def unpack_kernel(
    at, parts, last_0, last_1, last_2, last_3, query_out, key_out, value_out, output_out, router_out, gain_1_out, gain_2_out, lasts,
):
    count, size, half = parts.shape
    tall = query_out.shape[0] // count
    short = output_out.shape[0] // count
    width = query_out.shape[1]
    rows = []
    for c in range(count):
        here = slice(c * tall, (c + 1) * tall)
        part = parts[c].astype(f32)
        query_out[here, :] = part[:tall, :width]
        key_out[here, :] = part[:tall, width : width + key_out.shape[1]]
        value_out[here, :] = part[:tall, width + key_out.shape[1] :]
        here = slice(c * short, (c + 1) * short)
        output_out[here, :half] = part[tall : tall + short, :]
        output_out[here, half:] = part[tall + short : tall + 2 * short, :]
        last = part[tall + 2 * short :, :]
        rows.append(jnp.concatenate([last[0:1, :], last[1:2, :]], axis=1))
    router_out[...] = jnp.concatenate(rows, axis=0)
    for d, part in enumerate((last_0, last_1, last_2, last_3)):
        lasts[(at[3] + d) % SIDE] = part[...]
    total = lasts[0] + lasts[1] + lasts[2] + lasts[3]
    gain_1_out[:, :half] = total[4:5, :]
    gain_1_out[:, half:] = total[5:6, :]
    gain_2_out[:, :half] = last_0[2:3, :]
    gain_2_out[:, half:] = last_0[3:4, :]


def quarters_kernel(at, own, sib, *refs):
    outs, total = refs[:-1], refs[-1]
    total[...] = (own[...].astype(f32) + sib[...].astype(f32)).astype(bf16)
    rows = outs[0].shape[0]
    for i, out in enumerate(outs):
        start = (at[3] + i // 2) % SIDE * (2 * rows) + i % 2 * rows
        out[...] = total[pl.ds(pl.multiple_of(start, rows), rows), :]


def owned_kernel(own_lo, own_hi, before_lo, before_hi, after_lo, after_hi, out):
    rows = own_lo.shape[0]
    out[:rows, :] = sum(ref[...].astype(f32) for ref in (own_lo, before_lo, after_lo)).astype(bf16)
    out[rows:, :] = sum(ref[...].astype(f32) for ref in (own_hi, before_hi, after_hi)).astype(bf16)


def expert_unpack_kernel(at, own, from_after, far_lo, far_hi, from_before, gate_out, up_out, down_out, whole):
    rows = own.shape[0]
    half = far_lo.shape[0]
    whole[place(at, 0, rows), :] = own[...]
    whole[place(at, 1, rows), :] = from_after[...]
    whole[place(at, 3, rows), :] = from_before[...]
    far = (at[3] + 2) % SIDE * rows
    whole[pl.ds(pl.multiple_of(far, half), half), :] = far_lo[...]
    whole[pl.ds(pl.multiple_of(far + half, half), half), :] = far_hi[...]
    depth, width = gate_out.shape[1:]
    gate_out[0] = whole[:depth, :width].astype(f32)
    up_out[0] = whole[:depth, width:].astype(f32)
    down_out[0] = whole[depth:, :].astype(f32)


def body(
    tokens,
    cotangent,
    routes,
    lengths,
    gain_attn,
    w_query,
    w_key,
    w_value,
    w_output,
    gain_mix,
    w_router,
    gate_weight,
    up_weight,
    down_weight,
):
    rows, depth = tokens.shape
    picks = routes.shape[1]
    experts = lax.axis_size(PLANE)
    length = rows * SIDE
    width = w_query.shape[1]
    hidden_units = gate_weight.shape[2]
    capacity = min(rows, 3 * rows * picks // (2 * experts))
    core, y = lax.axis_index("core"), lax.axis_index("head")
    z, x = lax.axis_index("z"), lax.axis_index("x")
    at = jnp.stack([z, x, core, y]).astype(jnp.int32)
    gain_1, gain_2 = gain_attn[None, :], gain_mix[None, :]
    smem = pl.BlockSpec(memory_space=pltpu.SMEM)
    vmem = pl.BlockSpec(memory_space=pltpu.VMEM)
    anywhere = pl.BlockSpec(memory_space=pl.ANY)
    hbm = pl.BlockSpec(memory_space=pltpu.HBM)

    ends = jnp.cumsum(lengths[0], dtype=jnp.int32)
    index = jnp.arange(length, dtype=jnp.int32)
    starts = jnp.max(jnp.where(index[:, None] >= ends[None, :], ends[None, :], 0), axis=1)
    lane = jnp.arange(LANES)
    frequency = rope_base ** (-2.0 * (lane % (HEAD_DIM // 2)).astype(f32) / HEAD_DIM)
    angles = (index - starts).astype(f32)[:, None] * frequency[None, :]
    cosine = jnp.cos(angles)
    sine = jnp.sin(angles) * jnp.where(lane % HEAD_DIM < HEAD_DIM // 2, -1.0, 1.0)[None, :]

    def doubled(columns):
        heads = [columns[:, i : i + HEAD_DIM] for i in range(0, columns.shape[1], HEAD_DIM)]
        return jnp.concatenate([head for one in heads for head in (one, one)], axis=1)

    w_all = jnp.concatenate([w_query, doubled(w_key), doubled(w_value)], axis=1)
    w_own = jnp.concatenate([w_query, w_key, w_value], axis=1)
    router_rows = w_router.T.astype(bf16)
    router_wide = jnp.pad(w_router, ((0, 0), (0, LANES - experts))).astype(bf16)
    own_weights = [gate_weight, up_weight, down_weight]
    sib_weights = [swap_core(a) for a in own_weights]
    made = (w_all, cosine, sine, starts, w_own, router_rows, router_wide, *sib_weights)
    token_parts = ring_gather(tokens, line_shift, *made)
    named = jnp.pad(routes.T.astype(bf16), ((0, 16 - picks), (0, depth - rows)))
    grad_plane = lax.all_gather(
        jnp.concatenate([cotangent, named], axis=0), CHIPS, axis=0, tiled=True
    )
    output_all = all_blocks(after(w_output, *token_parts[2:4]), "head")

    normed, query, key, value, mixed, log_total, *mixed_out = call(
        attend_kernel,
        [
            array((length, depth), bf16),
            *[array((length, width), bf16)] * 4,
            array((length, LANES), f32),
            *[array((rows, width), bf16)] * SIDE,
        ],
        [at, *token_parts, gain_1, w_all, cosine, sine, starts[:, None]],
        specs=[smem] + [vmem] * 10,
        out_specs=[hbm] * 6 + [vmem] * 4,
        scratch=[
            *[pltpu.VMEM((length, depth), bf16)] * 2,
            *[pltpu.VMEM((length, width), bf16)] * 4,
            pltpu.VMEM((length, LANES), f32),
            pltpu.SemaphoreType.DMA((SIDE, 6)),
        ],
        flops=12 * 10**9,
    )
    mixed_in = direct_swap(mixed_out, line_shift)
    hidden, inputs = call(
        join_kernel,
        [array((rows, depth), f32), array((rows, depth), bf16)],
        [at, *mixed_in, output_all, tokens, gain_2],
        specs=[smem] + [vmem] * 7,
        flops=3 * 10**9,
    )

    u_rest = [shift_u(inputs, -1), shift_u(inputs, 2), shift_u(inputs, 1)]
    before_own, after_own = shift_w(inputs, 1), shift_w(inputs, -1)
    u_rest = jnp.concatenate(u_rest, axis=0)
    before_rest, after_rest = shift_w(u_rest, 1), shift_w(u_rest, -1)
    slots = SIDE * capacity
    half = array((length // 2 + 32, depth), bf16)

    def experts_on(distance, x_parts, mix_in):
        outs = [
            half,
            half,
            array((experts, rows), f32),
            array((SIDE * length, depth), bf16),
            array((2, slots, depth), bf16),
            array((2, slots, depth), bf16),
            array((2, slots, hidden_units), bf16),
            array((2, slots, 2 * hidden_units), bf16),
        ]
        args = [at, *x_parts, grad_plane, router_wide, *own_weights, *sib_weights]

        def fixed(a):
            return pl.BlockSpec(a.shape, lambda e: (0,) * len(a.shape))

        def by_expert(a):
            return pl.BlockSpec((1, *a.shape[1:]), lambda e: (e, 0, 0))

        specs = [smem, *[anywhere] * 3, fixed(router_wide), *[anywhere] * 6]
        aliases = {}
        if mix_in is not None:
            aliases = {len(args): 3}
            args.append(mix_in)
            specs.append(anywhere)
        return call(
            functools.partial(expert_kernel, capacity, distance),
            outs,
            args,
            specs=specs,
            grid=(2,),
            out_specs=[hbm, hbm, fixed(outs[2]), hbm, *map(by_expert, outs[4:])],
            scratch=[
                pltpu.VMEM((SIDE, rows, depth), bf16),
                pltpu.VMEM((SIDE, rows + 16, depth), bf16),
                pltpu.VMEM((2, depth, hidden_units), bf16),
                pltpu.VMEM((2, depth, hidden_units), bf16),
                pltpu.VMEM((2, hidden_units, depth), bf16),
                pltpu.VMEM((8, length), f32),
                pltpu.VMEM((8, length), f32),
                pltpu.VMEM((SIDE, experts, rows), f32),
                pltpu.VMEM((slots, depth), bf16),
                pltpu.VMEM((SIDE, 2 * capacity, rows), bf16),
                pltpu.VMEM((SIDE, 2 * capacity, depth), bf16),
                pltpu.VMEM((SIDE, 2 * capacity, depth), bf16),
                pltpu.VMEM((SIDE, rows + 16, depth), bf16),
                pltpu.VMEM((SIDE, rows, depth), bf16),
                pltpu.SemaphoreType.DMA((SIDE,)),
                pltpu.SemaphoreType.DMA((SIDE,)),
                pltpu.SemaphoreType.DMA((2, 3)),
                pltpu.SemaphoreType.DMA((SIDE,)),
                pltpu.SemaphoreType.DMA((SIDE,)),
            ],
            flops=18 * 10**9,
            aliases=aliases,
        )

    column = experts_on(0, [inputs, u_rest], None)
    far_own = shift_w(after(before_own, column[2]), 1)
    far_rest = shift_w(after(after_rest, column[2]), -1)
    right = experts_on(1, [after_own, after_rest], column[3])
    far = experts_on(2, [far_own, far_rest], right[3])
    left = experts_on(3, [before_own, before_rest], far[3])
    results = [column, right, far, left]
    mix_all = left[3]

    weight_rows = depth + hidden_units
    flat = [a for r in results for a in r[4:]]

    def expert_weights(e, earlier):
        return call(
            expert_weights_kernel,
            [array((weight_rows, depth), bf16)],
            [after(flat[0], earlier), *flat[1:]],
            specs=[pl.BlockSpec((1, *a.shape[1:]), lambda i: (e, 0, 0)) for a in flat],
            grid=(1,),
            out_specs=[pl.BlockSpec((weight_rows, depth), lambda i: (0, 0))],
            flops=10 * 10**9,
        )[0]

    sib_grads = expert_weights(1, mix_all)
    own_grads = expert_weights(0, sib_grads)
    from_before, from_after = ring_sum([(r[0], r[1]) for r in results], shift_w)
    folded = call(
        fold_kernel,
        [array((rows + 16, depth), bf16)] * SIDE,
        [after(column[0], own_grads), column[1], *from_before, *from_after],
        flops=2 * 10**9,
    )
    grad_terms = direct_swap(folded, shift_u)

    grad_hidden, grad_low = call(
        turn_kernel,
        [array((rows, depth), f32), array((rows + experts + 16, depth), bf16)],
        [*grad_terms, column[2], router_rows, inputs, hidden, gain_2, cotangent],
        flops=4 * 10**9,
    )
    grad_parts = ring_gather(grad_low, line_shift)
    sib_sums = swap_core(sib_grads)
    grads, *grads_out = call(
        attend_back_kernel,
        [array((length, 2 * width), bf16), *[array((rows, 2 * width), bf16)] * SIDE],
        [
            after(at, sib_sums),
            *grad_parts,
            w_output,
            query,
            key,
            value,
            mixed,
            log_total,
            starts[None, :],
            cosine,
            sine,
        ],
        specs=[smem] + [vmem] * 14,
        scratch=[pltpu.VMEM((length, width), bf16), pltpu.VMEM((length, width), f32)],
        flops=12 * 10**9,
    )
    grads_in = direct_swap(grads_out, line_shift)
    w_parts = lax.all_gather(after(w_own, inputs), "head", axis=0)

    tall, short = depth // experts, width // experts
    size = tall + 2 * short + 16
    packed = call(
        pack_kernel,
        [array((experts, size, depth // 2), bf16)],
        [at, normed, grads, mixed, *grad_parts, w_own, gain_1],
        specs=[smem] + [vmem] * 10,
        scratch=[pltpu.VMEM((SIDE, experts + 16, depth), f32)],
        flops=8 * 10**9,
    )[0]
    packed = after(packed, *grads_in)
    grad_tokens = call(
        finish_kernel,
        [array((rows, depth), f32)],
        [after(at, packed), *grads_in, w_parts, tokens, gain_1, grad_hidden],
        specs=[smem] + [vmem] * 8,
        flops=4 * 10**9,
    )[0]
    eighth = weight_rows // (2 * SIDE)
    quarters = call(
        quarters_kernel,
        [array((eighth, depth), bf16)] * (2 * SIDE),
        [after(at, grad_tokens), own_grads, sib_sums],
        specs=[smem] + [vmem] * 2,
        scratch=[pltpu.VMEM((weight_rows, depth), bf16)],
        flops=3 * 10**9,
    )
    pairs = [(quarters[2 * d], quarters[2 * d + 1]) for d in range(SIDE)]
    from_before, from_after = ring_sum(pairs, line_shift)
    shared, last = call(
        share_kernel,
        [array(packed.shape, bf16), array((16, depth // 2), f32)],
        [after(swap_all(packed, PLANE), *from_before, *from_after)],
        flops=2 * 10**9,
    )
    lasts = [last, line_shift(last, -1), line_shift(last, 2), line_shift(last, 1)]
    expert_owned = call(
        owned_kernel,
        [array((2 * eighth, depth), bf16)],
        [*pairs[0], *from_before, *from_after],
        flops=10**9,
    )[0]
    expert_parts = ring_gather(expert_owned, line_shift)
    expert_totals = call(
        expert_unpack_kernel,
        [
            array((1, depth, hidden_units), f32),
            array((1, depth, hidden_units), f32),
            array((1, hidden_units, depth), f32),
        ],
        [at, *expert_parts],
        specs=[smem] + [vmem] * 5,
        scratch=[pltpu.VMEM((weight_rows, depth), bf16)],
        flops=4 * 10**9,
    )
    gathered = after(swap_all(shared, PLANE), *lasts, *expert_totals)
    grad_query, grad_key, grad_value, grad_output, grad_router, grad_gain_1, grad_gain_2 = call(
        unpack_kernel,
        [
            array((depth, width), f32),
            array((depth, LANES), f32),
            array((depth, LANES), f32),
            array((width, depth), f32),
            array((experts, depth), f32),
            array((1, depth), f32),
            array((1, depth), f32),
        ],
        [at, gathered, *lasts],
        specs=[smem] + [vmem] * 5,
        scratch=[pltpu.VMEM((SIDE, 16, depth // 2), f32)],
        flops=4 * 10**9,
    )

    mixture = lax.psum_scatter(after(mix_all, *folded), CHIPS, scatter_dimension=0, tiled=True)
    output = (hidden + mixture.astype(f32)).astype(bf16)

    return (
        output,
        grad_tokens,
        grad_gain_1[0],
        grad_query,
        grad_key,
        grad_value,
        grad_output,
        grad_gain_2[0],
        grad_router.T,
        *expert_totals,
    )


def solution(mesh):
    axes = (*PLANE, "head")
    mesh = jax.sharding.Mesh(mesh.devices.reshape(SIDE, SIDE, 2, SIDE), axes)
    rows = P(axes, None)
    per_expert = P(PLANE, None, None)
    columns = P(None, "head")
    in_specs = (
        rows,
        rows,
        rows,
        P(PLANE, None),
        P(),
        columns,
        columns,
        columns,
        P("head", None),
        P(),
        P(),
        per_expert,
        per_expert,
        per_expert,
    )
    out_specs = (
        rows,
        rows,
        P(),
        columns,
        columns,
        columns,
        P("head", None),
        P(),
        P(),
        per_expert,
        per_expert,
        per_expert,
    )
    return jax.shard_map(body, mesh=mesh, in_specs=in_specs, out_specs=out_specs, check_vma=False)
```

time: 999 us -> 432 us (0.43)
  waiting for transfers between devices: 587 us -> 125 us
  Pallas kernels: 0 us -> 166 us
  matrix products: 158 us -> 0 us
  blocking collectives: 75.8 us -> 0 us
  other arithmetic: 57.3 us -> 13.6 us
  starting transfers between devices: 62.6 us -> 86.6 us
    psum x3 -> x0, waiting for transfers between devices: 310 us -> none  [summed(): return lax.psum(part.astype(bf16), axis).astype(jnp.float32)]
    all_to_all x9 -> x3, waiting for transfers between devices: 277 us -> 0.01 us  [swap_all(): return lax.all_to_all(values, axes, 0, 0, tiled=True)]
    pallas_call x0 -> x18, Pallas kernels: none -> 166 us  [call(): pl.pallas_call(kernel, out_shape=out_shapes, in_specs=specs or [whole] *...]
    dot_general x35 -> x0, matrix products: 158 us -> none  [the longest x22 107 us: wide(): return jnp.einsum(spec, left, right, preferred_element_type=jnp.float32)]
    ppermute x0 -> x49, waiting for transfers between devices: none -> 125 us  [the longest x27 84.2 us: line_shift(): return lax.ppermute(values, 'head', pairs)]
    psum x1 -> x0, blocking collectives: 65 us -> none  [summed(): return lax.psum(part.astype(bf16), axis).astype(jnp.float32)]
    ppermute x0 -> x49, starting transfers between devices: none -> 63.8 us  [the longest x27 39.1 us: line_shift(): return lax.ppermute(values, 'head', pairs)]
    all_to_all x9 -> x3, starting transfers between devices: 61.9 us -> 22.3 us  [swap_all(): return lax.all_to_all(values, axes, 0, 0, tiled=True)]
  transfers between devices with their start and end apart: 12 -> 55, of which waited for: 11 -> 21; matrix products, arithmetic and copies ran while one was open for 10% -> 5% of each run, Pallas kernels for 0% -> 39%
where the time goes in v2:
time: 432 us; the launch traced here: 428 us
  Pallas kernels  166 us (38%)
  waiting for transfers between devices  125 us (29%)
  starting transfers between devices  86.6 us (20%)
  local copies, waits for them, and re-layouts  22.1 us (5%)
  between operations  14.6 us (3%)
  other arithmetic  13.6 us (3%)
    pallas_call x18, Pallas kernels, call(): pl.pallas_call(kernel, out_shape=out_shapes, in_specs=specs or [whole] *...  166 us
    ppermute x27, waiting for transfers between devices, line_shift(): return lax.ppermute(values, 'head', pairs)  84.2 us
    ppermute x18, waiting for transfers between devices, plane_shift(): return lax.ppermute(values, PLANE, pairs)  40.3 us
    ppermute x27, starting transfers between devices, line_shift(): return lax.ppermute(values, 'head', pairs)  39.1 us
    ppermute x18, starting transfers between devices, plane_shift(): return lax.ppermute(values, PLANE, pairs)  24 us
    all_to_all x3, starting transfers between devices, swap_all(): return lax.all_to_all(values, axes, 0, 0, tiled=True)  22.3 us
    unnamed x98, local copies, waits for them, and re-layouts  13.3 us
  transfers between devices with their start and end apart: 55, of which 21 were waited for; matrix products, arithmetic and copies ran while one was open for 5% of the time, Pallas kernels for 39%

profile of v2, /device:TPU:4, one launch (start us, length us, event | category | flops | bytes accessed | tf_op | source)
XLA Modules:
  0.0 427.9 jit_solution(2710919738641769154)
XLA Ops:
  20.9 4.4 %collective-permute-done.from_before = bf16[256,1024]{1,0:T(8,128)(2,1)} collective-permute-done((bf16[256,1024]{1,0:T(8,128)(2,1)}, bf16[256,1024]{1,0:T(8,128)(2,1)}, u32[]{:S(2)}, u32[]{:S(2)}) %collective-permute-start) | collective-permute-done | bytes 524320 | tf_op jit(solution)/shard_map/ppermute | solution.py:63
  30.6 4.2 collective-permute-done.5.far_lo
  37.2 4.5 %all-to-all-start = ((bf16[4,256,1024]{2,1,0:T(8,128)(2,1)}), bf16[4,256,1024]{2,1,0:T(8,128)(2,1)S(1)}, u32[]{:S(2)}, u32[]{:S(2)}) async-start(bf16[4,256,1024]{2,1,0:T(8,128)(2,1)} %broadcast_in_dim.44), calls=%async_computation | async-start | bytes 4194304 | tf_op jit(solution)/shard_map/all_to_all | solution.py:113
  43.8 13.1 %shard_map.229 = (bf16[1024,1024]{1,0:T(8,128)(2,1)}, bf16[1024,256]{1,0:T(8,128)(2,1)}, bf16[1024,256]{1,0:T(8,128)(2,1)}, bf16[1024,256]{1,0:T(8,128)(2,1)}, b...) custom-call(s32[4]{0:T(128)} %pad_add_fusion.at, ...), custom_call_target="tpu_custom_call" | custom-call | flops 12000000000 | bytes 9969680 | tf_op jit(solution)/shard_map/pallas_call | solution.py:40
  61.9 7.1 %collective-permute-done.7.mixed_1 = bf16[256,256]{1,0:T(8,128)(2,1)S(1)} collective-permute-done((bf16[256,256]{1,0:T(8,128)(2,1)}, bf16[256,256]{1,0:T(8,128)(2,1)S(1)}, u32[]{:S(2)}, u32[]{:S(2)}) %collective-permute-start.7) | collective-permute-done | bytes 131104 | tf_op jit(solution)/shard_map/ppermute | solution.py:63
  73.2 3.9 shard_map.230
  77.1 4.0 collective-permute-start.11
  85.3 8.9 %collective-permute-done.11 = bf16[256,1024]{1,0:T(8,128)(2,1)S(1)} collective-permute-done((bf16[256,1024]{1,0:T(8,128)(2,1)}, bf16[256,1024]{1,0:T(8,128)(2,1)S(1)}, u32[]{:S(2)}, u32[]{:S(2)}) %collective-permute-start.11) | collective-permute-done | bytes 524320 | tf_op jit(solution)/shard_map/ppermute | solution.py:75
  98.3 4.4 %collective-permute-done.13 = bf16[256,1024]{1,0:T(8,128)(2,1)S(1)} collective-permute-done((bf16[256,1024]{1,0:T(8,128)(2,1)}, bf16[256,1024]{1,0:T(8,128)(2,1)S(1)}, u32[]{:S(2)}, u32[]{:S(2)}) %collective-permute-start.13) | collective-permute-done | bytes 524320 | tf_op jit(solution)/shard_map/ppermute | solution.py:75
  105.6 17.3 %shard_map.231 = (bf16[544,1024]{1,0:T(8,128)(2,1)}, bf16[544,1024]{1,0:T(8,128)(2,1)}, f32[32,256]{1,0:T(8,128)}, bf16[4096,1024]{1,0:T(8,128)(2,1)}, bf16[2,38...) custom-call(s32[4]{0:T(128)} %pad_add_fusion.at, ...), custom_call_target="tpu_custom_call" | custom-call | flops 17999998976 | bytes 33718288 | tf_op jit(solution)/shard_map/pallas_call | solution.py:40
  126.5 16.8 %shard_map.232 = (bf16[544,1024]{1,0:T(8,128)(2,1)}, bf16[544,1024]{1,0:T(8,128)(2,1)}, f32[32,256]{1,0:T(8,128)}, bf16[4096,1024]{1,0:T(8,128)(2,1)}, bf16[2,38...) custom-call(s32[4]{0:T(128)} %pad_add_fusion.at, ...), custom_call_target="tpu_custom_call", output_to_operand_aliasing={{3}: (11, {})} | custom-call | flops 17999998976 | bytes 42106896 | tf_op jit(solution)/shard_map/pallas_call | solution.py:40
  146.1 17.1 %shard_map.233 = (bf16[544,1024]{1,0:T(8,128)(2,1)}, bf16[544,1024]{1,0:T(8,128)(2,1)}, f32[32,256]{1,0:T(8,128)}, bf16[4096,1024]{1,0:T(8,128)(2,1)}, bf16[2,38...) custom-call(s32[4]{0:T(128)} %pad_add_fusion.at, ...), custom_call_target="tpu_custom_call", output_to_operand_aliasing={{3}: (11, {})} | custom-call | flops 17999998976 | bytes 42106896 | tf_op jit(solution)/shard_map/pallas_call | solution.py:40
  167.8 17.1 %shard_map.234 = (bf16[544,1024]{1,0:T(8,128)(2,1)}, bf16[544,1024]{1,0:T(8,128)(2,1)}, f32[32,256]{1,0:T(8,128)}, bf16[4096,1024]{1,0:T(8,128)(2,1)}, bf16[2,38...) custom-call(s32[4]{0:T(128)} %pad_add_fusion.at, ...), custom_call_target="tpu_custom_call", output_to_operand_aliasing={{3}: (11, {})} | custom-call | flops 17999998976 | bytes 42106896 | tf_op jit(solution)/shard_map/pallas_call | solution.py:40
  190.1 12.5 %shard_map.235 = bf16[1536,1024]{1,0:T(8,128)(2,1)} custom-call(bf16[2,384,1024]{2,1,0:T(8,128)(2,1)} %get-tuple-element.134.refs_0_, bf16[2,384,1024]{2,1,0:T(8,128)(2,1)} %get-tuple-element.119.refs_1_, bf16[2,384,512]{2,1,0:T(8,128)(2,1)} %get-tuple-element.120.refs_2_, bf16[2,384,1024]{2,1,0:T(8,128)(2,1)} %get-tuple-element.121.refs_3_, ...), custom_call_target="tpu_custom_call" | custom-call | flops 10000000000 | bytes 25165824 | tf_op jit(solution)/shard_map/pallas_call | solution.py:40
  202.6 12.5 %shard_map.236.own = bf16[1536,1024]{1,0:T(8,128)(2,1)} custom-call(bf16[2,384,1024]{2,1,0:T(8,128)(2,1)} %get-tuple-element.134.refs_0_, bf16[2,384,1024]{2,1,0:T(8,128)(2,1)} %get-tuple-element.119.refs_1_, bf16[2,384,512]{2,1,0:T(8,128)(2,1)} %get-tuple-element.120.refs_2_, bf16[2,384,1024]{2,1,0:T(8,128)(2,1)} %get-tuple-element.121.refs_3_, ...), custom_call_target="tpu_custom_call" | custom-call | flops 10000000000 | bytes 25165824 | tf_op jit(solution)/shard_map/pallas_call | solution.py:40
  216.2 4.5 %shard_map.237 = (bf16[272,1024]{1,0:T(8,128)(2,1)}, bf16[272,1024]{1,0:T(8,128)(2,1)}, bf16[272,1024]{1,0:T(8,128)(2,1)}, bf16[272,1024]{1,0:T(8,128)(2,1)}) custom-call(bf16[544,1024]{1,0:T(8,128)(2,1)} %get-tuple-element.135.own_lo, bf16[544,1024]{1,0:T(8,128)(2,1)} %get-tuple-element.136.own_hi, bf16[544,1024]{1,0:T(8,128)(2,1)} %collective-permute-done.20.before_lo, ...), custom_call_target="tpu_custom_call" | custom-call | flops 2000000000 | bytes 8912896 | tf_op jit(solution)/shard_map/pallas_call | solution.py:40
  226.0 9.2 %collective-permute-done.26.term_1 = bf16[272,1024]{1,0:T(8,128)(2,1)S(1)} collective-permute-done((bf16[272,1024]{1,0:T(8,128)(2,1)S(1)}, bf16[272,1024]{1,0:T(8,128)(2,1)S(1)}, u32[]{:S(2)}, u32[]{:S(2)}) %collective-permute-start.26) | collective-permute-done | bytes 557088 | tf_op jit(solution)/shard_map/ppermute | solution.py:75
  235.1 13.2 %collective-permute-done.28.term_3 = bf16[272,1024]{1,0:T(8,128)(2,1)S(1)} collective-permute-done((bf16[272,1024]{1,0:T(8,128)(2,1)S(1)}, bf16[272,1024]{1,0:T(8,128)(2,1)S(1)}, u32[]{:S(2)}, u32[]{:S(2)}) %collective-permute-start.28) | collective-permute-done | bytes 557088 | tf_op jit(solution)/shard_map/ppermute | solution.py:75
  249.2 4.5 %shard_map.238 = (f32[256,1024]{1,0:T(8,128)}, bf16[304,1024]{1,0:T(8,128)(2,1)}) custom-call(bf16[272,1024]{1,0:T(8,128)(2,1)} %get-tuple-element.143.term_0, bf16[272,1024]{1,0:T(8,128)(2,1)} %copy-done.23, bf16[272,1024]{1,0:T(8,128)(2,1)} %copy-done.24, bf16[272,1024]{1,0:T(8,128)(2,1)} %copy-done.25, f32[32,256]{1,0:T(8,128)} %get-tuple-element.109.shares, ...), custom_call_target="tpu_custom_call" | custom-call | flops 4000000000 | bytes 6098944 | tf_op jit(solution)/shard_map/pallas_call | solution.py:40
  256.8 11.9 %collective-permute-done.29.part_1 = bf16[304,1024]{1,0:T(8,128)(2,1)S(1)} collective-permute-done((bf16[304,1024]{1,0:T(8,128)(2,1)}, bf16[304,1024]{1,0:T(8,128)(2,1)S(1)}, u32[]{:S(2)}, u32[]{:S(2)}) %collective-permute-start.29) | collective-permute-done | bytes 622624 | tf_op jit(solution)/shard_map/ppermute | solution.py:63
  272.5 7.9 %collective-permute-done.31.part_2a = bf16[144,1024]{1,0:T(8,128)(2,1)S(1)} collective-permute-done((bf16[144,1024]{1,0:T(8,128)(2,1)S(1)}, bf16[144,1024]{1,0:T(8,128)(2,1)S(1)}, u32[]{:S(2)}, u32[]{:S(2)}) %collective-permute-start.31) | collective-permute-done | bytes 294944 | tf_op jit(solution)/shard_map/ppermute | solution.py:63
  281.2 13.9 %shard_map.239 = (bf16[1024,512]{1,0:T(8,128)(2,1)}, bf16[256,512]{1,0:T(8,128)(2,1)}, bf16[256,512]{1,0:T(8,128)(2,1)}, bf16[256,512]{1,0:T(8,128)(2,1)}, bf16[256,512]{1,0:T(8,128)(2,1)}) custom-call(s32[4]{0:T(128)} %pad_add_fusion.at, bf16[304,1024]{1,0:T(8,128)(2,1)} %get-tuple-element.150.part_0, bf16[304,1024]{1,0:T(8,128)(2,1)} %copy-done.14, ...), custom_call_target="tpu_custom_call" | custom-call | flops 12000000000 | bytes 8785936 | tf_op jit(solution)/shard_map/pallas_call | solution.py:40
  297.3 7.1 %shard_map.240 = bf16[32,64,512]{2,1,0:T(8,128)(2,1)} custom-call(s32[4]{0:T(128)} %pad_add_fusion.at, bf16[1024,1024]{1,0:T(8,128)(2,1)} %get-tuple-element.148.normed, bf16[1024,512]{1,0:T(8,128)(2,1)} %get-tuple-element.156.grads, bf16[1024,256]{1,0:T(8,128)(2,1)} %get-tuple-element.154.mixed, bf16[304,1024]{1,0:T(8,128)(2,1)} %get-tuple-element.150.part_0, ...), custom_call_target="tpu_custom_call" | custom-call | flops 8000000000 | bytes 9310224 | tf_op jit(solution)/shard_map/pallas_call | solution.py:40
  307.7 10.4 %all-to-all-start.1 = ((bf16[32,64,512]{2,1,0:T(8,128)(2,1)}), bf16[32,64,512]{2,1,0:T(8,128)(2,1)S(1)}, u32[]{:S(2)}, u32[]{:S(2)}) async-start(bf16[32,64,512]{2,1,0:T(8,128)(2,1)} %shard_map.240), calls=%async_computation.2 | async-start | bytes 4194304 | tf_op jit(solution)/shard_map/all_to_all | solution.py:113
  318.2 5.4 %shard_map.241 = f32[256,1024]{1,0:T(8,128)} custom-call(s32[4]{0:T(128)} %pad_add_fusion.at, bf16[256,512]{1,0:T(8,128)(2,1)} %get-tuple-element.157.g_0, bf16[256,512]{1,0:T(8,128)(2,1)} %copy-done.36, bf16[256,512]{1,0:T(8,128)(2,1)} %copy-done.37, bf16[256,512]{1,0:T(8,128)(2,1)} %copy-done.38, bf16[4,1024,512]{2,1,0:T(8,128)(2,1)} %bitcast.21, ...), custom_call_target="tpu_custom_call" | custom-call | flops 4000000000 | bytes 7868432 | tf_op jit(solution)/shard_map/pallas_call | solution.py:40
  323.6 6.2 %shard_map.242 = (bf16[192,1024]{1,0:T(8,128)(2,1)}, bf16[192,1024]{1,0:T(8,128)(2,1)}, bf16[192,1024]{1,0:T(8,128)(2,1)}, bf16[192,1024]{1,0:T(8,128)(2,1)}, bf...) custom-call(s32[4]{0:T(128)} %pad_add_fusion.at, ...), custom_call_target="tpu_custom_call" | custom-call | flops 3000000000 | bytes 9437200 | tf_op jit(solution)/shard_map/pallas_call | solution.py:40
  336.3 6.9 %collective-permute-done.36 = bf16[192,1024]{1,0:T(8,128)(2,1)S(1)} collective-permute-done((bf16[192,1024]{1,0:T(8,128)(2,1)}, bf16[192,1024]{1,0:T(8,128)(2,1)S(1)}, u32[]{:S(2)}, u32[]{:S(2)}) %collective-permute-start.36) | collective-permute-done | bytes 393248 | tf_op jit(solution)/shard_map/ppermute | solution.py:63
  351.6 7.6 %collective-permute-done.37.before_lo = bf16[192,1024]{1,0:T(8,128)(2,1)S(1)} collective-permute-done((bf16[192,1024]{1,0:T(8,128)(2,1)S(1)}, bf16[192,1024]{1,0:T(8,128)(2,1)S(1)}, u32[]{:S(2)}, u32[]{:S(2)}) %collective-permute-start.37) | collective-permute-done | bytes 393248 | tf_op jit(solution)/shard_map/ppermute | solution.py:63
  363.9 7.4 %all-to-all-start.2 = ((bf16[32,64,512]{2,1,0:T(8,128)(2,1)}), bf16[32,64,512]{2,1,0:T(8,128)(2,1)S(1)}, u32[]{:S(2)}, u32[]{:S(2)}) async-start(bf16[32,64,512]{2,1,0:T(8,128)(2,1)} %get-tuple-element.173), calls=%async_computation.3 | async-start | bytes 4194304 | tf_op jit(solution)/shard_map/all_to_all | solution.py:113
  377.3 17.9 %collective-permute-done.46.from_before = bf16[384,1024]{1,0:T(8,128)(2,1)S(1)} collective-permute-done((bf16[384,1024]{1,0:T(8,128)(2,1)}, bf16[384,1024]{1,0:T(8,128)(2,1)S(1)}, u32[]{:S(2)}, u32[]{:S(2)}) %collective-permute-start.46) | collective-permute-done | bytes 786464 | tf_op jit(solution)/shard_map/ppermute | solution.py:63
  400.6 7.3 %collective-permute-done.47.far_lo = bf16[192,1024]{1,0:T(8,128)(2,1)S(1)} collective-permute-done((bf16[192,1024]{1,0:T(8,128)(2,1)S(1)}, bf16[192,1024]{1,0:T(8,128)(2,1)S(1)}, u32[]{:S(2)}, u32[]{:S(2)}) %collective-permute-start.47) | collective-permute-done | bytes 393248 | tf_op jit(solution)/shard_map/ppermute | solution.py:63
  409.4 4.9 %shard_map.245 = (f32[1,1024,512]{2,1,0:T(8,128)}, f32[1,1024,512]{2,1,0:T(8,128)}, f32[1,512,1024]{2,1,0:T(8,128)}) custom-call(s32[4]{0:T(128)} %pad_add_fusion.at, bf16[384,1024]{1,0:T(8,128)(2,1)} %shard_map.244.own, bf16[384,1024]{1,0:T(8,128)(2,1)} %copy-done.13, bf16[192,1024]{1,0:T(8,128)(2,1)} %copy-done.30, bf16[192,1024]{1,0:T(8,128)(2,1)} %copy-done.31, ...), custom_call_target="tpu_custom_call" | custom-call | flops 4000000000 | bytes 9437200 | tf_op jit(solution)/shard_map/pallas_call | solution.py:40
  (226 shorter events, 119.3 us)
Async XLA Ops:
  7.2 98.4 %all-gather.4.cloned.1.call-start = ((), (), s32[]{:S(2)}) async-start(), calls=%async_computation.4 | async-start | bytes 9469952 | tf_op jit(solution)/shard_map/all_gather | solution.py:647
  10.0 15.3 %collective-permute-start = (bf16[256,1024]{1,0:T(8,128)(2,1)}, bf16[256,1024]{1,0:T(8,128)(2,1)}, u32[]{:S(2)}, u32[]{:S(2)}) collective-permute-start(bf16[256,1024]{1,0:T(8,128)(2,1)} %tokens.3), channel_id=1, source_target_pairs={{0,1},{1,2},{2,3},{3,0},{4,5},{5,6},{6,7},{7,4},{8,9},{9,10},{10,1... | collective-permute-start | bytes 1572872 | tf_op jit(solution)/shard_map/ppermute | solution.py:63
  37.2 34.6 %all-to-all-start = ((bf16[4,256,1024]{2,1,0:T(8,128)(2,1)}), bf16[4,256,1024]{2,1,0:T(8,128)(2,1)S(1)}, u32[]{:S(2)}, u32[]{:S(2)}) async-start(bf16[4,256,1024]{2,1,0:T(8,128)(2,1)} %broadcast_in_dim.44), calls=%async_computation | async-start | bytes 4194304 | tf_op jit(solution)/shard_map/all_to_all | solution.py:113
  41.7 276.4 %all-gather.6.cloned.1.call-start = ((), (), s32[]{:S(2)}) async-start(), calls=%async_computation.6 | async-start | bytes 5242880 | tf_op jit(solution)/shard_map/all_gather | solution.py:807
  77.1 17.2 %collective-permute-start.11 = (bf16[256,1024]{1,0:T(8,128)(2,1)}, bf16[256,1024]{1,0:T(8,128)(2,1)S(1)}, u32[]{:S(2)}, u32[]{:S(2)}) collective-permute-start(bf16[256,1024]{1,0:T(8,128)(2,1)} %get-tuple-element.108.x_a.inputs), channel_id=1, source_target_pairs={{0,96},{4,28},{8,104},{12,4},{16,112},{20,12},{24,120},{28,20},{32... | collective-permute-start | bytes 1572872 | tf_op jit(solution)/shard_map/ppermute | solution.py:75
  81.0 16.5 %collective-permute-start.12 = (bf16[256,1024]{1,0:T(8,128)(2,1)}, bf16[256,1024]{1,0:T(8,128)(2,1)S(1)}, u32[]{:S(2)}, u32[]{:S(2)}) collective-permute-start(bf16[256,1024]{1,0:T(8,128)(2,1)} %get-tuple-element.108.x_a.inputs), channel_id=1, source_target_pairs={{0,64},{4,20},{8,72},{12,28},{16,80},{20,4},{24,88},{28,12},{32,96... | collective-permute-start | bytes 1572872 | tf_op jit(solution)/shard_map/ppermute | solution.py:75
  81.1 21.7 %collective-permute-start.13 = (bf16[256,1024]{1,0:T(8,128)(2,1)}, bf16[256,1024]{1,0:T(8,128)(2,1)S(1)}, u32[]{:S(2)}, u32[]{:S(2)}) collective-permute-start(bf16[256,1024]{1,0:T(8,128)(2,1)} %get-tuple-element.108.x_a.inputs), channel_id=1, source_target_pairs={{0,32},{4,12},{8,40},{12,20},{16,48},{20,28},{24,56},{28,4},{32,64... | collective-permute-start | bytes 1572872 | tf_op jit(solution)/shard_map/ppermute | solution.py:75
  83.1 39.8 %collective-permute-start.10 = (bf16[256,1024]{1,0:T(8,128)(2,1)}, bf16[256,1024]{1,0:T(8,128)(2,1)}, u32[]{:S(2)}, u32[]{:S(2)}) collective-permute-start(bf16[256,1024]{1,0:T(8,128)(2,1)} %get-tuple-element.108.x_a.inputs), channel_id=1, source_target_pairs={{0,8},{4,36},{8,16},{12,44},{16,24},{20,52},{24,0},{28,60},{32,40}... | collective-permute-start | bytes 1572872 | tf_op jit(solution)/shard_map/ppermute | solution.py:75
  84.4 42.0 %collective-permute-start.18 = (bf16[256,1024]{1,0:T(8,128)(2,1)}, bf16[256,1024]{1,0:T(8,128)(2,1)}, u32[]{:S(2)}, u32[]{:S(2)}) collective-permute-start(bf16[256,1024]{1,0:T(8,128)(2,1)} %get-tuple-element.108.x_a.inputs), channel_id=1, source_target_pairs={{0,24},{4,100},{8,0},{12,108},{16,8},{20,116},{24,16},{28,124},{32... | collective-permute-start | bytes 1572872 | tf_op jit(solution)/shard_map/ppermute | solution.py:75
  85.3 333.9 %reduce-scatter.2.cloned.1.call-start = ((), (), s32[]{:S(2)}) async-start(), calls=%async_computation.5 | async-start | bytes 8912896 | tf_op jit(solution)/shard_map/reduce_scatter | solution.py:882
  103.6 63.0 %collective-permute-start.14 = (bf16[768,1024]{1,0:T(8,128)(2,1)}, bf16[768,1024]{1,0:T(8,128)(2,1)S(1)}, u32[]{:S(2)}, u32[]{:S(2)}) collective-permute-start(bf16[768,1024]{1,0:T(8,128)(2,1)} %constant_dynamic-update-slice_fusion.3.x_b), channel_id=1, source_target_pairs={{0,8},{4,36},{8,16},{12,44},{16,24},{20,52},{24,0},{28,60},{32,40}... | collective-permute-start | bytes 4718600 | tf_op jit(solution)/shard_map/ppermute | solution.py:75
  104.7 20.6 %collective-permute-start.16 = (bf16[768,1024]{1,0:T(8,128)(2,1)}, bf16[768,1024]{1,0:T(8,128)(2,1)S(1)}, u32[]{:S(2)}, u32[]{:S(2)}) collective-permute-start(bf16[768,1024]{1,0:T(8,128)(2,1)} %constant_dynamic-update-slice_fusion.3.x_b), channel_id=1, source_target_pairs={{0,24},{4,100},{8,0},{12,108},{16,8},{20,116},{24,16},{28,124},{32... | collective-permute-start | bytes 4718600 | tf_op jit(solution)/shard_map/ppermute | solution.py:75
  122.9 22.2 %collective-permute-start.15 = (bf16[256,1024]{1,0:T(8,128)(2,1)}, bf16[256,1024]{1,0:T(8,128)(2,1)S(1)}, u32[]{:S(2)}, u32[]{:S(2)}) collective-permute-start(bf16[256,1024]{1,0:T(8,128)(2,1)} %collective-permute-done.10.x_a), channel_id=1, source_target_pairs={{0,8},{4,36},{8,16},{12,44},{16,24},{20,52},{24,0},{28,60},{32,40}... | collective-permute-start | bytes 1572872 | tf_op jit(solution)/shard_map/ppermute | solution.py:75
  125.4 20.7 %collective-permute-start.17 = (bf16[768,1024]{1,0:T(8,128)(2,1)S(1)}, bf16[768,1024]{1,0:T(8,128)(2,1)}, u32[]{:S(2)}, u32[]{:S(2)}) collective-permute-start(bf16[768,1024]{1,0:T(8,128)(2,1)S(1)} %collective-permute-done.16.x_b), channel_id=1, source_target_pairs={{0,24},{4,100},{8,0},{12,108},{16,8},{20,116},{24,16},{28,124},{32... | collective-permute-start | bytes 4718600 | tf_op jit(solution)/shard_map/ppermute | solution.py:75
  143.4 71.8 %collective-permute-start.21 = (bf16[544,1024]{1,0:T(8,128)(2,1)}, bf16[544,1024]{1,0:T(8,128)(2,1)}, u32[]{:S(2)}, u32[]{:S(2)}) collective-permute-start(bf16[544,1024]{1,0:T(8,128)(2,1)} %get-tuple-element.139), channel_id=1, source_target_pairs={{0,8},{4,36},{8,16},{12,44},{16,24},{20,52},{24,0},{28,60},{32,40}... | collective-permute-start | bytes 3342344 | tf_op jit(solution)/shard_map/ppermute | solution.py:75
  163.2 21.7 %collective-permute-start.19 = (bf16[544,1024]{1,0:T(8,128)(2,1)}, bf16[544,1024]{1,0:T(8,128)(2,1)}, u32[]{:S(2)}, u32[]{:S(2)}) collective-permute-start(bf16[544,1024]{1,0:T(8,128)(2,1)} %get-tuple-element.138), channel_id=1, source_target_pairs={{0,8},{4,36},{8,16},{12,44},{16,24},{20,52},{24,0},{28,60},{32,40}... | collective-permute-start | bytes 3342344 | tf_op jit(solution)/shard_map/ppermute | solution.py:75
  166.2 22.6 %collective-permute-start.23 = (bf16[544,1024]{1,0:T(8,128)(2,1)}, bf16[544,1024]{1,0:T(8,128)(2,1)S(1)}, u32[]{:S(2)}, u32[]{:S(2)}) collective-permute-start(bf16[544,1024]{1,0:T(8,128)(2,1)} %get-tuple-element.142), channel_id=1, source_target_pairs={{0,24},{4,100},{8,0},{12,108},{16,8},{20,116},{24,16},{28,124},{32... | collective-permute-start | bytes 3342344 | tf_op jit(solution)/shard_map/ppermute | solution.py:75
  184.8 30.4 %collective-permute-start.22 = (bf16[544,1024]{1,0:T(8,128)(2,1)}, bf16[544,1024]{1,0:T(8,128)(2,1)}, u32[]{:S(2)}, u32[]{:S(2)}) collective-permute-start(bf16[544,1024]{1,0:T(8,128)(2,1)} %get-tuple-element.140), channel_id=1, source_target_pairs={{0,24},{4,100},{8,0},{12,108},{16,8},{20,116},{24,16},{28,124},{32... | collective-permute-start | bytes 3342344 | tf_op jit(solution)/shard_map/ppermute | solution.py:75
  186.7 28.5 %collective-permute-start.20 = (bf16[544,1024]{1,0:T(8,128)(2,1)S(1)}, bf16[544,1024]{1,0:T(8,128)(2,1)}, u32[]{:S(2)}, u32[]{:S(2)}) collective-permute-start(bf16[544,1024]{1,0:T(8,128)(2,1)S(1)} %add_convert_fusion.1), channel_id=1, source_target_pairs={{0,8},{4,36},{8,16},{12,44},{16,24},{20,52},{24,0},{28,60},{32,40}... | collective-permute-start | bytes 3342344 | tf_op jit(solution)/shard_map/ppermute | solution.py:75
  189.2 26.0 %collective-permute-start.24 = (bf16[544,1024]{1,0:T(8,128)(2,1)S(1)}, bf16[544,1024]{1,0:T(8,128)(2,1)S(1)}, u32[]{:S(2)}, u32[]{:S(2)}) collective-permute-start(bf16[544,1024]{1,0:T(8,128)(2,1)S(1)} %add_convert_fusion), channel_id=1, source_target_pairs={{0,24},{4,100},{8,0},{12,108},{16,8},{20,116},{24,16},{28,124},{32... | collective-permute-start | bytes 3342344 | tf_op jit(solution)/shard_map/ppermute | solution.py:75
  220.8 51.7 %collective-permute-start.25 = (bf16[1536,1024]{1,0:T(8,128)(2,1)}, bf16[1536,1024]{1,0:T(8,128)(2,1)}, u32[]{:S(2)}, u32[]{:S(2)}) collective-permute-start(bf16[1536,1024]{1,0:T(8,128)(2,1)} %shard_map.235), channel_id=1, source_target_pairs={{0,4},{4,0},{1,5},{5,1},{2,6},{6,2},{3,7},{7,3},{8,12},{12,8},{9,1... | collective-permute-start | bytes 9437192 | tf_op jit(solution)/shard_map/ppermute | solution.py:83
  225.6 22.8 %collective-permute-start.28 = (bf16[272,1024]{1,0:T(8,128)(2,1)S(1)}, bf16[272,1024]{1,0:T(8,128)(2,1)S(1)}, u32[]{:S(2)}, u32[]{:S(2)}) collective-permute-start(bf16[272,1024]{1,0:T(8,128)(2,1)S(1)} %copy-done.20), channel_id=1, source_target_pairs={{0,32},{4,12},{8,40},{12,20},{16,48},{20,28},{24,56},{28,4},{32,64... | collective-permute-start | bytes 1671176 | tf_op jit(solution)/shard_map/ppermute | solution.py:75
  253.7 14.9 %collective-permute-start.29 = (bf16[304,1024]{1,0:T(8,128)(2,1)}, bf16[304,1024]{1,0:T(8,128)(2,1)S(1)}, u32[]{:S(2)}, u32[]{:S(2)}) collective-permute-start(bf16[304,1024]{1,0:T(8,128)(2,1)} %get-tuple-element.150.part_0), channel_id=1, source_target_pairs={{0,3},{1,0},{2,1},{3,2},{4,7},{5,4},{6,5},{7,6},{8,11},{9,8},{10,9... | collective-permute-start | bytes 1867784 | tf_op jit(solution)/shard_map/ppermute | solution.py:63
  256.8 15.6 %collective-permute-start.30 = (bf16[304,1024]{1,0:T(8,128)(2,1)}, bf16[304,1024]{1,0:T(8,128)(2,1)S(1)}, u32[]{:S(2)}, u32[]{:S(2)}) collective-permute-start(bf16[304,1024]{1,0:T(8,128)(2,1)} %get-tuple-element.150.part_0), channel_id=1, source_target_pairs={{0,1},{1,2},{2,3},{3,0},{4,5},{5,6},{6,7},{7,4},{8,9},{9,10},{10,1... | collective-permute-start | bytes 1867784 | tf_op jit(solution)/shard_map/ppermute | solution.py:63
  307.7 51.5 %all-to-all-start.1 = ((bf16[32,64,512]{2,1,0:T(8,128)(2,1)}), bf16[32,64,512]{2,1,0:T(8,128)(2,1)S(1)}, u32[]{:S(2)}, u32[]{:S(2)}) async-start(bf16[32,64,512]{2,1,0:T(8,128)(2,1)} %shard_map.240), calls=%async_computation.2 | async-start | bytes 4194304 | tf_op jit(solution)/shard_map/all_to_all | solution.py:113
  333.0 18.6 %collective-permute-start.38 = (bf16[192,1024]{1,0:T(8,128)(2,1)}, bf16[192,1024]{1,0:T(8,128)(2,1)S(1)}, u32[]{:S(2)}, u32[]{:S(2)}) collective-permute-start(bf16[192,1024]{1,0:T(8,128)(2,1)} %get-tuple-element.168), channel_id=1, source_target_pairs={{0,1},{1,2},{2,3},{3,0},{4,5},{5,6},{6,7},{7,4},{8,9},{9,10},{10,1... | collective-permute-start | bytes 1179656 | tf_op jit(solution)/shard_map/ppermute | solution.py:63
  333.0 18.6 %collective-permute-start.39 = (bf16[192,1024]{1,0:T(8,128)(2,1)}, bf16[192,1024]{1,0:T(8,128)(2,1)S(1)}, u32[]{:S(2)}, u32[]{:S(2)}) collective-permute-start(bf16[192,1024]{1,0:T(8,128)(2,1)} %get-tuple-element.169), channel_id=1, source_target_pairs={{0,3},{1,0},{2,1},{3,2},{4,7},{5,4},{6,5},{7,6},{8,11},{9,8},{10,9... | collective-permute-start | bytes 1179656 | tf_op jit(solution)/shard_map/ppermute | solution.py:63
  363.9 50.5 %all-to-all-start.2 = ((bf16[32,64,512]{2,1,0:T(8,128)(2,1)}), bf16[32,64,512]{2,1,0:T(8,128)(2,1)S(1)}, u32[]{:S(2)}, u32[]{:S(2)}) async-start(bf16[32,64,512]{2,1,0:T(8,128)(2,1)} %get-tuple-element.173), calls=%async_computation.3 | async-start | bytes 4194304 | tf_op jit(solution)/shard_map/all_to_all | solution.py:113
  374.1 21.1 %collective-permute-start.46 = (bf16[384,1024]{1,0:T(8,128)(2,1)}, bf16[384,1024]{1,0:T(8,128)(2,1)S(1)}, u32[]{:S(2)}, u32[]{:S(2)}) collective-permute-start(bf16[384,1024]{1,0:T(8,128)(2,1)} %shard_map.244.own), channel_id=1, source_target_pairs={{0,1},{1,2},{2,3},{3,0},{4,5},{5,6},{6,7},{7,4},{8,9},{9,10},{10,1... | collective-permute-start | bytes 2359304 | tf_op jit(solution)/shard_map/ppermute | solution.py:63
  375.0 20.3 %collective-permute-start.45 = (bf16[384,1024]{1,0:T(8,128)(2,1)}, bf16[384,1024]{1,0:T(8,128)(2,1)S(1)}, u32[]{:S(2)}, u32[]{:S(2)}) collective-permute-start(bf16[384,1024]{1,0:T(8,128)(2,1)} %shard_map.244.own), channel_id=1, source_target_pairs={{0,3},{1,0},{2,1},{3,2},{4,7},{5,4},{6,5},{7,6},{8,11},{9,8},{10,9... | collective-permute-start | bytes 2359304 | tf_op jit(solution)/shard_map/ppermute | solution.py:63
  398.6 15.7 %collective-permute-start.42 = (f32[16,512]{1,0:T(8,128)S(1)}, f32[16,512]{1,0:T(8,128)S(1)}, u32[]{:S(2)}, u32[]{:S(2)}) collective-permute-start(f32[16,512]{1,0:T(8,128)S(1)} %copy-done.42), channel_id=1, source_target_pairs={{0,3},{1,0},{2,1},{3,2},{4,7},{5,4},{6,5},{7,6},{8,11},{9,8},{10,9... | collective-permute-start | bytes 98312 | tf_op jit(solution)/shard_map/ppermute | solution.py:63
  399.1 15.2 %collective-permute-start.43 = (f32[16,512]{1,0:T(8,128)S(1)}, f32[16,512]{1,0:T(8,128)S(1)}, u32[]{:S(2)}, u32[]{:S(2)}) collective-permute-start(f32[16,512]{1,0:T(8,128)S(1)} %copy-done.42), channel_id=1, source_target_pairs={{0,2},{1,3},{2,0},{3,1},{4,6},{5,7},{6,4},{7,5},{8,10},{9,11},{10,... | collective-permute-start | bytes 98312 | tf_op jit(solution)/shard_map/ppermute | solution.py:63
  (70 other events, 532.9 us)
Sparse Core Ops, SparseCore 0:
  10.8 79.3 all-gather.3
  92.4 52.3 all-gather.5
  220.9 91.2 reduce-scatter.1

commit v3 on v2

--- a/solution.py
+++ b/solution.py
@@ -32,21 +32,18 @@
     return lax.dot_general(left, right, (((0,), (0,)), ((), ())), preferred_element_type=f32)
 
 
-def call(kernel, out_shapes, args, specs=None, grid=None, out_specs=None, scratch=(), flops=0, vmem=60, aliases=None):
+def call(kernel, out_shapes, args, specs=None, out_specs=None, scratch=(), flops=0, vmem=60):
     moved = sum(a.size * a.dtype.itemsize for a in args)
     moved += sum(s.size * s.dtype.itemsize for s in out_shapes)
     whole = pl.BlockSpec(memory_space=pltpu.VMEM)
-    settings = {} if grid is None else {"grid": grid}
     return pl.pallas_call(
         kernel,
         out_shape=out_shapes,
         in_specs=specs or [whole] * len(args),
         out_specs=out_specs or [whole] * len(out_shapes),
         scratch_shapes=list(scratch),
-        input_output_aliases=aliases or {},
         compiler_params=pltpu.CompilerParams(vmem_limit_bytes=vmem * MIB),
         cost_estimate=pl.CostEstimate(flops=flops, bytes_accessed=moved, transcendentals=0),
-        **settings,
     )(*args)
 
 
@@ -83,17 +80,17 @@
     return lax.ppermute(values, "core", [(0, 1), (1, 0)])
 
 
-def after(values, *earlier):
-    return lax.optimization_barrier((values, *earlier))[0]
+def together(*values):
+    return lax.optimization_barrier(values)
 
 
 def ring_gather(block, shift, *between):
     half = block.shape[0] // 32 * 16
     from_before, from_after = shift(block, 1), shift(block, -1)
-    if between:
-        from_before, from_after, *_ = lax.optimization_barrier((from_before, from_after, *between))
+    from_before, from_after, *between = together(from_before, from_after, *between)
     far_lo, far_hi = shift(from_before[:half], 1), shift(from_after[half:], -1)
-    return block, from_after, far_lo, far_hi, from_before
+    parts = [block, from_after, far_lo, far_hi, from_before]
+    return (parts, between) if between else parts
 
 
 def direct_swap(parts, shift):
@@ -106,7 +103,7 @@
     up = (parts[1][0].astype(f32) + low_in.astype(f32)).astype(bf16)
     down = (parts[3][1].astype(f32) + high_in.astype(f32)).astype(bf16)
     before_low, after_high = shift(up, 1), shift(down, -1)
-    return (before_low, before_high), (after_low, after_high)
+    return (before_low, before_high), (after_low, after_high), (up, down)
 
 
 def swap_all(values, axes):
@@ -133,12 +130,21 @@
     return jnp.concatenate(out, axis=1)
 
 
+def twice(values):
+    lane = lax.broadcasted_iota(jnp.int32, values.shape, 1)
+    swapped = pltpu.roll(values, HEAD_DIM, 1)
+    first = lane < HEAD_DIM
+    return jnp.concatenate(
+        [jnp.where(first, values, swapped), jnp.where(first, swapped, values)], axis=1
+    )
+
+
 def place(at, distance, rows):
     return pl.ds(pl.multiple_of((at[3] + distance) % SIDE * rows, rows), rows)
 
 
 def attend_kernel(
-    at, own, from_after, far_lo, far_hi, from_before, gain, weights, cosine, sine, starts,
+    at, own, from_after, far_lo, far_hi, from_before, gain, w_query, w_key, w_value, cosine, sine, starts,
     normed_out, query_out, key_out, value_out, mixed_out, log_out, mixed_0, mixed_1, mixed_2, mixed_3,
     rows_in, normed, query, key, value, mixed, log_total, sems,
 ):
@@ -167,12 +173,12 @@
         scale = lax.rsqrt(jnp.mean(x * x, axis=1, keepdims=True) + eps_norm)
         low = (x * scale * gain[...]).astype(bf16)
         normed[here, :] = low
-        raw = dot(low, weights[...])
-        q = rope(raw[:, :width], cosine[here, :], sine[here, :]).astype(bf16)
+        q = rope(dot(low, w_query[...]), cosine[here, :], sine[here, :]).astype(bf16)
         q = q * jnp.asarray(HEAD_DIM**-0.5, bf16)
         query[here, :] = q
-        key[here, :] = rope(raw[:, width : 2 * width], cosine[here, :], sine[here, :]).astype(bf16)
-        value[here, :] = raw[:, 2 * width :].astype(bf16)
+        raw = rope(dot(low, w_key[...]), cosine[here, :], sine[here, :])
+        key[here, :] = twice(raw).astype(bf16)
+        value[here, :] = twice(dot(low, w_value[...])).astype(bf16)
         column = lax.broadcasted_iota(jnp.int32, (rows, extent), 1)
         row = i * rows + lax.broadcasted_iota(jnp.int32, (rows, extent), 0)
         bias = jnp.where((column >= starts[here, :]) & (column <= row), 0.0, mask_fill)
@@ -267,22 +273,26 @@
 
 
 def join_kernel(
-    at, mixed_0, mixed_1, mixed_2, mixed_3, weights, tokens, gain, hidden_out, inputs_out,
+    at, mixed_0, mixed_1, mixed_2, mixed_3, weights, sib_weights, tokens, gain, hidden_out, inputs_out,
 ):
+    half = weights.shape[1]
+    mine = pl.ds(pl.multiple_of(at[2] * half, half), half)
+    other = pl.ds(pl.multiple_of((1 - at[2]) * half, half), half)
     hidden = tokens[...].astype(f32)
     for d, part in enumerate((mixed_0, mixed_1, mixed_2, mixed_3)):
-        hidden = hidden + dot(part[...], weights[(at[3] + d) % SIDE])
+        owner = (at[3] + d) % SIDE
+        hidden = hidden + dot(part[:, mine], weights[owner])
+        hidden = hidden + dot(part[:, other], sib_weights[owner])
     scale = lax.rsqrt(jnp.mean(hidden * hidden, axis=1, keepdims=True) + eps_norm)
     hidden_out[...] = hidden
     inputs_out[...] = (hidden * scale * gain[...]).astype(bf16)
 
 
-def expert_kernel(capacity, distance, at, x_a, x_b, g_all, router, *refs):
+def expert_kernel(capacity, at, x_a, x_b, g_a, g_b, router, *refs):
     own, sib = refs[:3], refs[3:6]
-    (grad_lo, grad_hi, share_out, mix_all, rows_out, grads_out, active_out, slopes_out,
-     x_blocks, g_blocks, w_gate, w_up, w_down, share, slots, gate_rows, g_rows, marks, grad_slots, mix_slots,
-     grad_blocks, mix_blocks, x_sem, g_sem, w_sem, mix_sem, grad_sem) = refs[6 if distance == 0 else 7 :]
-    step = pl.program_id(0)
+    (grad_lo, grad_hi, share_out, mix_out, rows_out, grads_out, active_out, slopes_out,
+     x_blocks, g_blocks, w_gate, w_up, w_down, taken_x, taken_g, grads, active, slopes, marks, grad_slots, mix_slots,
+     grad_blocks, mix_blocks, x_sem, g_sem, w_sem, mix_sem, grad_sem, save_sem) = refs[6:]
     rows = x_a.shape[0]
     picks = 8
     experts = share_out.shape[0]
@@ -290,151 +300,156 @@
     z, x, core = at[0], at[1], at[2]
     me = (z * SIDE + x) * 2 + core
     ids = (me, me + 1 - 2 * core)
-    first_core = core == 0
-    u, w = jnp.where(first_core, z, x), jnp.where(first_core, x, z)
     x_from = (x_a, *[x_b.at[pl.ds(b * rows, rows), :] for b in range(SIDE - 1)])
-
-    def source(b):
-        there, away = (u + b) % SIDE, (w + distance) % SIDE
-        return jnp.where(first_core, there * SIDE + away, away * SIDE + there)
+    g_from = (g_a, *[g_b.at[pl.ds(b * taken, taken), :] for b in range(SIDE - 1)])
+    saved = ((taken_x, rows_out), (grads, grads_out), (active, active_out), (slopes, slopes_out))
 
     def x_copy(b):
         return pltpu.make_async_copy(x_from[b], x_blocks.at[b], x_sem.at[b])
 
     def g_copy(b):
-        there = pl.ds(pl.multiple_of(source(b) * taken, taken), taken)
-        return pltpu.make_async_copy(g_all.at[there, :], g_blocks.at[b], g_sem.at[b])
+        return pltpu.make_async_copy(g_from[b], g_blocks.at[b], g_sem.at[b])
 
     def w_copy(e, n):
         there = (w_gate, w_up, w_down)[n].at[e]
         return pltpu.make_async_copy((own, sib)[e][n].at[0], there, w_sem.at[e, n])
 
     def mix_copy(b):
-        there = pl.ds(pl.multiple_of(source(b) * rows, rows), rows)
-        return pltpu.make_async_copy(mix_blocks.at[b], mix_all.at[there, :], mix_sem.at[b])
+        there = mix_out.at[pl.ds(b * rows, rows), :]
+        return pltpu.make_async_copy(mix_blocks.at[b], there, mix_sem.at[b])
 
     def grad_copy(b):
         out = grad_lo if b < SIDE // 2 else grad_hi
         there = pl.ds(b % (SIDE // 2) * taken, taken)
         return pltpu.make_async_copy(grad_blocks.at[b], out.at[there, :], grad_sem.at[b])
 
-    @pl.when(step == 0)
-    def _():
-        for b in range(SIDE):
-            x_copy(b).start()
-            g_copy(b).start()
-        for e in range(2):
-            for n in range(3):
-                w_copy(e, n).start()
-        gate_rows[...] = jnp.zeros_like(gate_rows)
-        expert = lax.broadcasted_iota(jnp.int32, (experts, rows), 0)
-        token = lax.broadcasted_iota(jnp.int32, (rows, rows), 0)
-        earlier = token < lax.broadcasted_iota(jnp.int32, (rows, rows), 1)
-        earlier = earlier.astype(f32).astype(bf16)
-        for b in range(SIDE):
-            here = slice(b * rows, (b + 1) * rows)
-            x_copy(b).wait()
-            g_copy(b).wait()
-            named = g_blocks[b, rows : rows + picks, :rows].astype(f32).astype(jnp.int32)
-            used = jnp.zeros((experts, rows), f32)
-            for p in range(picks):
-                used = jnp.where(named[p : p + 1, :] == expert, 1.0, used)
-            rank = jnp.where(used > 0, dot(used.astype(bf16), earlier), -1.0)
-            logits = jnp.transpose(dot(x_blocks[b], router[...]))[:experts, :]
-            peak = jnp.max(jnp.where(used > 0, logits, mask_fill), axis=0, keepdims=True)
-            raised = jnp.where(used > 0, jnp.exp(jnp.minimum(logits - peak, 0.0)), 0.0)
-            ratio = raised / jnp.sum(raised, axis=0, keepdims=True)
-            if b == 0:
-                share_out[...] = ratio
-            for e in range(2):
-                mine = expert == ids[e]
-                share[e : e + 1, here] = jnp.sum(jnp.where(mine, ratio, 0.0), axis=0, keepdims=True)
-                slots[e : e + 1, here] = jnp.sum(jnp.where(mine, rank, 0.0), axis=0, keepdims=True)
+    def save(e, n):
+        return pltpu.make_async_copy(saved[n][0].at[e], saved[n][1].at[e], save_sem.at[e, n])
+
+    for b in range(SIDE):
+        g_copy(b).start()
+        x_copy(b).start()
+    for e in range(2):
         for n in range(3):
-            w_copy(0, n).wait()
-
-    @pl.when(step == 1)
-    def _():
-        for n in range(3):
-            w_copy(1, n).wait()
-
-    slot_index = lax.broadcasted_iota(jnp.int32, (capacity, rows), 0).astype(f32)
-    shares, slots_here = share[pl.ds(step, 1), :], slots[pl.ds(step, 1), :]
-    target = pl.ds(pl.multiple_of(step * capacity, capacity), capacity)
-    expert_row = lax.broadcasted_iota(jnp.int32, (experts, rows), 0)
-    expert_row = expert_row == jnp.where(step == 0, ids[0], ids[1])
-    gates, masks = [], []
-    for b in range(SIDE):
-        here = slice(b * rows, (b + 1) * rows)
-        there = slice(b * capacity, (b + 1) * capacity)
-        mask = slot_index == slots_here[:, here]
-        masks.append(mask)
-        mark = mask.astype(f32).astype(bf16)
-        marks[b, target, :] = mark
-        rows_out[0, there, :] = dot(mark, x_blocks[b]).astype(bf16)
-        g_rows[there, :] = dot(mark, g_blocks[b, :rows, :]).astype(bf16)
-        gates.append(jnp.sum(jnp.where(mask, shares[:, here], 0.0), axis=1, keepdims=True))
-    gate = jnp.concatenate(gates, axis=0)
-    x = rows_out[0]
-    gate_pre = dot(x, w_gate[step])
-    up_pre = dot(x, w_up[step])
-    sigmoid = 1.0 / (1.0 + jnp.exp(-gate_pre))
-    silu = gate_pre * sigmoid
-    active = (silu * up_pre).astype(bf16)
-    active_out[0] = active
-    produced = dot(active, w_down[step]).astype(bf16).astype(f32)
-    wide_g = g_rows[...].astype(f32)
-    products = jnp.sum(wide_g * produced, axis=1, keepdims=True)
-    grad_produced = (gate * wide_g).astype(bf16)
-    grads_out[0] = grad_produced
-    mix = (gate * produced).astype(bf16)
-    grad_active = dot_rows(grad_produced, w_down[step])
-    grad_up = (grad_active * silu).astype(bf16)
-    slope = sigmoid * (1.0 + gate_pre * (1.0 - sigmoid))
-    grad_gate = (grad_active * up_pre * slope).astype(bf16)
-    width = grad_gate.shape[1]
-    slopes_out[0, :, :width] = grad_gate
-    slopes_out[0, :, width:] = grad_up
-    grad_x = (dot_rows(grad_gate, w_gate[step]) + dot_rows(grad_up, w_up[step])).astype(bf16)
+            w_copy(e, n).start()
+
+    expert = lax.broadcasted_iota(jnp.int32, (experts, rows), 0)
+    token = lax.broadcasted_iota(jnp.int32, (rows, rows), 0)
+    earlier = token < lax.broadcasted_iota(jnp.int32, (rows, rows), 1)
+    earlier = earlier.astype(f32).astype(bf16)
+    slot = lax.broadcasted_iota(jnp.int32, (capacity, rows), 0).astype(f32)
+    gates, masks = ([], []), ([], [])
     for b in range(SIDE):
         there = slice(b * capacity, (b + 1) * capacity)
-        grad_slots[b, target, :] = grad_x[there, :]
-        mix_slots[b, target, :] = mix[there, :]
-        row = jnp.sum(jnp.where(masks[b], products[there, :], 0.0), axis=0, keepdims=True)
-        gate_rows[b] = jnp.where(expert_row, row, gate_rows[b])
-
-    @pl.when(step == 1)
-    def _():
+        g_copy(b).wait()
+        named = g_blocks[b, rows : rows + picks, :rows].astype(f32).astype(jnp.int32)
+        used = jnp.zeros((experts, rows), f32)
+        for p in range(picks):
+            used = jnp.where(named[p : p + 1, :] == expert, 1.0, used)
+        rank = jnp.where(used > 0, dot(used.astype(bf16), earlier), -1.0)
+        x_copy(b).wait()
+        logits = jnp.transpose(dot(x_blocks[b], router[...]))[:experts, :]
+        peak = jnp.max(jnp.where(used > 0, logits, mask_fill), axis=0, keepdims=True)
+        raised = jnp.where(used > 0, jnp.exp(jnp.minimum(logits - peak, 0.0)), 0.0)
+        ratio = raised / jnp.sum(raised, axis=0, keepdims=True)
+        if b == 0:
+            share_out[...] = ratio
+        for e in range(2):
+            mine = expert == ids[e]
+            place_row = jnp.sum(jnp.where(mine, rank, 0.0), axis=0, keepdims=True)
+            share_row = jnp.sum(jnp.where(mine, ratio, 0.0), axis=0, keepdims=True)
+            mask = slot == place_row
+            masks[e].append(mask)
+            marks[b, e * capacity : (e + 1) * capacity, :] = mask.astype(f32).astype(bf16)
+            gates[e].append(jnp.sum(jnp.where(mask, share_row, 0.0), axis=1, keepdims=True))
+        both = dot(marks[b], x_blocks[b]).astype(bf16)
+        taken_x[0, there, :], taken_x[1, there, :] = both[:capacity, :], both[capacity:, :]
+        both = dot(marks[b], g_blocks[b, :rows, :]).astype(bf16)
+        taken_g[0, there, :], taken_g[1, there, :] = both[:capacity, :], both[capacity:, :]
+    products = []
+    for e in range(2):
+        save(e, 0).start()
+        gate = jnp.concatenate(gates[e], axis=0)
+        here = slice(e * capacity, (e + 1) * capacity)
+        w_copy(e, 0).wait()
+        w_copy(e, 1).wait()
+        gate_pre = dot(taken_x[e], w_gate[e])
+        up_pre = dot(taken_x[e], w_up[e])
+        sigmoid = 1.0 / (1.0 + jnp.exp(-gate_pre))
+        silu = gate_pre * sigmoid
+        active[e] = (silu * up_pre).astype(bf16)
+        save(e, 2).start()
+        w_copy(e, 2).wait()
+        produced = dot(active[e], w_down[e]).astype(bf16).astype(f32)
+        wide_g = taken_g[e].astype(f32)
+        products.append(jnp.sum(wide_g * produced, axis=1, keepdims=True))
+        grads[e] = (gate * wide_g).astype(bf16)
+        save(e, 1).start()
+        mix = (gate * produced).astype(bf16)
         for b in range(SIDE):
-            grad_blocks[b, :rows, :] = dot_cols(marks[b], grad_slots[b]).astype(bf16)
-            full = gate_rows[b]
-            high = full.astype(bf16)
-            low = (full - high.astype(f32)).astype(bf16)
-            parts = [part[i : i + 16, :] for part in (high, low) for i in range(0, experts, 16)]
-            tail = jnp.concatenate(parts, axis=1)
-            grad_blocks[b, rows:, : tail.shape[1]] = tail
-            if tail.shape[1] < grad_blocks.shape[2]:
-                grad_blocks[b, rows:, tail.shape[1] :] = jnp.zeros_like(
-                    grad_blocks[b, rows:, tail.shape[1] :]
-                )
-            grad_copy(b).start()
-            mix_blocks[b] = dot_cols(marks[b], mix_slots[b]).astype(bf16)
-            mix_copy(b).start()
+            mix_slots[b, here, :] = mix[b * capacity : (b + 1) * capacity, :]
+            if e == 1:
+                mix_blocks[b] = dot_cols(marks[b], mix_slots[b]).astype(bf16)
+                mix_copy(b).start()
+        grad_active = dot_rows(grads[e], w_down[e])
+        grad_up = (grad_active * silu).astype(bf16)
+        slope = sigmoid * (1.0 + gate_pre * (1.0 - sigmoid))
+        grad_gate = (grad_active * up_pre * slope).astype(bf16)
+        width = grad_gate.shape[1]
+        slopes[e, :, :width] = grad_gate
+        slopes[e, :, width:] = grad_up
+        save(e, 3).start()
+        grad_x = (dot_rows(grad_gate, w_gate[e]) + dot_rows(grad_up, w_up[e])).astype(bf16)
         for b in range(SIDE):
-            grad_copy(b).wait()
-            mix_copy(b).wait()
-
-
-def expert_weights_kernel(*refs):
-    out = refs[-1]
-    groups = [refs[4 * i : 4 * i + 4] for i in range(SIDE)]
-    for name in range(2):
-        total = None
-        for rows_in, grads, active, slopes in groups:
-            term = dot_cols(rows_in[0], slopes[0]) if name == 0 else dot_cols(active[0], grads[0])
-            total = term if total is None else total + term
-        at = 0 if name == 0 else out.shape[1]
-        out[at : at + total.shape[0], :] = total.astype(bf16)
+            grad_slots[b, here, :] = grad_x[b * capacity : (b + 1) * capacity, :]
+    for b in range(SIDE):
+        there = slice(b * capacity, (b + 1) * capacity)
+        grad_blocks[b, :rows, :] = dot_cols(marks[b], grad_slots[b]).astype(bf16)
+        full = jnp.zeros((experts, rows), f32)
+        for e in range(2):
+            row = jnp.where(masks[e][b], products[e][there, :], 0.0)
+            full = jnp.where(expert == ids[e], jnp.sum(row, axis=0, keepdims=True), full)
+        high = full.astype(bf16)
+        low = (full - high.astype(f32)).astype(bf16)
+        parts = [part[i : i + 16, :] for part in (high, low) for i in range(0, experts, 16)]
+        tail = jnp.concatenate(parts, axis=1)
+        grad_blocks[b, rows:, : tail.shape[1]] = tail
+        if tail.shape[1] < grad_blocks.shape[2]:
+            rest = grad_blocks[b, rows:, tail.shape[1] :]
+            grad_blocks[b, rows:, tail.shape[1] :] = jnp.zeros_like(rest)
+        grad_copy(b).start()
+    for b in range(SIDE):
+        mix_copy(b).wait()
+        grad_copy(b).wait()
+    for e in range(2):
+        for n in range(4):
+            save(e, n).wait()
+
+
+def expert_weights_kernel(e, *refs):
+    sources, out = refs[: 4 * SIDE], refs[4 * SIDE]
+    *scratch, total, sems = refs[4 * SIDE + 1 :]
+
+    def load(i, n):
+        return pltpu.make_async_copy(sources[4 * i + n].at[e], scratch[n].at[i], sems.at[i, n])
+
+    for i in range(SIDE):
+        for n in range(4):
+            load(i, n).start()
+    depth = out.shape[1]
+    for i in range(SIDE):
+        for n in range(4):
+            load(i, n).wait()
+        rows_in, grads, active, slopes = (ref[i] for ref in scratch)
+        upper, lower = dot_cols(rows_in, slopes), dot_cols(active, grads)
+        if i:
+            upper, lower = total[:depth, :] + upper, total[depth:, :] + lower
+        if i < SIDE - 1:
+            total[:depth, :] = upper
+            total[depth:, :] = lower
+        else:
+            out[:depth, :] = upper.astype(bf16)
+            out[depth:, :] = lower.astype(bf16)
 
 
 def fold_kernel(own_lo, own_hi, before_lo, before_hi, after_lo, after_hi, *outs):
@@ -443,6 +458,13 @@
         part = slice(i % 2 * rows, (i % 2 + 1) * rows)
         refs = (own_lo, before_lo, after_lo) if i < 2 else (own_hi, before_hi, after_hi)
         out[...] = sum(ref[part, :].astype(f32) for ref in refs).astype(bf16)
+
+
+def fold_mix_kernel(own, before, after_, *outs):
+    rows = outs[0].shape[0]
+    for i, out in enumerate(outs):
+        part = slice(i * rows, (i + 1) * rows)
+        out[...] = sum(ref[part, :].astype(f32) for ref in (own, before, after_)).astype(bf16)
 
 
 def turn_kernel(
@@ -470,10 +492,14 @@
     out[:rows, :] = grad.astype(bf16)
 
 
-def finish_kernel(at, g_0, g_1, g_2, g_3, weights, tokens, gain, grad_hidden, out):
-    grad = dot_rows(g_0[...], weights[at[3]])
-    for d, part in ((1, g_1), (2, g_2), (3, g_3)):
-        grad = grad + dot_rows(part[...], weights[(at[3] + d) % SIDE])
+def finish_kernel(at, g_0, g_1, g_2, g_3, weights, sib_weights, tokens, gain, grad_hidden, out):
+    mine = other = None
+    for d, part in enumerate((g_0, g_1, g_2, g_3)):
+        owner = (at[3] + d) % SIDE
+        terms = dot_rows(part[...], weights[owner]), dot_rows(part[...], sib_weights[owner])
+        mine, other = terms if d == 0 else (mine + terms[0], other + terms[1])
+    first = at[2] == 0
+    grad = jnp.concatenate([jnp.where(first, mine, other), jnp.where(first, other, mine)], axis=1)
     grad = grad * gain[...]
     x = tokens[...].astype(f32)
     scale = lax.rsqrt(jnp.mean(x * x, axis=1, keepdims=True) + eps_norm)
@@ -564,15 +590,13 @@
     outs, total = refs[:-1], refs[-1]
     total[...] = (own[...].astype(f32) + sib[...].astype(f32)).astype(bf16)
     rows = outs[0].shape[0]
-    for i, out in enumerate(outs):
-        start = (at[3] + i // 2) % SIDE * (2 * rows) + i % 2 * rows
-        out[...] = total[pl.ds(pl.multiple_of(start, rows), rows), :]
-
-
-def owned_kernel(own_lo, own_hi, before_lo, before_hi, after_lo, after_hi, out):
-    rows = own_lo.shape[0]
-    out[:rows, :] = sum(ref[...].astype(f32) for ref in (own_lo, before_lo, after_lo)).astype(bf16)
-    out[rows:, :] = sum(ref[...].astype(f32) for ref in (own_hi, before_hi, after_hi)).astype(bf16)
+    for d, out in enumerate(outs):
+        out[...] = total[place(at, d, rows), :]
+
+
+def owned_kernel(own, from_before, from_after, out):
+    total = own[...].astype(f32) + from_before[...].astype(f32) + from_after[...].astype(f32)
+    out[...] = total.astype(bf16)
 
 
 def expert_unpack_kernel(at, own, from_after, far_lo, far_hi, from_before, gate_out, up_out, down_out, whole):
@@ -625,29 +649,28 @@
     ends = jnp.cumsum(lengths[0], dtype=jnp.int32)
     index = jnp.arange(length, dtype=jnp.int32)
     starts = jnp.max(jnp.where(index[:, None] >= ends[None, :], ends[None, :], 0), axis=1)
+    column_starts = starts[:, None]
     lane = jnp.arange(LANES)
     frequency = rope_base ** (-2.0 * (lane % (HEAD_DIM // 2)).astype(f32) / HEAD_DIM)
     angles = (index - starts).astype(f32)[:, None] * frequency[None, :]
     cosine = jnp.cos(angles)
     sine = jnp.sin(angles) * jnp.where(lane % HEAD_DIM < HEAD_DIM // 2, -1.0, 1.0)[None, :]
 
-    def doubled(columns):
-        heads = [columns[:, i : i + HEAD_DIM] for i in range(0, columns.shape[1], HEAD_DIM)]
-        return jnp.concatenate([head for one in heads for head in (one, one)], axis=1)
-
-    w_all = jnp.concatenate([w_query, doubled(w_key), doubled(w_value)], axis=1)
-    w_own = jnp.concatenate([w_query, w_key, w_value], axis=1)
-    router_rows = w_router.T.astype(bf16)
-    router_wide = jnp.pad(w_router, ((0, 0), (0, LANES - experts))).astype(bf16)
+    half = width // 2
+    mine = lax.dynamic_slice_in_dim(w_output, core * half, half, axis=0)
+    mine = jnp.broadcast_to(mine[None], (SIDE, half, depth))
+    token_parts = ring_gather(tokens, line_shift)
     own_weights = [gate_weight, up_weight, down_weight]
     sib_weights = [swap_core(a) for a in own_weights]
-    made = (w_all, cosine, sine, starts, w_own, router_rows, router_wide, *sib_weights)
-    token_parts = ring_gather(tokens, line_shift, *made)
     named = jnp.pad(routes.T.astype(bf16), ((0, 16 - picks), (0, depth - rows)))
-    grad_plane = lax.all_gather(
-        jnp.concatenate([cotangent, named], axis=0), CHIPS, axis=0, tiled=True
-    )
-    output_all = all_blocks(after(w_output, *token_parts[2:4]), "head")
+    marked = jnp.concatenate([cotangent, named], axis=0)
+    grads_u = [shift_u(marked, -1), shift_u(marked, 2), shift_u(marked, 1)]
+    grads_before, grads_after = shift_w(marked, 1), shift_w(marked, -1)
+    mine, *token_parts[2:4] = together(mine, *token_parts[2:4])
+    output_mine = swap_all(mine, "head")
+    grads_rest = jnp.concatenate(grads_u, axis=0)
+    token_parts[2], grads_rest = together(token_parts[2], grads_rest)
+    grads_before_rest, grads_after_rest = shift_w(grads_rest, 1), shift_w(grads_rest, -1)
 
     normed, query, key, value, mixed, log_total, *mixed_out = call(
         attend_kernel,
@@ -657,8 +680,8 @@
             array((length, LANES), f32),
             *[array((rows, width), bf16)] * SIDE,
         ],
-        [at, *token_parts, gain_1, w_all, cosine, sine, starts[:, None]],
-        specs=[smem] + [vmem] * 10,
+        [at, *token_parts, gain_1, w_query, w_key, w_value, cosine, sine, column_starts],
+        specs=[smem] + [vmem] * 12,
         out_specs=[hbm] * 6 + [vmem] * 4,
         scratch=[
             *[pltpu.VMEM((length, depth), bf16)] * 2,
@@ -669,63 +692,64 @@
         flops=12 * 10**9,
     )
     mixed_in = direct_swap(mixed_out, line_shift)
+    output_mine, mixed_in[0] = together(output_mine, mixed_in[0])
+    output_sib = swap_core(output_mine)
+    router_rows = w_router.T.astype(bf16)
+    router_wide = jnp.pad(w_router, ((0, 0), (0, LANES - experts))).astype(bf16)
+    at_join, grads_before_rest, grads_after_rest = together(
+        at, grads_before_rest, grads_after_rest
+    )
     hidden, inputs = call(
         join_kernel,
         [array((rows, depth), f32), array((rows, depth), bf16)],
-        [at, *mixed_in, output_all, tokens, gain_2],
-        specs=[smem] + [vmem] * 7,
+        [at_join, *mixed_in, output_mine, output_sib, tokens, gain_2],
+        specs=[smem] + [vmem] * 8,
         flops=3 * 10**9,
-    )
-
-    u_rest = [shift_u(inputs, -1), shift_u(inputs, 2), shift_u(inputs, 1)]
+        vmem=40,
+    )
+
+    u_parts = [shift_u(inputs, -1), shift_u(inputs, 2), shift_u(inputs, 1)]
     before_own, after_own = shift_w(inputs, 1), shift_w(inputs, -1)
-    u_rest = jnp.concatenate(u_rest, axis=0)
+    u_parts[0], grads_before, grads_after_rest, q_late, k_late, v_late = together(
+        u_parts[0], grads_before, grads_after_rest, w_query, w_key, w_value
+    )
+    grads_far_own = shift_w(grads_before, 1)
+    grads_far_rest = shift_w(grads_after_rest, -1)
+    w_own = jnp.concatenate([q_late, k_late, v_late], axis=1)
+    w_mine = lax.dynamic_slice_in_dim(w_own, core * (depth // 2), depth // 2, axis=0)
+    w_mine = all_blocks(w_mine, "head")
+    u_rest = jnp.concatenate(u_parts, axis=0)
     before_rest, after_rest = shift_w(u_rest, 1), shift_w(u_rest, -1)
     slots = SIDE * capacity
     half = array((length // 2 + 32, depth), bf16)
 
-    def experts_on(distance, x_parts, mix_in):
+    def experts_on(at, x_parts, g_parts):
         outs = [
             half,
             half,
             array((experts, rows), f32),
-            array((SIDE * length, depth), bf16),
+            array((length, depth), bf16),
             array((2, slots, depth), bf16),
             array((2, slots, depth), bf16),
             array((2, slots, hidden_units), bf16),
             array((2, slots, 2 * hidden_units), bf16),
         ]
-        args = [at, *x_parts, grad_plane, router_wide, *own_weights, *sib_weights]
-
-        def fixed(a):
-            return pl.BlockSpec(a.shape, lambda e: (0,) * len(a.shape))
-
-        def by_expert(a):
-            return pl.BlockSpec((1, *a.shape[1:]), lambda e: (e, 0, 0))
-
-        specs = [smem, *[anywhere] * 3, fixed(router_wide), *[anywhere] * 6]
-        aliases = {}
-        if mix_in is not None:
-            aliases = {len(args): 3}
-            args.append(mix_in)
-            specs.append(anywhere)
-        return call(
-            functools.partial(expert_kernel, capacity, distance),
+        args = [at, *x_parts, *g_parts, router_wide, *own_weights, *sib_weights]
+        return list(call(
+            functools.partial(expert_kernel, capacity),
             outs,
             args,
-            specs=specs,
-            grid=(2,),
-            out_specs=[hbm, hbm, fixed(outs[2]), hbm, *map(by_expert, outs[4:])],
+            specs=[smem, *[anywhere] * 4, vmem, *[anywhere] * 6],
+            out_specs=[hbm, hbm, vmem, *[hbm] * 5],
             scratch=[
                 pltpu.VMEM((SIDE, rows, depth), bf16),
                 pltpu.VMEM((SIDE, rows + 16, depth), bf16),
                 pltpu.VMEM((2, depth, hidden_units), bf16),
                 pltpu.VMEM((2, depth, hidden_units), bf16),
                 pltpu.VMEM((2, hidden_units, depth), bf16),
-                pltpu.VMEM((8, length), f32),
-                pltpu.VMEM((8, length), f32),
-                pltpu.VMEM((SIDE, experts, rows), f32),
-                pltpu.VMEM((slots, depth), bf16),
+                *[pltpu.VMEM((2, slots, depth), bf16)] * 3,
+                pltpu.VMEM((2, slots, hidden_units), bf16),
+                pltpu.VMEM((2, slots, 2 * hidden_units), bf16),
                 pltpu.VMEM((SIDE, 2 * capacity, rows), bf16),
                 pltpu.VMEM((SIDE, 2 * capacity, depth), bf16),
                 pltpu.VMEM((SIDE, 2 * capacity, depth), bf16),
@@ -736,58 +760,84 @@
                 pltpu.SemaphoreType.DMA((2, 3)),
                 pltpu.SemaphoreType.DMA((SIDE,)),
                 pltpu.SemaphoreType.DMA((SIDE,)),
+                pltpu.SemaphoreType.DMA((2, 4)),
             ],
-            flops=18 * 10**9,
-            aliases=aliases,
-        )
-
-    column = experts_on(0, [inputs, u_rest], None)
-    far_own = shift_w(after(before_own, column[2]), 1)
-    far_rest = shift_w(after(after_rest, column[2]), -1)
-    right = experts_on(1, [after_own, after_rest], column[3])
-    far = experts_on(2, [far_own, far_rest], right[3])
-    left = experts_on(3, [before_own, before_rest], far[3])
+            flops=14 * 10**9,
+        ))
+
+    column = experts_on(at, [inputs, u_rest], [marked, grads_rest])
+    before_own, after_rest, before_rest, column[0] = together(
+        before_own, after_rest, before_rest, column[0]
+    )
+    far_own, far_rest = shift_w(before_own, 1), shift_w(after_rest, -1)
+    at_next, column[0], grads_far_own, grads_far_rest = together(
+        at, column[0], grads_far_own, grads_far_rest
+    )
+    right = experts_on(at_next, [after_own, after_rest], [grads_after, grads_after_rest])
+    at_next, right[0], w_mine = together(at, right[0], w_mine)
+    w_sib = swap_core(w_mine)
+    far = experts_on(at_next, [far_own, far_rest], [grads_far_own, grads_far_rest])
+    at_next, far[0] = together(at, far[0])
+    left = experts_on(at_next, [before_own, before_rest], [grads_before, grads_before_rest])
     results = [column, right, far, left]
-    mix_all = left[3]
 
     weight_rows = depth + hidden_units
     flat = [a for r in results for a in r[4:]]
 
-    def expert_weights(e, earlier):
+    def expert_weights(e):
         return call(
-            expert_weights_kernel,
+            functools.partial(expert_weights_kernel, e),
             [array((weight_rows, depth), bf16)],
-            [after(flat[0], earlier), *flat[1:]],
-            specs=[pl.BlockSpec((1, *a.shape[1:]), lambda i: (e, 0, 0)) for a in flat],
-            grid=(1,),
-            out_specs=[pl.BlockSpec((weight_rows, depth), lambda i: (0, 0))],
+            flat,
+            specs=[anywhere] * len(flat),
+            scratch=[
+                *[pltpu.VMEM((SIDE, *a.shape[1:]), bf16) for a in flat[:4]],
+                pltpu.VMEM((weight_rows, depth), f32),
+                pltpu.SemaphoreType.DMA((SIDE, 4)),
+            ],
             flops=10 * 10**9,
         )[0]
 
-    sib_grads = expert_weights(1, mix_all)
-    own_grads = expert_weights(0, sib_grads)
-    from_before, from_after = ring_sum([(r[0], r[1]) for r in results], shift_w)
-    folded = call(
+    from_before, from_after, _ = ring_sum([(r[0], r[1]) for r in results], shift_w)
+    folded = list(call(
         fold_kernel,
         [array((rows + 16, depth), bf16)] * SIDE,
-        [after(column[0], own_grads), column[1], *from_before, *from_after],
+        [column[0], column[1], *from_before, *from_after],
         flops=2 * 10**9,
-    )
+    ))
+    flat[0], folded[0] = together(flat[0], folded[0])
+    own_grads = expert_weights(0)
     grad_terms = direct_swap(folded, shift_u)
+    grad_terms[0], own_grads = together(grad_terms[0], own_grads)
 
     grad_hidden, grad_low = call(
         turn_kernel,
         [array((rows, depth), f32), array((rows + experts + 16, depth), bf16)],
         [*grad_terms, column[2], router_rows, inputs, hidden, gain_2, cotangent],
         flops=4 * 10**9,
-    )
-    grad_parts = ring_gather(grad_low, line_shift)
+        vmem=40,
+    )
+    flat[0], grad_low = together(flat[0], grad_low)
+    sib_grads = expert_weights(1)
+    grad_parts, (sib_grads,) = ring_gather(grad_low, line_shift, sib_grads)
     sib_sums = swap_core(sib_grads)
+    quarters = list(call(
+        quarters_kernel,
+        [array((weight_rows // SIDE, depth), bf16)] * SIDE,
+        [at, own_grads, sib_sums],
+        specs=[smem] + [vmem] * 2,
+        scratch=[pltpu.VMEM((weight_rows, depth), bf16)],
+        flops=3 * 10**9,
+    ))
+    quarter_far, quarter_after = line_shift(quarters[2], 1), line_shift(quarters[3], -1)
+    at_back, quarters[0] = together(at, quarters[0])
+    *mixes, grad_hidden = together(*[r[3] for r in results], grad_hidden)
+    mix_far, mix_after = shift_w(mixes[2], 1), shift_w(mixes[3], -1)
     grads, *grads_out = call(
         attend_back_kernel,
         [array((length, 2 * width), bf16), *[array((rows, 2 * width), bf16)] * SIDE],
         [
-            after(at, sib_sums),
+            at_back,
             *grad_parts,
             w_output,
             query,
@@ -804,51 +854,63 @@
         flops=12 * 10**9,
     )
     grads_in = direct_swap(grads_out, line_shift)
-    w_parts = lax.all_gather(after(w_own, inputs), "head", axis=0)
-
     tall, short = depth // experts, width // experts
     size = tall + 2 * short + 16
+    quarter_up = (quarters[1].astype(f32) + quarter_far.astype(f32)).astype(bf16)
+    at_pack, quarter_up, quarter_after, mix_after = together(
+        at, quarter_up, quarter_after, mix_after
+    )
+    quarter_before = line_shift(quarter_up, 1)
+    mix_far, grads = together(mix_far, grads)
+    mix_up = (mixes[1].astype(f32) + mix_far.astype(f32)).astype(bf16)
+    at_pack, mix_up = together(at_pack, mix_up)
+    mix_before = shift_w(mix_up, 1)
     packed = call(
         pack_kernel,
         [array((experts, size, depth // 2), bf16)],
-        [at, normed, grads, mixed, *grad_parts, w_own, gain_1],
+        [at_pack, normed, grads, mixed, *grad_parts, w_own, gain_1],
         specs=[smem] + [vmem] * 10,
         scratch=[pltpu.VMEM((SIDE, experts + 16, depth), f32)],
-        flops=8 * 10**9,
+        flops=6 * 10**9,
     )[0]
-    packed = after(packed, *grads_in)
+    packed, *grads_in = together(packed, *grads_in)
+    arrived = swap_all(packed, PLANE)
+    at_finish, packed, mix_before = together(at, packed, mix_before)
     grad_tokens = call(
         finish_kernel,
         [array((rows, depth), f32)],
-        [after(at, packed), *grads_in, w_parts, tokens, gain_1, grad_hidden],
-        specs=[smem] + [vmem] * 8,
+        [at_finish, *grads_in, w_mine, w_sib, tokens, gain_1, grad_hidden],
+        specs=[smem] + [vmem] * 9,
         flops=4 * 10**9,
     )[0]
-    eighth = weight_rows // (2 * SIDE)
-    quarters = call(
-        quarters_kernel,
-        [array((eighth, depth), bf16)] * (2 * SIDE),
-        [after(at, grad_tokens), own_grads, sib_sums],
-        specs=[smem] + [vmem] * 2,
-        scratch=[pltpu.VMEM((weight_rows, depth), bf16)],
-        flops=3 * 10**9,
-    )
-    pairs = [(quarters[2 * d], quarters[2 * d + 1]) for d in range(SIDE)]
-    from_before, from_after = ring_sum(pairs, line_shift)
+    mixes[0], grad_tokens = together(mixes[0], grad_tokens)
+    mix_folded = list(call(
+        fold_mix_kernel,
+        [array((rows, depth), bf16)] * SIDE,
+        [mixes[0], mix_before, mix_after],
+        flops=2 * 10**9,
+    ))
+    mix_terms = direct_swap(mix_folded, shift_u)
+    arrived, mix_folded[0] = together(arrived, mix_folded[0])
     shared, last = call(
         share_kernel,
         [array(packed.shape, bf16), array((16, depth // 2), f32)],
-        [after(swap_all(packed, PLANE), *from_before, *from_after)],
+        [arrived],
         flops=2 * 10**9,
     )
-    lasts = [last, line_shift(last, -1), line_shift(last, 2), line_shift(last, 1)]
+    quarters[0], last = together(quarters[0], last)
     expert_owned = call(
         owned_kernel,
-        [array((2 * eighth, depth), bf16)],
-        [*pairs[0], *from_before, *from_after],
+        [array((weight_rows // SIDE, depth), bf16)],
+        [quarters[0], quarter_before, quarter_after],
         flops=10**9,
     )[0]
     expert_parts = ring_gather(expert_owned, line_shift)
+    lasts = [last, line_shift(last, -1), line_shift(last, 2), line_shift(last, 1)]
+    output = (hidden + sum(term.astype(f32) for term in mix_terms)).astype(bf16)
+    mix_terms[1], mix_terms[2], mix_terms[3], expert_parts[2] = together(
+        mix_terms[1], mix_terms[2], mix_terms[3], expert_parts[2]
+    )
     expert_totals = call(
         expert_unpack_kernel,
         [
@@ -861,7 +923,7 @@
         scratch=[pltpu.VMEM((weight_rows, depth), bf16)],
         flops=4 * 10**9,
     )
-    gathered = after(swap_all(shared, PLANE), *lasts, *expert_totals)
+    gathered, output, *expert_totals = together(swap_all(shared, PLANE), output, *expert_totals)
     grad_query, grad_key, grad_value, grad_output, grad_router, grad_gain_1, grad_gain_2 = call(
         unpack_kernel,
         [
@@ -878,9 +940,6 @@
         scratch=[pltpu.VMEM((SIDE, 16, depth // 2), f32)],
         flops=4 * 10**9,
     )
-
-    mixture = lax.psum_scatter(after(mix_all, *folded), CHIPS, scatter_dimension=0, tiled=True)
-    output = (hidden + mixture.astype(f32)).astype(bf16)
 
     return (
         output,

time: 432 us -> 413 us (0.956)
  starting transfers between devices: 86.6 us -> 106 us
  waiting for transfers between devices: 125 us -> 108 us
  Pallas kernels: 166 us -> 151 us
  between operations: 14.6 us -> 1.8 us
  other arithmetic: 13.6 us -> 18.3 us
    ppermute x27 -> x24, waiting for transfers between devices: 84.2 us -> 27.9 us  [line_shift(): return lax.ppermute(values, 'head', pairs)]
    ppermute x18 -> x33, starting transfers between devices: 24 us -> 53.3 us  [plane_shift(): return lax.ppermute(values, PLANE, pairs)]
    ppermute x18 -> x33, waiting for transfers between devices: 40.3 us -> 62 us  [plane_shift(): return lax.ppermute(values, PLANE, pairs)]
    all_to_all x3 -> x4, waiting for transfers between devices: 0.01 us -> 17.6 us  [swap_all(): return lax.all_to_all(values, axes, 0, 0, tiled=True)]
    pallas_call x18 -> x19, Pallas kernels: 166 us -> 151 us  [call(): pl.pallas_call(kernel, out_shape=out_shapes, in_specs=specs or [whole] *...]
    ppermute x27 -> x24, starting transfers between devices: 39.1 us -> 29.1 us  [line_shift(): return lax.ppermute(values, 'head', pairs)]
    convert_element_type x1 -> x3, other arithmetic: 1.98 us -> 7.6 us  [the longest x1 3.94 us: body(): mix_up = (mixes[1].astype(f32) + mix_far.astype(f32)).astype(bf16)]
    unnamed x98 -> x97, local copies, waits for them, and re-layouts: 13.3 us -> 15 us
  transfers between devices with their start and end apart: 55 -> 67, of which waited for: 21 -> 23; matrix products, arithmetic and copies ran while one was open for 5% -> 7% of each run, Pallas kernels for 39% -> 35%
where the time goes in v3:
time: 413 us; the launch traced here: 406 us
  Pallas kernels  151 us (37%)
  waiting for transfers between devices  108 us (26%)
  starting transfers between devices  106 us (26%)
  local copies, waits for them, and re-layouts  21.4 us (5%)
  other arithmetic  18.3 us (4%)
    pallas_call x19, Pallas kernels, call(): pl.pallas_call(kernel, out_shape=out_shapes, in_specs=specs or [whole] *...  151 us
    ppermute x33, waiting for transfers between devices, plane_shift(): return lax.ppermute(values, PLANE, pairs)  62 us
    ppermute x33, starting transfers between devices, plane_shift(): return lax.ppermute(values, PLANE, pairs)  53.3 us
    ppermute x24, starting transfers between devices, line_shift(): return lax.ppermute(values, 'head', pairs)  29.1 us
    ppermute x24, waiting for transfers between devices, line_shift(): return lax.ppermute(values, 'head', pairs)  27.9 us
    all_to_all x4, starting transfers between devices, swap_all(): return lax.all_to_all(values, axes, 0, 0, tiled=True)  23.2 us
    all_to_all x4, waiting for transfers between devices, swap_all(): return lax.all_to_all(values, axes, 0, 0, tiled=True)  17.6 us
    unnamed x97, local copies, waits for them, and re-layouts  15 us
  transfers between devices with their start and end apart: 67, of which 23 were waited for; matrix products, arithmetic and copies ran while one was open for 7% of the time, Pallas kernels for 35%

profile of v3, /device:TPU:4, one launch (start us, length us, event | category | flops | bytes accessed | tf_op | source)
XLA Modules:
  0.0 406.3 jit_solution(11055657326571442597)
XLA Ops:
  30.3 4.4 %all-to-all-start = ((bf16[4,128,1024]{2,1,0:T(8,128)(2,1)}), bf16[4,128,1024]{2,1,0:T(8,128)(2,1)S(1)}, u32[]{:S(2)}, u32[]{:S(2)}) async-start(bf16[4,128,1024]{2,1,0:T(8,128)(2,1)} %broadcast_in_dim.28), calls=%async_computation | async-start | bytes 2097152 | tf_op jit(solution)/shard_map/all_to_all | solution.py:110
  34.7 12.3 %shard_map.229 = (bf16[1024,1024]{1,0:T(8,128)(2,1)}, bf16[1024,256]{1,0:T(8,128)(2,1)}, bf16[1024,256]{1,0:T(8,128)(2,1)}, bf16[1024,256]{1,0:T(8,128)(2,1)}, b...) custom-call(s32[4]{0:T(128)} %pad_add_fusion.at, ...), custom_call_target="tpu_custom_call" | custom-call | flops 12000000000 | bytes 9445392 | tf_op jit(solution)/shard_map/pallas_call | solution.py:39
  66.9 5.7 %collective-permute-done.13 = bf16[256,1024]{1,0:T(8,128)(2,1)S(1)} collective-permute-done((bf16[256,1024]{1,0:T(8,128)(2,1)S(1)}, bf16[256,1024]{1,0:T(8,128)(2,1)S(1)}, u32[]{:S(2)}, u32[]{:S(2)}) %collective-permute-start.13) | collective-permute-done | bytes 524320 | tf_op jit(solution)/shard_map/ppermute | solution.py:72
  76.5 4.7 %collective-permute-done.16 = bf16[256,1024]{1,0:T(8,128)(2,1)S(1)} collective-permute-done((bf16[256,1024]{1,0:T(8,128)(2,1)S(1)}, bf16[256,1024]{1,0:T(8,128)(2,1)S(1)}, u32[]{:S(2)}, u32[]{:S(2)}) %collective-permute-start.16) | collective-permute-done | bytes 524320 | tf_op jit(solution)/shard_map/ppermute | solution.py:72
  92.3 4.4 %all-to-all-start.1 = ((bf16[4,512,512]{2,1,0:T(8,128)(2,1)}), bf16[4,512,512]{2,1,0:T(8,128)(2,1)}, u32[]{:S(2)}, u32[]{:S(2)}) async-start(bf16[4,512,512]{2,1,0:T(8,128)(2,1)} %broadcast_in_dim.52), calls=%async_computation.1 | async-start | bytes 4194304 | tf_op jit(solution)/shard_map/all_to_all | solution.py:110
  105.5 14.4 %shard_map.231 = (bf16[544,1024]{1,0:T(8,128)(2,1)}, bf16[544,1024]{1,0:T(8,128)(2,1)}, f32[32,256]{1,0:T(8,128)}, bf16[1024,1024]{1,0:T(8,128)(2,1)}, bf16[2,38...) custom-call(s32[4]{0:T(128)} %pad_add_fusion.at, ...), custom_call_target="tpu_custom_call" | custom-call | flops 14000000000 | bytes 20742160 | tf_op jit(solution)/shard_map/pallas_call | solution.py:39
  122.5 4.2 %collective-permute-done.26.g_a = bf16[272,1024]{1,0:T(8,128)(2,1)} collective-permute-done((bf16[272,1024]{1,0:T(8,128)(2,1)}, bf16[272,1024]{1,0:T(8,128)(2,1)}, u32[]{:S(2)}, u32[]{:S(2)}) %collective-permute-start.26) | collective-permute-done | bytes 557088 | tf_op jit(solution)/shard_map/ppermute | solution.py:72
  126.7 5.6 %collective-permute-done.25.x_a = bf16[256,1024]{1,0:T(8,128)(2,1)} collective-permute-done((bf16[256,1024]{1,0:T(8,128)(2,1)S(1)}, bf16[256,1024]{1,0:T(8,128)(2,1)}, u32[]{:S(2)}, u32[]{:S(2)}) %collective-permute-start.25) | collective-permute-done | bytes 524320 | tf_op jit(solution)/shard_map/ppermute | solution.py:72
  132.3 14.4 %shard_map.232 = (bf16[544,1024]{1,0:T(8,128)(2,1)}, bf16[544,1024]{1,0:T(8,128)(2,1)}, f32[32,256]{1,0:T(8,128)}, bf16[1024,1024]{1,0:T(8,128)(2,1)}, bf16[2,38...) custom-call(s32[4]{0:T(128)} %pad_add_fusion.at, ...), custom_call_target="tpu_custom_call" | custom-call | flops 14000000000 | bytes 20742160 | tf_op jit(solution)/shard_map/pallas_call | solution.py:39
  150.8 14.3 %shard_map.233 = (bf16[544,1024]{1,0:T(8,128)(2,1)}, bf16[544,1024]{1,0:T(8,128)(2,1)}, f32[32,256]{1,0:T(8,128)}, bf16[1024,1024]{1,0:T(8,128)(2,1)}, bf16[2,38...) custom-call(s32[4]{0:T(128)} %pad_add_fusion.at, ...), custom_call_target="tpu_custom_call" | custom-call | flops 14000000000 | bytes 20742160 | tf_op jit(solution)/shard_map/pallas_call | solution.py:39
  167.5 14.5 %shard_map.234 = (bf16[544,1024]{1,0:T(8,128)(2,1)}, bf16[544,1024]{1,0:T(8,128)(2,1)}, f32[32,256]{1,0:T(8,128)}, bf16[1024,1024]{1,0:T(8,128)(2,1)}, bf16[2,38...) custom-call(s32[4]{0:T(128)} %pad_add_fusion.at, ...), custom_call_target="tpu_custom_call" | custom-call | flops 14000000000 | bytes 20742160 | tf_op jit(solution)/shard_map/pallas_call | solution.py:39
  188.8 9.0 %collective-permute-done.32.after_lo = bf16[544,1024]{1,0:T(8,128)(2,1)S(1)} collective-permute-done((bf16[544,1024]{1,0:T(8,128)(2,1)}, bf16[544,1024]{1,0:T(8,128)(2,1)S(1)}, u32[]{:S(2)}, u32[]{:S(2)}) %collective-permute-start.32) | collective-permute-done | bytes 1114144 | tf_op jit(solution)/shard_map/ppermute | solution.py:72
  197.8 3.9 collective-permute-done.30.before_lo
  201.8 8.0 %collective-permute-done.34.after_hi = bf16[544,1024]{1,0:T(8,128)(2,1)S(1)} collective-permute-done((bf16[544,1024]{1,0:T(8,128)(2,1)S(1)}, bf16[544,1024]{1,0:T(8,128)(2,1)S(1)}, u32[]{:S(2)}, u32[]{:S(2)}) %collective-permute-start.34) | collective-permute-done | bytes 1114144 | tf_op jit(solution)/shard_map/ppermute | solution.py:72
  210.8 4.5 %shard_map.235 = (bf16[272,1024]{1,0:T(8,128)(2,1)}, bf16[272,1024]{1,0:T(8,128)(2,1)}, bf16[272,1024]{1,0:T(8,128)(2,1)}, bf16[272,1024]{1,0:T(8,128)(2,1)}) custom-call(bf16[544,1024]{1,0:T(8,128)(2,1)} %get-tuple-element.181.own_lo, bf16[544,1024]{1,0:T(8,128)(2,1)} %get-tuple-element.182.own_hi, bf16[544,1024]{1,0:T(8,128)(2,1)} %copy-done.30, ...), custom_call_target="tpu_custom_call" | custom-call | flops 2000000000 | bytes 8912896 | tf_op jit(solution)/shard_map/pallas_call | solution.py:39
  218.4 11.0 %shard_map.236.own = bf16[1536,1024]{1,0:T(8,128)(2,1)} custom-call(bf16[2,384,1024]{2,1,0:T(8,128)(2,1)} %get-tuple-element.230.refs_0_, bf16[2,384,1024]{2,1,0:T(8,128)(2,1)} %get-tuple-element.206.refs_1_, bf16[2,384,512]{2,1,0:T(8,128)(2,1)} %get-tuple-element.207.refs_2_, bf16[2,384,1024]{2,1,0:T(8,128)(2,1)} %get-tuple-element.208.refs_3_, ...), custom_call_target="tpu_custom_call" | custom-call | flops 10000000000 | bytes 25165824 | tf_op jit(solution)/shard_map/pallas_call | solution.py:39
  229.3 4.6 %collective-permute-done.37.term_3 = bf16[272,1024]{1,0:T(8,128)(2,1)S(1)} collective-permute-done((bf16[272,1024]{1,0:T(8,128)(2,1)}, bf16[272,1024]{1,0:T(8,128)(2,1)S(1)}, u32[]{:S(2)}, u32[]{:S(2)}) %collective-permute-start.37) | collective-permute-done | bytes 557088 | tf_op jit(solution)/shard_map/ppermute | solution.py:72
  241.3 10.9 %shard_map.238 = bf16[1536,1024]{1,0:T(8,128)(2,1)} custom-call(bf16[2,384,1024]{2,1,0:T(8,128)(2,1)} %get-tuple-element.230.refs_0_, bf16[2,384,1024]{2,1,0:T(8,128)(2,1)} %get-tuple-element.206.refs_1_, bf16[2,384,512]{2,1,0:T(8,128)(2,1)} %get-tuple-element.207.refs_2_, bf16[2,384,1024]{2,1,0:T(8,128)(2,1)} %get-tuple-element.208.refs_3_, ...), custom_call_target="tpu_custom_call" | custom-call | flops 10000000000 | bytes 25165824 | tf_op jit(solution)/shard_map/pallas_call | solution.py:39
  258.4 6.3 %shard_map.239 = (bf16[384,1024]{1,0:T(8,128)(2,1)}, bf16[384,1024]{1,0:T(8,128)(2,1)}, bf16[384,1024]{1,0:T(8,128)(2,1)}, bf16[384,1024]{1,0:T(8,128)(2,1)}) custom-call(s32[4]{0:T(128)} %pad_add_fusion.at, bf16[1536,1024]{1,0:T(8,128)(2,1)} %shard_map.236.own, bf16[1536,1024]{1,0:T(8,128)(2,1)} %collective-permute-done.40.sib), custom_call_target="tpu_custom_call" | custom-call | flops 3000000000 | bytes 9437200 | tf_op jit(solution)/shard_map/pallas_call | solution.py:39
  268.9 13.9 %shard_map.240 = (bf16[1024,512]{1,0:T(8,128)(2,1)}, bf16[256,512]{1,0:T(8,128)(2,1)}, bf16[256,512]{1,0:T(8,128)(2,1)}, bf16[256,512]{1,0:T(8,128)(2,1)}, bf16[256,512]{1,0:T(8,128)(2,1)}) custom-call(s32[4]{0:T(128)} %pad_add_fusion.at, bf16[304,1024]{1,0:T(8,128)(2,1)} %copy-done.2, bf16[304,1024]{1,0:T(8,128)(2,1)} %copy-done.23, ...), custom_call_target="tpu_custom_call" | custom-call | flops 12000000000 | bytes 8785936 | tf_op jit(solution)/shard_map/pallas_call | solution.py:39
  282.8 3.9 add_convert_fusion
  294.8 7.0 %shard_map.241 = bf16[32,64,512]{2,1,0:T(8,128)(2,1)} custom-call(s32[4]{0:T(128)} %pad_add_fusion.at, bf16[1024,1024]{1,0:T(8,128)(2,1)} %get-tuple-element.256.normed, bf16[1024,512]{1,0:T(8,128)(2,1)} %get-tuple-element.257.grads, bf16[1024,256]{1,0:T(8,128)(2,1)} %get-tuple-element.251.mixed, bf16[304,1024]{1,0:T(8,128)(2,1)} %copy-done.2, ...), custom_call_target="tpu_custom_call" | custom-call | flops 6000000000 | bytes 9310224 | tf_op jit(solution)/shard_map/pallas_call | solution.py:39
  303.4 5.2 %collective-permute-done.49.g_3 = bf16[256,512]{1,0:T(8,128)(2,1)S(1)} collective-permute-done((bf16[256,512]{1,0:T(8,128)(2,1)S(1)}, bf16[256,512]{1,0:T(8,128)(2,1)S(1)}, u32[]{:S(2)}, u32[]{:S(2)}) %collective-permute-start.49) | collective-permute-done | bytes 262176 | tf_op jit(solution)/shard_map/ppermute | solution.py:60
  309.3 7.0 %all-to-all-start.2 = ((bf16[32,64,512]{2,1,0:T(8,128)(2,1)}), bf16[32,64,512]{2,1,0:T(8,128)(2,1)S(1)}, u32[]{:S(2)}, u32[]{:S(2)}) async-start(bf16[32,64,512]{2,1,0:T(8,128)(2,1)} %shard_map.241), calls=%async_computation.2 | async-start | bytes 4194304 | tf_op jit(solution)/shard_map/all_to_all | solution.py:110
  316.4 5.5 %shard_map.242 = f32[256,1024]{1,0:T(8,128)} custom-call(s32[4]{0:T(128)} %pad_add_fusion.at, bf16[256,512]{1,0:T(8,128)(2,1)} %get-tuple-element.266.g_0, bf16[256,512]{1,0:T(8,128)(2,1)} %copy-done.43, bf16[256,512]{1,0:T(8,128)(2,1)} %copy-done.44, bf16[256,512]{1,0:T(8,128)(2,1)} %copy-done.45, bf16[4,512,512]{2,1,0:T(8,128)(2,1)} %all-to-all-done.1.weights, ...), custom_call_target="tpu_custom_call" | custom-call | flops 4000000000 | bytes 7868432 | tf_op jit(solution)/shard_map/pallas_call | solution.py:39
  322.0 4.4 %shard_map.243 = (bf16[256,1024]{1,0:T(8,128)(2,1)}, bf16[256,1024]{1,0:T(8,128)(2,1)}, bf16[256,1024]{1,0:T(8,128)(2,1)}, bf16[256,1024]{1,0:T(8,128)(2,1)}) custom-call(bf16[1024,1024]{1,0:T(8,128)(2,1)} %get-tuple-element.272.own, bf16[1024,1024]{1,0:T(8,128)(2,1)} %collective-permute-done.50.before, bf16[1024,1024]{1,0:T(8,128)(2,1)} %collective-permute-done.43.after_), custom_call_target="tpu_custom_call" | custom-call | flops 2000000000 | bytes 8388608 | tf_op jit(solution)/shard_map/pallas_call | solution.py:39
  326.4 16.5 %all-to-all-done.2.parts = bf16[32,64,512]{2,1,0:T(8,128)(2,1)S(1)} async-done(((bf16[32,64,512]{2,1,0:T(8,128)(2,1)}), bf16[32,64,512]{2,1,0:T(8,128)(2,1)S(1)}, u32[]{:S(2)}, u32[]{:S(2)}) %all-to-all-start.2) | async-done | bytes 2097184 | tf_op jit(solution)/shard_map/all_to_all | solution.py:110
  347.5 7.4 %all-to-all-start.3 = ((bf16[32,64,512]{2,1,0:T(8,128)(2,1)}), bf16[32,64,512]{2,1,0:T(8,128)(2,1)S(1)}, u32[]{:S(2)}, u32[]{:S(2)}) async-start(bf16[32,64,512]{2,1,0:T(8,128)(2,1)} %get-tuple-element.277), calls=%async_computation.3 | async-start | bytes 4194304 | tf_op jit(solution)/shard_map/all_to_all | solution.py:110
  366.7 12.1 %collective-permute-done.56.from_before = bf16[384,1024]{1,0:T(8,128)(2,1)S(1)} collective-permute-done((bf16[384,1024]{1,0:T(8,128)(2,1)}, bf16[384,1024]{1,0:T(8,128)(2,1)S(1)}, u32[]{:S(2)}, u32[]{:S(2)}) %collective-permute-start.56) | collective-permute-done | bytes 786464 | tf_op jit(solution)/shard_map/ppermute | solution.py:60
  382.2 4.7 %collective-permute-done.54 = bf16[256,1024]{1,0:T(8,128)(2,1)S(1)} collective-permute-done((bf16[256,1024]{1,0:T(8,128)(2,1)}, bf16[256,1024]{1,0:T(8,128)(2,1)S(1)}, u32[]{:S(2)}, u32[]{:S(2)}) %collective-permute-start.54) | collective-permute-done | bytes 524320 | tf_op jit(solution)/shard_map/ppermute | solution.py:72
  387.5 5.2 %collective-permute-done.53 = bf16[256,1024]{1,0:T(8,128)(2,1)S(1)} collective-permute-done((bf16[256,1024]{1,0:T(8,128)(2,1)}, bf16[256,1024]{1,0:T(8,128)(2,1)S(1)}, u32[]{:S(2)}, u32[]{:S(2)}) %collective-permute-start.53) | collective-permute-done | bytes 524320 | tf_op jit(solution)/shard_map/ppermute | solution.py:72
  396.3 4.9 %shard_map.246 = (f32[1,1024,512]{2,1,0:T(8,128)}, f32[1,1024,512]{2,1,0:T(8,128)}, f32[1,512,1024]{2,1,0:T(8,128)}) custom-call(s32[4]{0:T(128)} %pad_add_fusion.at, bf16[384,1024]{1,0:T(8,128)(2,1)} %shard_map.245.own, bf16[384,1024]{1,0:T(8,128)(2,1)} %copy-done.22, bf16[192,1024]{1,0:T(8,128)(2,1)} %copy-done.35, ...), custom_call_target="tpu_custom_call" | custom-call | flops 4000000000 | bytes 9437200 | tf_op jit(solution)/shard_map/pallas_call | solution.py:39
  (248 shorter events, 149.7 us)
Async XLA Ops:
  0.6 18.4 %collective-permute-start = (bf16[256,1024]{1,0:T(8,128)(2,1)}, bf16[256,1024]{1,0:T(8,128)(2,1)S(1)}, u32[]{:S(2)}, u32[]{:S(2)}) collective-permute-start(bf16[256,1024]{1,0:T(8,128)(2,1)} %tokens.3), channel_id=1, source_target_pairs={{0,1},{1,2},{2,3},{3,0},{4,5},{5,6},{6,7},{7,4},{8,9},{9,10},{10,1... | collective-permute-start | bytes 1572872 | tf_op jit(solution)/shard_map/ppermute | solution.py:60
  8.5 17.3 %collective-permute-start.5 = (bf16[272,1024]{1,0:T(8,128)(2,1)}, bf16[272,1024]{1,0:T(8,128)(2,1)S(1)}, u32[]{:S(2)}, u32[]{:S(2)}) collective-permute-start(bf16[272,1024]{1,0:T(8,128)(2,1)} %fusion.1.g_a), channel_id=1, source_target_pairs={{0,64},{4,20},{8,72},{12,28},{16,80},{20,4},{24,88},{28,12},{32,96... | collective-permute-start | bytes 1671176 | tf_op jit(solution)/shard_map/ppermute | solution.py:72
  28.3 23.0 %collective-permute-start.7 = (bf16[816,1024]{1,0:T(8,128)(2,1)}, bf16[816,1024]{1,0:T(8,128)(2,1)}, u32[]{:S(2)}, u32[]{:S(2)}) collective-permute-start(bf16[816,1024]{1,0:T(8,128)(2,1)} %pad_maximum_fusion.g_b), channel_id=1, source_target_pairs={{0,8},{4,36},{8,16},{12,44},{16,24},{20,52},{24,0},{28,60},{32,40}... | collective-permute-start | bytes 5013512 | tf_op jit(solution)/shard_map/ppermute | solution.py:72
  29.5 22.7 %collective-permute-start.8 = (bf16[816,1024]{1,0:T(8,128)(2,1)}, bf16[816,1024]{1,0:T(8,128)(2,1)}, u32[]{:S(2)}, u32[]{:S(2)}) collective-permute-start(bf16[816,1024]{1,0:T(8,128)(2,1)} %pad_maximum_fusion.g_b), channel_id=1, source_target_pairs={{0,24},{4,100},{8,0},{12,108},{16,8},{20,116},{24,16},{28,124},{32... | collective-permute-start | bytes 5013512 | tf_op jit(solution)/shard_map/ppermute | solution.py:72
  30.3 17.8 %all-to-all-start = ((bf16[4,128,1024]{2,1,0:T(8,128)(2,1)}), bf16[4,128,1024]{2,1,0:T(8,128)(2,1)S(1)}, u32[]{:S(2)}, u32[]{:S(2)}) async-start(bf16[4,128,1024]{2,1,0:T(8,128)(2,1)} %broadcast_in_dim.28), calls=%async_computation | async-start | bytes 2097152 | tf_op jit(solution)/shard_map/all_to_all | solution.py:110
  82.1 20.7 %collective-permute-start.21 = (bf16[768,1024]{1,0:T(8,128)(2,1)}, bf16[768,1024]{1,0:T(8,128)(2,1)}, u32[]{:S(2)}, u32[]{:S(2)}) collective-permute-start(bf16[768,1024]{1,0:T(8,128)(2,1)} %constant_dynamic-update-slice_fusion.x_b), channel_id=1, source_target_pairs={{0,24},{4,100},{8,0},{12,108},{16,8},{20,116},{24,16},{28,124},{32... | collective-permute-start | bytes 4718600 | tf_op jit(solution)/shard_map/ppermute | solution.py:72
  86.8 33.2 %collective-permute-start.22 = (bf16[768,1024]{1,0:T(8,128)(2,1)}, bf16[768,1024]{1,0:T(8,128)(2,1)}, u32[]{:S(2)}, u32[]{:S(2)}) collective-permute-start(bf16[768,1024]{1,0:T(8,128)(2,1)} %constant_dynamic-update-slice_fusion.x_b), channel_id=1, source_target_pairs={{0,8},{4,36},{8,16},{12,44},{16,24},{20,52},{24,0},{28,60},{32,40}... | collective-permute-start | bytes 4718600 | tf_op jit(solution)/shard_map/ppermute | solution.py:72
  90.7 31.8 %collective-permute-start.24 = (bf16[816,1024]{1,0:T(8,128)(2,1)}, bf16[816,1024]{1,0:T(8,128)(2,1)}, u32[]{:S(2)}, u32[]{:S(2)}) collective-permute-start(bf16[816,1024]{1,0:T(8,128)(2,1)} %collective-permute-done.8.g_b), channel_id=1, source_target_pairs={{0,24},{4,100},{8,0},{12,108},{16,8},{20,116},{24,16},{28,124},{32... | collective-permute-start | bytes 5013512 | tf_op jit(solution)/shard_map/ppermute | solution.py:72
  92.3 54.4 %all-to-all-start.1 = ((bf16[4,512,512]{2,1,0:T(8,128)(2,1)}), bf16[4,512,512]{2,1,0:T(8,128)(2,1)}, u32[]{:S(2)}, u32[]{:S(2)}) async-start(bf16[4,512,512]{2,1,0:T(8,128)(2,1)} %broadcast_in_dim.52), calls=%async_computation.1 | async-start | bytes 4194304 | tf_op jit(solution)/shard_map/all_to_all | solution.py:110
  96.8 29.9 %collective-permute-start.26 = (bf16[272,1024]{1,0:T(8,128)(2,1)}, bf16[272,1024]{1,0:T(8,128)(2,1)}, u32[]{:S(2)}, u32[]{:S(2)}) collective-permute-start(bf16[272,1024]{1,0:T(8,128)(2,1)} %fusion.1.g_a), channel_id=1, source_target_pairs={{0,24},{4,100},{8,0},{12,108},{16,8},{20,116},{24,16},{28,124},{32... | collective-permute-start | bytes 1671176 | tf_op jit(solution)/shard_map/ppermute | solution.py:72
  98.4 33.9 %collective-permute-start.25 = (bf16[256,1024]{1,0:T(8,128)(2,1)S(1)}, bf16[256,1024]{1,0:T(8,128)(2,1)}, u32[]{:S(2)}, u32[]{:S(2)}) collective-permute-start(bf16[256,1024]{1,0:T(8,128)(2,1)S(1)} %get-tuple-element.173.x_a.inputs), channel_id=1, source_target_pairs={{0,24},{4,100},{8,0},{12,108},{16,8},{20,116},{24,16},{28,124},{32... | collective-permute-start | bytes 1572872 | tf_op jit(solution)/shard_map/ppermute | solution.py:72
  102.8 17.2 %collective-permute-start.23 = (bf16[272,1024]{1,0:T(8,128)(2,1)}, bf16[272,1024]{1,0:T(8,128)(2,1)S(1)}, u32[]{:S(2)}, u32[]{:S(2)}) collective-permute-start(bf16[272,1024]{1,0:T(8,128)(2,1)} %copy-done.32), channel_id=1, source_target_pairs={{0,8},{4,36},{8,16},{12,44},{16,24},{20,52},{24,0},{28,60},{32,40}... | collective-permute-start | bytes 1671176 | tf_op jit(solution)/shard_map/ppermute | solution.py:72
  119.9 29.7 %collective-permute-start.28 = (bf16[768,1024]{1,0:T(8,128)(2,1)}, bf16[768,1024]{1,0:T(8,128)(2,1)S(1)}, u32[]{:S(2)}, u32[]{:S(2)}) collective-permute-start(bf16[768,1024]{1,0:T(8,128)(2,1)} %collective-permute-done.21.x_b), channel_id=1, source_target_pairs={{0,24},{4,100},{8,0},{12,108},{16,8},{20,116},{24,16},{28,124},{32... | collective-permute-start | bytes 4718600 | tf_op jit(solution)/shard_map/ppermute | solution.py:72
  120.0 29.6 %collective-permute-start.27 = (bf16[256,1024]{1,0:T(8,128)(2,1)}, bf16[256,1024]{1,0:T(8,128)(2,1)}, u32[]{:S(2)}, u32[]{:S(2)}) collective-permute-start(bf16[256,1024]{1,0:T(8,128)(2,1)} %collective-permute-done.20.x_a), channel_id=1, source_target_pairs={{0,8},{4,36},{8,16},{12,44},{16,24},{20,52},{24,0},{28,60},{32,40}... | collective-permute-start | bytes 1572872 | tf_op jit(solution)/shard_map/ppermute | solution.py:72
  146.7 42.2 %collective-permute-start.31 = (bf16[544,1024]{1,0:T(8,128)(2,1)}, bf16[544,1024]{1,0:T(8,128)(2,1)}, u32[]{:S(2)}, u32[]{:S(2)}) collective-permute-start(bf16[544,1024]{1,0:T(8,128)(2,1)} %get-tuple-element.196), channel_id=1, source_target_pairs={{0,8},{4,36},{8,16},{12,44},{16,24},{20,52},{24,0},{28,60},{32,40}... | collective-permute-start | bytes 3342344 | tf_op jit(solution)/shard_map/ppermute | solution.py:72
  165.2 18.2 %collective-permute-start.29 = (bf16[544,1024]{1,0:T(8,128)(2,1)}, bf16[544,1024]{1,0:T(8,128)(2,1)}, u32[]{:S(2)}, u32[]{:S(2)}) collective-permute-start(bf16[544,1024]{1,0:T(8,128)(2,1)} %get-tuple-element.195), channel_id=1, source_target_pairs={{0,8},{4,36},{8,16},{12,44},{16,24},{20,52},{24,0},{28,60},{32,40}... | collective-permute-start | bytes 3342344 | tf_op jit(solution)/shard_map/ppermute | solution.py:72
  167.3 18.6 %collective-permute-start.33 = (bf16[544,1024]{1,0:T(8,128)(2,1)}, bf16[544,1024]{1,0:T(8,128)(2,1)S(1)}, u32[]{:S(2)}, u32[]{:S(2)}) collective-permute-start(bf16[544,1024]{1,0:T(8,128)(2,1)} %get-tuple-element.202), channel_id=1, source_target_pairs={{0,24},{4,100},{8,0},{12,108},{16,8},{20,116},{24,16},{28,124},{32... | collective-permute-start | bytes 3342344 | tf_op jit(solution)/shard_map/ppermute | solution.py:72
  186.4 23.3 %collective-permute-start.34 = (bf16[544,1024]{1,0:T(8,128)(2,1)S(1)}, bf16[544,1024]{1,0:T(8,128)(2,1)S(1)}, u32[]{:S(2)}, u32[]{:S(2)}) collective-permute-start(bf16[544,1024]{1,0:T(8,128)(2,1)S(1)} %add_convert_fusion.1), channel_id=1, source_target_pairs={{0,24},{4,100},{8,0},{12,108},{16,8},{20,116},{24,16},{28,124},{32... | collective-permute-start | bytes 3342344 | tf_op jit(solution)/shard_map/ppermute | solution.py:72
  252.4 30.4 %collective-permute-start.44 = (bf16[1024,1024]{1,0:T(8,128)(2,1)}, bf16[1024,1024]{1,0:T(8,128)(2,1)}, u32[]{:S(2)}, u32[]{:S(2)}) collective-permute-start(bf16[1024,1024]{1,0:T(8,128)(2,1)} %get-tuple-element.243), channel_id=1, source_target_pairs={{0,8},{4,36},{8,16},{12,44},{16,24},{20,52},{24,0},{28,60},{32,40}... | collective-permute-start | bytes 6291464 | tf_op jit(solution)/shard_map/ppermute | solution.py:72
  256.1 33.1 %collective-permute-start.43 = (bf16[1024,1024]{1,0:T(8,128)(2,1)}, bf16[1024,1024]{1,0:T(8,128)(2,1)}, u32[]{:S(2)}, u32[]{:S(2)}) collective-permute-start(bf16[1024,1024]{1,0:T(8,128)(2,1)} %get-tuple-element.240), channel_id=1, source_target_pairs={{0,24},{4,100},{8,0},{12,108},{16,8},{20,116},{24,16},{28,124},{32... | collective-permute-start | bytes 6291464 | tf_op jit(solution)/shard_map/ppermute | solution.py:72
  264.7 22.1 %collective-permute-start.41 = (bf16[384,1024]{1,0:T(8,128)(2,1)}, bf16[384,1024]{1,0:T(8,128)(2,1)}, u32[]{:S(2)}, u32[]{:S(2)}) collective-permute-start(bf16[384,1024]{1,0:T(8,128)(2,1)} %get-tuple-element.233), channel_id=1, source_target_pairs={{0,1},{1,2},{2,3},{3,0},{4,5},{5,6},{6,7},{7,4},{8,9},{9,10},{10,1... | collective-permute-start | bytes 2359304 | tf_op jit(solution)/shard_map/ppermute | solution.py:60
  266.5 22.7 %collective-permute-start.42 = (bf16[384,1024]{1,0:T(8,128)(2,1)}, bf16[384,1024]{1,0:T(8,128)(2,1)}, u32[]{:S(2)}, u32[]{:S(2)}) collective-permute-start(bf16[384,1024]{1,0:T(8,128)(2,1)} %get-tuple-element.234), channel_id=1, source_target_pairs={{0,3},{1,0},{2,1},{3,2},{4,7},{5,4},{6,5},{7,6},{8,11},{9,8},{10,9... | collective-permute-start | bytes 2359304 | tf_op jit(solution)/shard_map/ppermute | solution.py:60
  289.2 27.2 %collective-permute-start.50 = (bf16[1024,1024]{1,0:T(8,128)(2,1)}, bf16[1024,1024]{1,0:T(8,128)(2,1)}, u32[]{:S(2)}, u32[]{:S(2)}) collective-permute-start(bf16[1024,1024]{1,0:T(8,128)(2,1)} %add_convert_fusion), channel_id=1, source_target_pairs={{0,8},{4,36},{8,16},{12,44},{16,24},{20,52},{24,0},{28,60},{32,40}... | collective-permute-start | bytes 6291464 | tf_op jit(solution)/shard_map/ppermute | solution.py:72
  292.4 24.0 %collective-permute-start.51 = (bf16[4,512,512]{2,1,0:T(8,128)(2,1)}, bf16[4,512,512]{2,1,0:T(8,128)(2,1)}, u32[]{:S(2)}, u32[]{:S(2)}) collective-permute-start(bf16[4,512,512]{2,1,0:T(8,128)(2,1)} %all-to-all-done.1.weights), channel_id=1, source_target_pairs={{0,4},{4,0},{1,5},{5,1},{2,6},{6,2},{3,7},{7,3},{8,12},{12,8},{9,1... | collective-permute-start | bytes 6291464 | tf_op jit(solution)/shard_map/ppermute | solution.py:80
  309.3 33.6 %all-to-all-start.2 = ((bf16[32,64,512]{2,1,0:T(8,128)(2,1)}), bf16[32,64,512]{2,1,0:T(8,128)(2,1)S(1)}, u32[]{:S(2)}, u32[]{:S(2)}) async-start(bf16[32,64,512]{2,1,0:T(8,128)(2,1)} %shard_map.241), calls=%async_computation.2 | async-start | bytes 4194304 | tf_op jit(solution)/shard_map/all_to_all | solution.py:110
  316.3 38.6 %collective-permute-start.55 = (bf16[384,1024]{1,0:T(8,128)(2,1)}, bf16[384,1024]{1,0:T(8,128)(2,1)}, u32[]{:S(2)}, u32[]{:S(2)}) collective-permute-start(bf16[384,1024]{1,0:T(8,128)(2,1)} %add_convert_fusion.3), channel_id=1, source_target_pairs={{0,1},{1,2},{2,3},{3,0},{4,5},{5,6},{6,7},{7,4},{8,9},{9,10},{10,1... | collective-permute-start | bytes 2359304 | tf_op jit(solution)/shard_map/ppermute | solution.py:60
  347.5 53.7 %all-to-all-start.3 = ((bf16[32,64,512]{2,1,0:T(8,128)(2,1)}), bf16[32,64,512]{2,1,0:T(8,128)(2,1)S(1)}, u32[]{:S(2)}, u32[]{:S(2)}) async-start(bf16[32,64,512]{2,1,0:T(8,128)(2,1)} %get-tuple-element.277), calls=%async_computation.3 | async-start | bytes 4194304 | tf_op jit(solution)/shard_map/all_to_all | solution.py:110
  357.7 21.0 %collective-permute-start.56 = (bf16[384,1024]{1,0:T(8,128)(2,1)}, bf16[384,1024]{1,0:T(8,128)(2,1)S(1)}, u32[]{:S(2)}, u32[]{:S(2)}) collective-permute-start(bf16[384,1024]{1,0:T(8,128)(2,1)} %shard_map.245.own), channel_id=1, source_target_pairs={{0,1},{1,2},{2,3},{3,0},{4,5},{5,6},{6,7},{7,4},{8,9},{9,10},{10,1... | collective-permute-start | bytes 2359304 | tf_op jit(solution)/shard_map/ppermute | solution.py:60
  357.7 21.0 %collective-permute-start.57 = (bf16[384,1024]{1,0:T(8,128)(2,1)}, bf16[384,1024]{1,0:T(8,128)(2,1)S(1)}, u32[]{:S(2)}, u32[]{:S(2)}) collective-permute-start(bf16[384,1024]{1,0:T(8,128)(2,1)} %shard_map.245.own), channel_id=1, source_target_pairs={{0,3},{1,0},{2,1},{3,2},{4,7},{5,4},{6,5},{7,6},{8,11},{9,8},{10,9... | collective-permute-start | bytes 2359304 | tf_op jit(solution)/shard_map/ppermute | solution.py:60
  361.0 25.9 %collective-permute-start.54 = (bf16[256,1024]{1,0:T(8,128)(2,1)}, bf16[256,1024]{1,0:T(8,128)(2,1)S(1)}, u32[]{:S(2)}, u32[]{:S(2)}) collective-permute-start(bf16[256,1024]{1,0:T(8,128)(2,1)} %get-tuple-element.280), channel_id=1, source_target_pairs={{0,32},{4,12},{8,40},{12,20},{16,48},{20,28},{24,56},{28,4},{32,64... | collective-permute-start | bytes 1572872 | tf_op jit(solution)/shard_map/ppermute | solution.py:72
  362.5 30.2 %collective-permute-start.53 = (bf16[256,1024]{1,0:T(8,128)(2,1)}, bf16[256,1024]{1,0:T(8,128)(2,1)S(1)}, u32[]{:S(2)}, u32[]{:S(2)}) collective-permute-start(bf16[256,1024]{1,0:T(8,128)(2,1)} %get-tuple-element.279), channel_id=1, source_target_pairs={{0,64},{4,20},{8,72},{12,28},{16,80},{20,4},{24,88},{28,12},{32,96... | collective-permute-start | bytes 1572872 | tf_op jit(solution)/shard_map/ppermute | solution.py:72
  365.3 28.5 %collective-permute-start.52 = (bf16[256,1024]{1,0:T(8,128)(2,1)S(1)}, bf16[256,1024]{1,0:T(8,128)(2,1)S(1)}, u32[]{:S(2)}, u32[]{:S(2)}) collective-permute-start(bf16[256,1024]{1,0:T(8,128)(2,1)S(1)} %copy-done.34), channel_id=1, source_target_pairs={{0,96},{4,28},{8,104},{12,4},{16,112},{20,12},{24,120},{28,20},{32... | collective-permute-start | bytes 1572872 | tf_op jit(solution)/shard_map/ppermute | solution.py:72
  (81 other events, 866.3 us)

commit v4 on v3

--- a/solution.py
+++ b/solution.py
@@ -891,7 +891,9 @@
         flops=2 * 10**9,
     ))
     mix_terms = direct_swap(mix_folded, shift_u)
-    arrived, mix_folded[0] = together(arrived, mix_folded[0])
+    arrived, mix_folded[0], mix_terms[1], mix_terms[3] = together(
+        arrived, mix_folded[0], mix_terms[1], mix_terms[3]
+    )
     shared, last = call(
         share_kernel,
         [array(packed.shape, bf16), array((16, depth // 2), f32)],

time: 413 us -> 410 us (level)
    ppermute x24, waiting for transfers between devices: 27.9 us -> 32.2 us  [line_shift(): return lax.ppermute(values, 'head', pairs)]
  transfers between devices with their start and end apart: 67 -> 67, of which waited for: 23 -> 25; matrix products, arithmetic and copies ran while one was open for 7% -> 7% of each run, Pallas kernels for 35% -> 35%
where the time goes in v4:
time: 410 us; the launch traced here: 405 us
  Pallas kernels  151 us (37%)
  waiting for transfers between devices  108 us (26%)
  starting transfers between devices  104 us (25%)
  local copies, waits for them, and re-layouts  20.1 us (5%)
  other arithmetic  19.4 us (5%)
    pallas_call x19, Pallas kernels, call(): pl.pallas_call(kernel, out_shape=out_shapes, in_specs=specs or [whole] *...  151 us
    ppermute x33, waiting for transfers between devices, plane_shift(): return lax.ppermute(values, PLANE, pairs)  60.6 us
    ppermute x33, starting transfers between devices, plane_shift(): return lax.ppermute(values, PLANE, pairs)  53.3 us
    ppermute x24, waiting for transfers between devices, line_shift(): return lax.ppermute(values, 'head', pairs)  32.2 us
    ppermute x24, starting transfers between devices, line_shift(): return lax.ppermute(values, 'head', pairs)  28.6 us
    all_to_all x4, starting transfers between devices, swap_all(): return lax.all_to_all(values, axes, 0, 0, tiled=True)  21.9 us
    all_to_all x4, waiting for transfers between devices, swap_all(): return lax.all_to_all(values, axes, 0, 0, tiled=True)  14.9 us
    unnamed x97, local copies, waits for them, and re-layouts  13.7 us
  transfers between devices with their start and end apart: 67, of which 25 were waited for; matrix products, arithmetic and copies ran while one was open for 7% of the time, Pallas kernels for 35%

profile of v4, /device:TPU:4, one launch (start us, length us, event | category | flops | bytes accessed | tf_op | source)
XLA Modules:
  0.0 404.8 jit_solution(1606337301656583866)
XLA Ops:
  30.3 4.4 %all-to-all-start = ((bf16[4,128,1024]{2,1,0:T(8,128)(2,1)}), bf16[4,128,1024]{2,1,0:T(8,128)(2,1)S(1)}, u32[]{:S(2)}, u32[]{:S(2)}) async-start(bf16[4,128,1024]{2,1,0:T(8,128)(2,1)} %broadcast_in_dim.28), calls=%async_computation | async-start | bytes 2097152 | tf_op jit(solution)/shard_map/all_to_all | solution.py:110
  34.7 12.3 %shard_map.229 = (bf16[1024,1024]{1,0:T(8,128)(2,1)}, bf16[1024,256]{1,0:T(8,128)(2,1)}, bf16[1024,256]{1,0:T(8,128)(2,1)}, bf16[1024,256]{1,0:T(8,128)(2,1)}, b...) custom-call(s32[4]{0:T(128)} %pad_add_fusion.at, ...), custom_call_target="tpu_custom_call" | custom-call | flops 12000000000 | bytes 9445392 | tf_op jit(solution)/shard_map/pallas_call | solution.py:39
  53.4 3.6 collective-permute-done.9.mixed_1
  66.9 5.7 %collective-permute-done.13 = bf16[256,1024]{1,0:T(8,128)(2,1)S(1)} collective-permute-done((bf16[256,1024]{1,0:T(8,128)(2,1)S(1)}, bf16[256,1024]{1,0:T(8,128)(2,1)S(1)}, u32[]{:S(2)}, u32[]{:S(2)}) %collective-permute-start.13) | collective-permute-done | bytes 524320 | tf_op jit(solution)/shard_map/ppermute | solution.py:72
  76.5 4.7 %collective-permute-done.16 = bf16[256,1024]{1,0:T(8,128)(2,1)S(1)} collective-permute-done((bf16[256,1024]{1,0:T(8,128)(2,1)S(1)}, bf16[256,1024]{1,0:T(8,128)(2,1)S(1)}, u32[]{:S(2)}, u32[]{:S(2)}) %collective-permute-start.16) | collective-permute-done | bytes 524320 | tf_op jit(solution)/shard_map/ppermute | solution.py:72
  92.3 4.4 %all-to-all-start.1 = ((bf16[4,512,512]{2,1,0:T(8,128)(2,1)}), bf16[4,512,512]{2,1,0:T(8,128)(2,1)}, u32[]{:S(2)}, u32[]{:S(2)}) async-start(bf16[4,512,512]{2,1,0:T(8,128)(2,1)} %broadcast_in_dim.52), calls=%async_computation.1 | async-start | bytes 4194304 | tf_op jit(solution)/shard_map/all_to_all | solution.py:110
  105.5 14.4 %shard_map.231 = (bf16[544,1024]{1,0:T(8,128)(2,1)}, bf16[544,1024]{1,0:T(8,128)(2,1)}, f32[32,256]{1,0:T(8,128)}, bf16[1024,1024]{1,0:T(8,128)(2,1)}, bf16[2,38...) custom-call(s32[4]{0:T(128)} %pad_add_fusion.at, ...), custom_call_target="tpu_custom_call" | custom-call | flops 14000000000 | bytes 20742160 | tf_op jit(solution)/shard_map/pallas_call | solution.py:39
  122.5 4.2 %collective-permute-done.26.g_a = bf16[272,1024]{1,0:T(8,128)(2,1)} collective-permute-done((bf16[272,1024]{1,0:T(8,128)(2,1)}, bf16[272,1024]{1,0:T(8,128)(2,1)}, u32[]{:S(2)}, u32[]{:S(2)}) %collective-permute-start.26) | collective-permute-done | bytes 557088 | tf_op jit(solution)/shard_map/ppermute | solution.py:72
  126.7 5.6 %collective-permute-done.25.x_a = bf16[256,1024]{1,0:T(8,128)(2,1)} collective-permute-done((bf16[256,1024]{1,0:T(8,128)(2,1)S(1)}, bf16[256,1024]{1,0:T(8,128)(2,1)}, u32[]{:S(2)}, u32[]{:S(2)}) %collective-permute-start.25) | collective-permute-done | bytes 524320 | tf_op jit(solution)/shard_map/ppermute | solution.py:72
  132.3 14.4 %shard_map.232 = (bf16[544,1024]{1,0:T(8,128)(2,1)}, bf16[544,1024]{1,0:T(8,128)(2,1)}, f32[32,256]{1,0:T(8,128)}, bf16[1024,1024]{1,0:T(8,128)(2,1)}, bf16[2,38...) custom-call(s32[4]{0:T(128)} %pad_add_fusion.at, ...), custom_call_target="tpu_custom_call" | custom-call | flops 14000000000 | bytes 20742160 | tf_op jit(solution)/shard_map/pallas_call | solution.py:39
  150.8 14.3 %shard_map.233 = (bf16[544,1024]{1,0:T(8,128)(2,1)}, bf16[544,1024]{1,0:T(8,128)(2,1)}, f32[32,256]{1,0:T(8,128)}, bf16[1024,1024]{1,0:T(8,128)(2,1)}, bf16[2,38...) custom-call(s32[4]{0:T(128)} %pad_add_fusion.at, ...), custom_call_target="tpu_custom_call" | custom-call | flops 14000000000 | bytes 20742160 | tf_op jit(solution)/shard_map/pallas_call | solution.py:39
  167.5 14.5 %shard_map.234 = (bf16[544,1024]{1,0:T(8,128)(2,1)}, bf16[544,1024]{1,0:T(8,128)(2,1)}, f32[32,256]{1,0:T(8,128)}, bf16[1024,1024]{1,0:T(8,128)(2,1)}, bf16[2,38...) custom-call(s32[4]{0:T(128)} %pad_add_fusion.at, ...), custom_call_target="tpu_custom_call" | custom-call | flops 14000000000 | bytes 20742160 | tf_op jit(solution)/shard_map/pallas_call | solution.py:39
  188.8 9.0 %collective-permute-done.32.after_lo = bf16[544,1024]{1,0:T(8,128)(2,1)S(1)} collective-permute-done((bf16[544,1024]{1,0:T(8,128)(2,1)}, bf16[544,1024]{1,0:T(8,128)(2,1)S(1)}, u32[]{:S(2)}, u32[]{:S(2)}) %collective-permute-start.32) | collective-permute-done | bytes 1114144 | tf_op jit(solution)/shard_map/ppermute | solution.py:72
  197.8 3.9 collective-permute-done.30.before_lo
  201.8 8.0 %collective-permute-done.34.after_hi = bf16[544,1024]{1,0:T(8,128)(2,1)S(1)} collective-permute-done((bf16[544,1024]{1,0:T(8,128)(2,1)S(1)}, bf16[544,1024]{1,0:T(8,128)(2,1)S(1)}, u32[]{:S(2)}, u32[]{:S(2)}) %collective-permute-start.34) | collective-permute-done | bytes 1114144 | tf_op jit(solution)/shard_map/ppermute | solution.py:72
  210.8 4.5 %shard_map.235 = (bf16[272,1024]{1,0:T(8,128)(2,1)}, bf16[272,1024]{1,0:T(8,128)(2,1)}, bf16[272,1024]{1,0:T(8,128)(2,1)}, bf16[272,1024]{1,0:T(8,128)(2,1)}) custom-call(bf16[544,1024]{1,0:T(8,128)(2,1)} %get-tuple-element.183.own_lo, bf16[544,1024]{1,0:T(8,128)(2,1)} %get-tuple-element.184.own_hi, bf16[544,1024]{1,0:T(8,128)(2,1)} %copy-done.30, ...), custom_call_target="tpu_custom_call" | custom-call | flops 2000000000 | bytes 8912896 | tf_op jit(solution)/shard_map/pallas_call | solution.py:39
  218.4 11.0 %shard_map.236.own = bf16[1536,1024]{1,0:T(8,128)(2,1)} custom-call(bf16[2,384,1024]{2,1,0:T(8,128)(2,1)} %get-tuple-element.232.refs_0_, bf16[2,384,1024]{2,1,0:T(8,128)(2,1)} %get-tuple-element.208.refs_1_, bf16[2,384,512]{2,1,0:T(8,128)(2,1)} %get-tuple-element.209.refs_2_, bf16[2,384,1024]{2,1,0:T(8,128)(2,1)} %get-tuple-element.210.refs_3_, ...), custom_call_target="tpu_custom_call" | custom-call | flops 10000000000 | bytes 25165824 | tf_op jit(solution)/shard_map/pallas_call | solution.py:39
  229.3 4.6 %collective-permute-done.37.term_3 = bf16[272,1024]{1,0:T(8,128)(2,1)S(1)} collective-permute-done((bf16[272,1024]{1,0:T(8,128)(2,1)}, bf16[272,1024]{1,0:T(8,128)(2,1)S(1)}, u32[]{:S(2)}, u32[]{:S(2)}) %collective-permute-start.37) | collective-permute-done | bytes 557088 | tf_op jit(solution)/shard_map/ppermute | solution.py:72
  241.3 10.9 %shard_map.238 = bf16[1536,1024]{1,0:T(8,128)(2,1)} custom-call(bf16[2,384,1024]{2,1,0:T(8,128)(2,1)} %get-tuple-element.232.refs_0_, bf16[2,384,1024]{2,1,0:T(8,128)(2,1)} %get-tuple-element.208.refs_1_, bf16[2,384,512]{2,1,0:T(8,128)(2,1)} %get-tuple-element.209.refs_2_, bf16[2,384,1024]{2,1,0:T(8,128)(2,1)} %get-tuple-element.210.refs_3_, ...), custom_call_target="tpu_custom_call" | custom-call | flops 10000000000 | bytes 25165824 | tf_op jit(solution)/shard_map/pallas_call | solution.py:39
  258.4 6.3 %shard_map.239 = (bf16[384,1024]{1,0:T(8,128)(2,1)}, bf16[384,1024]{1,0:T(8,128)(2,1)}, bf16[384,1024]{1,0:T(8,128)(2,1)}, bf16[384,1024]{1,0:T(8,128)(2,1)}) custom-call(s32[4]{0:T(128)} %pad_add_fusion.at, bf16[1536,1024]{1,0:T(8,128)(2,1)} %shard_map.236.own, bf16[1536,1024]{1,0:T(8,128)(2,1)} %collective-permute-done.40.sib), custom_call_target="tpu_custom_call" | custom-call | flops 3000000000 | bytes 9437200 | tf_op jit(solution)/shard_map/pallas_call | solution.py:39
  268.9 13.9 %shard_map.240 = (bf16[1024,512]{1,0:T(8,128)(2,1)}, bf16[256,512]{1,0:T(8,128)(2,1)}, bf16[256,512]{1,0:T(8,128)(2,1)}, bf16[256,512]{1,0:T(8,128)(2,1)}, bf16[256,512]{1,0:T(8,128)(2,1)}) custom-call(s32[4]{0:T(128)} %pad_add_fusion.at, bf16[304,1024]{1,0:T(8,128)(2,1)} %copy-done.2, bf16[304,1024]{1,0:T(8,128)(2,1)} %copy-done.23, ...), custom_call_target="tpu_custom_call" | custom-call | flops 12000000000 | bytes 8785936 | tf_op jit(solution)/shard_map/pallas_call | solution.py:39
  282.8 3.9 add_convert_fusion
  294.8 7.0 %shard_map.241 = bf16[32,64,512]{2,1,0:T(8,128)(2,1)} custom-call(s32[4]{0:T(128)} %pad_add_fusion.at, bf16[1024,1024]{1,0:T(8,128)(2,1)} %get-tuple-element.258.normed, bf16[1024,512]{1,0:T(8,128)(2,1)} %get-tuple-element.259.grads, bf16[1024,256]{1,0:T(8,128)(2,1)} %get-tuple-element.253.mixed, bf16[304,1024]{1,0:T(8,128)(2,1)} %copy-done.2, ...), custom_call_target="tpu_custom_call" | custom-call | flops 6000000000 | bytes 9310224 | tf_op jit(solution)/shard_map/pallas_call | solution.py:39
  303.4 5.2 %collective-permute-done.49.g_3 = bf16[256,512]{1,0:T(8,128)(2,1)S(1)} collective-permute-done((bf16[256,512]{1,0:T(8,128)(2,1)S(1)}, bf16[256,512]{1,0:T(8,128)(2,1)S(1)}, u32[]{:S(2)}, u32[]{:S(2)}) %collective-permute-start.49) | collective-permute-done | bytes 262176 | tf_op jit(solution)/shard_map/ppermute | solution.py:60
  309.3 7.0 %all-to-all-start.2 = ((bf16[32,64,512]{2,1,0:T(8,128)(2,1)}), bf16[32,64,512]{2,1,0:T(8,128)(2,1)S(1)}, u32[]{:S(2)}, u32[]{:S(2)}) async-start(bf16[32,64,512]{2,1,0:T(8,128)(2,1)} %shard_map.241), calls=%async_computation.2 | async-start | bytes 4194304 | tf_op jit(solution)/shard_map/all_to_all | solution.py:110
  316.4 5.6 %shard_map.242 = f32[256,1024]{1,0:T(8,128)} custom-call(s32[4]{0:T(128)} %pad_add_fusion.at, bf16[256,512]{1,0:T(8,128)(2,1)} %get-tuple-element.268.g_0, bf16[256,512]{1,0:T(8,128)(2,1)} %copy-done.43, bf16[256,512]{1,0:T(8,128)(2,1)} %copy-done.44, bf16[256,512]{1,0:T(8,128)(2,1)} %copy-done.45, bf16[4,512,512]{2,1,0:T(8,128)(2,1)} %all-to-all-done.1.weights, ...), custom_call_target="tpu_custom_call" | custom-call | flops 4000000000 | bytes 7868432 | tf_op jit(solution)/shard_map/pallas_call | solution.py:39
  322.0 4.4 %shard_map.243 = (bf16[256,1024]{1,0:T(8,128)(2,1)}, bf16[256,1024]{1,0:T(8,128)(2,1)}, bf16[256,1024]{1,0:T(8,128)(2,1)}, bf16[256,1024]{1,0:T(8,128)(2,1)}) custom-call(bf16[1024,1024]{1,0:T(8,128)(2,1)} %get-tuple-element.274.own, bf16[1024,1024]{1,0:T(8,128)(2,1)} %collective-permute-done.50.before, bf16[1024,1024]{1,0:T(8,128)(2,1)} %collective-permute-done.43.after_), custom_call_target="tpu_custom_call" | custom-call | flops 2000000000 | bytes 8388608 | tf_op jit(solution)/shard_map/pallas_call | solution.py:39
  329.2 13.8 %all-to-all-done.2.parts = bf16[32,64,512]{2,1,0:T(8,128)(2,1)S(1)} async-done(((bf16[32,64,512]{2,1,0:T(8,128)(2,1)}), bf16[32,64,512]{2,1,0:T(8,128)(2,1)S(1)}, u32[]{:S(2)}, u32[]{:S(2)}) %all-to-all-start.2) | async-done | bytes 2097184 | tf_op jit(solution)/shard_map/all_to_all | solution.py:110
  342.9 4.2 %collective-permute-done.52 = bf16[256,1024]{1,0:T(8,128)(2,1)} collective-permute-done((bf16[256,1024]{1,0:T(8,128)(2,1)}, bf16[256,1024]{1,0:T(8,128)(2,1)}, u32[]{:S(2)}, u32[]{:S(2)}) %collective-permute-start.52) | collective-permute-done | bytes 524320 | tf_op jit(solution)/shard_map/ppermute | solution.py:72
  351.7 6.1 %all-to-all-start.3 = ((bf16[32,64,512]{2,1,0:T(8,128)(2,1)}), bf16[32,64,512]{2,1,0:T(8,128)(2,1)S(1)}, u32[]{:S(2)}, u32[]{:S(2)}) async-start(bf16[32,64,512]{2,1,0:T(8,128)(2,1)} %get-tuple-element.281), calls=%async_computation.3 | async-start | bytes 4194304 | tf_op jit(solution)/shard_map/all_to_all | solution.py:110
  366.8 14.8 %collective-permute-done.56.from_before = bf16[384,1024]{1,0:T(8,128)(2,1)S(1)} collective-permute-done((bf16[384,1024]{1,0:T(8,128)(2,1)}, bf16[384,1024]{1,0:T(8,128)(2,1)S(1)}, u32[]{:S(2)}, u32[]{:S(2)}) %collective-permute-start.56) | collective-permute-done | bytes 786464 | tf_op jit(solution)/shard_map/ppermute | solution.py:60
  394.7 4.9 %shard_map.246 = (f32[1,1024,512]{2,1,0:T(8,128)}, f32[1,1024,512]{2,1,0:T(8,128)}, f32[1,512,1024]{2,1,0:T(8,128)}) custom-call(s32[4]{0:T(128)} %pad_add_fusion.at, bf16[384,1024]{1,0:T(8,128)(2,1)} %shard_map.245.own, bf16[384,1024]{1,0:T(8,128)(2,1)} %copy-done.22, bf16[192,1024]{1,0:T(8,128)(2,1)} %copy-done.35, ...), custom_call_target="tpu_custom_call" | custom-call | flops 4000000000 | bytes 9437200 | tf_op jit(solution)/shard_map/pallas_call | solution.py:39
  (248 shorter events, 151.5 us)
Async XLA Ops:
  0.6 18.4 %collective-permute-start = (bf16[256,1024]{1,0:T(8,128)(2,1)}, bf16[256,1024]{1,0:T(8,128)(2,1)S(1)}, u32[]{:S(2)}, u32[]{:S(2)}) collective-permute-start(bf16[256,1024]{1,0:T(8,128)(2,1)} %tokens.3), channel_id=1, source_target_pairs={{0,1},{1,2},{2,3},{3,0},{4,5},{5,6},{6,7},{7,4},{8,9},{9,10},{10,1... | collective-permute-start | bytes 1572872 | tf_op jit(solution)/shard_map/ppermute | solution.py:60
  8.5 17.3 %collective-permute-start.5 = (bf16[272,1024]{1,0:T(8,128)(2,1)}, bf16[272,1024]{1,0:T(8,128)(2,1)S(1)}, u32[]{:S(2)}, u32[]{:S(2)}) collective-permute-start(bf16[272,1024]{1,0:T(8,128)(2,1)} %fusion.1.g_a), channel_id=1, source_target_pairs={{0,64},{4,20},{8,72},{12,28},{16,80},{20,4},{24,88},{28,12},{32,96... | collective-permute-start | bytes 1671176 | tf_op jit(solution)/shard_map/ppermute | solution.py:72
  28.3 23.0 %collective-permute-start.7 = (bf16[816,1024]{1,0:T(8,128)(2,1)}, bf16[816,1024]{1,0:T(8,128)(2,1)}, u32[]{:S(2)}, u32[]{:S(2)}) collective-permute-start(bf16[816,1024]{1,0:T(8,128)(2,1)} %pad_maximum_fusion.g_b), channel_id=1, source_target_pairs={{0,8},{4,36},{8,16},{12,44},{16,24},{20,52},{24,0},{28,60},{32,40}... | collective-permute-start | bytes 5013512 | tf_op jit(solution)/shard_map/ppermute | solution.py:72
  29.5 22.7 %collective-permute-start.8 = (bf16[816,1024]{1,0:T(8,128)(2,1)}, bf16[816,1024]{1,0:T(8,128)(2,1)}, u32[]{:S(2)}, u32[]{:S(2)}) collective-permute-start(bf16[816,1024]{1,0:T(8,128)(2,1)} %pad_maximum_fusion.g_b), channel_id=1, source_target_pairs={{0,24},{4,100},{8,0},{12,108},{16,8},{20,116},{24,16},{28,124},{32... | collective-permute-start | bytes 5013512 | tf_op jit(solution)/shard_map/ppermute | solution.py:72
  30.3 17.8 %all-to-all-start = ((bf16[4,128,1024]{2,1,0:T(8,128)(2,1)}), bf16[4,128,1024]{2,1,0:T(8,128)(2,1)S(1)}, u32[]{:S(2)}, u32[]{:S(2)}) async-start(bf16[4,128,1024]{2,1,0:T(8,128)(2,1)} %broadcast_in_dim.28), calls=%async_computation | async-start | bytes 2097152 | tf_op jit(solution)/shard_map/all_to_all | solution.py:110
  82.1 20.7 %collective-permute-start.21 = (bf16[768,1024]{1,0:T(8,128)(2,1)}, bf16[768,1024]{1,0:T(8,128)(2,1)}, u32[]{:S(2)}, u32[]{:S(2)}) collective-permute-start(bf16[768,1024]{1,0:T(8,128)(2,1)} %constant_dynamic-update-slice_fusion.x_b), channel_id=1, source_target_pairs={{0,24},{4,100},{8,0},{12,108},{16,8},{20,116},{24,16},{28,124},{32... | collective-permute-start | bytes 4718600 | tf_op jit(solution)/shard_map/ppermute | solution.py:72
  86.8 33.2 %collective-permute-start.22 = (bf16[768,1024]{1,0:T(8,128)(2,1)}, bf16[768,1024]{1,0:T(8,128)(2,1)}, u32[]{:S(2)}, u32[]{:S(2)}) collective-permute-start(bf16[768,1024]{1,0:T(8,128)(2,1)} %constant_dynamic-update-slice_fusion.x_b), channel_id=1, source_target_pairs={{0,8},{4,36},{8,16},{12,44},{16,24},{20,52},{24,0},{28,60},{32,40}... | collective-permute-start | bytes 4718600 | tf_op jit(solution)/shard_map/ppermute | solution.py:72
  90.7 31.8 %collective-permute-start.24 = (bf16[816,1024]{1,0:T(8,128)(2,1)}, bf16[816,1024]{1,0:T(8,128)(2,1)}, u32[]{:S(2)}, u32[]{:S(2)}) collective-permute-start(bf16[816,1024]{1,0:T(8,128)(2,1)} %collective-permute-done.8.g_b), channel_id=1, source_target_pairs={{0,24},{4,100},{8,0},{12,108},{16,8},{20,116},{24,16},{28,124},{32... | collective-permute-start | bytes 5013512 | tf_op jit(solution)/shard_map/ppermute | solution.py:72
  92.3 54.4 %all-to-all-start.1 = ((bf16[4,512,512]{2,1,0:T(8,128)(2,1)}), bf16[4,512,512]{2,1,0:T(8,128)(2,1)}, u32[]{:S(2)}, u32[]{:S(2)}) async-start(bf16[4,512,512]{2,1,0:T(8,128)(2,1)} %broadcast_in_dim.52), calls=%async_computation.1 | async-start | bytes 4194304 | tf_op jit(solution)/shard_map/all_to_all | solution.py:110
  96.8 29.9 %collective-permute-start.26 = (bf16[272,1024]{1,0:T(8,128)(2,1)}, bf16[272,1024]{1,0:T(8,128)(2,1)}, u32[]{:S(2)}, u32[]{:S(2)}) collective-permute-start(bf16[272,1024]{1,0:T(8,128)(2,1)} %fusion.1.g_a), channel_id=1, source_target_pairs={{0,24},{4,100},{8,0},{12,108},{16,8},{20,116},{24,16},{28,124},{32... | collective-permute-start | bytes 1671176 | tf_op jit(solution)/shard_map/ppermute | solution.py:72
  98.4 33.9 %collective-permute-start.25 = (bf16[256,1024]{1,0:T(8,128)(2,1)S(1)}, bf16[256,1024]{1,0:T(8,128)(2,1)}, u32[]{:S(2)}, u32[]{:S(2)}) collective-permute-start(bf16[256,1024]{1,0:T(8,128)(2,1)S(1)} %get-tuple-element.175.x_a.inputs), channel_id=1, source_target_pairs={{0,24},{4,100},{8,0},{12,108},{16,8},{20,116},{24,16},{28,124},{32... | collective-permute-start | bytes 1572872 | tf_op jit(solution)/shard_map/ppermute | solution.py:72
  102.8 17.2 %collective-permute-start.23 = (bf16[272,1024]{1,0:T(8,128)(2,1)}, bf16[272,1024]{1,0:T(8,128)(2,1)S(1)}, u32[]{:S(2)}, u32[]{:S(2)}) collective-permute-start(bf16[272,1024]{1,0:T(8,128)(2,1)} %copy-done.32), channel_id=1, source_target_pairs={{0,8},{4,36},{8,16},{12,44},{16,24},{20,52},{24,0},{28,60},{32,40}... | collective-permute-start | bytes 1671176 | tf_op jit(solution)/shard_map/ppermute | solution.py:72
  119.9 29.7 %collective-permute-start.28 = (bf16[768,1024]{1,0:T(8,128)(2,1)}, bf16[768,1024]{1,0:T(8,128)(2,1)S(1)}, u32[]{:S(2)}, u32[]{:S(2)}) collective-permute-start(bf16[768,1024]{1,0:T(8,128)(2,1)} %collective-permute-done.21.x_b), channel_id=1, source_target_pairs={{0,24},{4,100},{8,0},{12,108},{16,8},{20,116},{24,16},{28,124},{32... | collective-permute-start | bytes 4718600 | tf_op jit(solution)/shard_map/ppermute | solution.py:72
  120.0 29.6 %collective-permute-start.27 = (bf16[256,1024]{1,0:T(8,128)(2,1)}, bf16[256,1024]{1,0:T(8,128)(2,1)}, u32[]{:S(2)}, u32[]{:S(2)}) collective-permute-start(bf16[256,1024]{1,0:T(8,128)(2,1)} %collective-permute-done.20.x_a), channel_id=1, source_target_pairs={{0,8},{4,36},{8,16},{12,44},{16,24},{20,52},{24,0},{28,60},{32,40}... | collective-permute-start | bytes 1572872 | tf_op jit(solution)/shard_map/ppermute | solution.py:72
  146.7 42.2 %collective-permute-start.31 = (bf16[544,1024]{1,0:T(8,128)(2,1)}, bf16[544,1024]{1,0:T(8,128)(2,1)}, u32[]{:S(2)}, u32[]{:S(2)}) collective-permute-start(bf16[544,1024]{1,0:T(8,128)(2,1)} %get-tuple-element.198), channel_id=1, source_target_pairs={{0,8},{4,36},{8,16},{12,44},{16,24},{20,52},{24,0},{28,60},{32,40}... | collective-permute-start | bytes 3342344 | tf_op jit(solution)/shard_map/ppermute | solution.py:72
  165.2 18.2 %collective-permute-start.29 = (bf16[544,1024]{1,0:T(8,128)(2,1)}, bf16[544,1024]{1,0:T(8,128)(2,1)}, u32[]{:S(2)}, u32[]{:S(2)}) collective-permute-start(bf16[544,1024]{1,0:T(8,128)(2,1)} %get-tuple-element.197), channel_id=1, source_target_pairs={{0,8},{4,36},{8,16},{12,44},{16,24},{20,52},{24,0},{28,60},{32,40}... | collective-permute-start | bytes 3342344 | tf_op jit(solution)/shard_map/ppermute | solution.py:72
  167.3 18.6 %collective-permute-start.33 = (bf16[544,1024]{1,0:T(8,128)(2,1)}, bf16[544,1024]{1,0:T(8,128)(2,1)S(1)}, u32[]{:S(2)}, u32[]{:S(2)}) collective-permute-start(bf16[544,1024]{1,0:T(8,128)(2,1)} %get-tuple-element.204), channel_id=1, source_target_pairs={{0,24},{4,100},{8,0},{12,108},{16,8},{20,116},{24,16},{28,124},{32... | collective-permute-start | bytes 3342344 | tf_op jit(solution)/shard_map/ppermute | solution.py:72
  186.4 23.3 %collective-permute-start.34 = (bf16[544,1024]{1,0:T(8,128)(2,1)S(1)}, bf16[544,1024]{1,0:T(8,128)(2,1)S(1)}, u32[]{:S(2)}, u32[]{:S(2)}) collective-permute-start(bf16[544,1024]{1,0:T(8,128)(2,1)S(1)} %add_convert_fusion.1), channel_id=1, source_target_pairs={{0,24},{4,100},{8,0},{12,108},{16,8},{20,116},{24,16},{28,124},{32... | collective-permute-start | bytes 3342344 | tf_op jit(solution)/shard_map/ppermute | solution.py:72
  252.4 30.4 %collective-permute-start.44 = (bf16[1024,1024]{1,0:T(8,128)(2,1)}, bf16[1024,1024]{1,0:T(8,128)(2,1)}, u32[]{:S(2)}, u32[]{:S(2)}) collective-permute-start(bf16[1024,1024]{1,0:T(8,128)(2,1)} %get-tuple-element.245), channel_id=1, source_target_pairs={{0,8},{4,36},{8,16},{12,44},{16,24},{20,52},{24,0},{28,60},{32,40}... | collective-permute-start | bytes 6291464 | tf_op jit(solution)/shard_map/ppermute | solution.py:72
  256.1 33.1 %collective-permute-start.43 = (bf16[1024,1024]{1,0:T(8,128)(2,1)}, bf16[1024,1024]{1,0:T(8,128)(2,1)}, u32[]{:S(2)}, u32[]{:S(2)}) collective-permute-start(bf16[1024,1024]{1,0:T(8,128)(2,1)} %get-tuple-element.242), channel_id=1, source_target_pairs={{0,24},{4,100},{8,0},{12,108},{16,8},{20,116},{24,16},{28,124},{32... | collective-permute-start | bytes 6291464 | tf_op jit(solution)/shard_map/ppermute | solution.py:72
  264.7 22.1 %collective-permute-start.41 = (bf16[384,1024]{1,0:T(8,128)(2,1)}, bf16[384,1024]{1,0:T(8,128)(2,1)}, u32[]{:S(2)}, u32[]{:S(2)}) collective-permute-start(bf16[384,1024]{1,0:T(8,128)(2,1)} %get-tuple-element.235), channel_id=1, source_target_pairs={{0,1},{1,2},{2,3},{3,0},{4,5},{5,6},{6,7},{7,4},{8,9},{9,10},{10,1... | collective-permute-start | bytes 2359304 | tf_op jit(solution)/shard_map/ppermute | solution.py:60
  266.5 22.7 %collective-permute-start.42 = (bf16[384,1024]{1,0:T(8,128)(2,1)}, bf16[384,1024]{1,0:T(8,128)(2,1)}, u32[]{:S(2)}, u32[]{:S(2)}) collective-permute-start(bf16[384,1024]{1,0:T(8,128)(2,1)} %get-tuple-element.236), channel_id=1, source_target_pairs={{0,3},{1,0},{2,1},{3,2},{4,7},{5,4},{6,5},{7,6},{8,11},{9,8},{10,9... | collective-permute-start | bytes 2359304 | tf_op jit(solution)/shard_map/ppermute | solution.py:60
  289.2 27.1 %collective-permute-start.50 = (bf16[1024,1024]{1,0:T(8,128)(2,1)}, bf16[1024,1024]{1,0:T(8,128)(2,1)}, u32[]{:S(2)}, u32[]{:S(2)}) collective-permute-start(bf16[1024,1024]{1,0:T(8,128)(2,1)} %add_convert_fusion), channel_id=1, source_target_pairs={{0,8},{4,36},{8,16},{12,44},{16,24},{20,52},{24,0},{28,60},{32,40}... | collective-permute-start | bytes 6291464 | tf_op jit(solution)/shard_map/ppermute | solution.py:72
  292.4 23.9 %collective-permute-start.51 = (bf16[4,512,512]{2,1,0:T(8,128)(2,1)}, bf16[4,512,512]{2,1,0:T(8,128)(2,1)}, u32[]{:S(2)}, u32[]{:S(2)}) collective-permute-start(bf16[4,512,512]{2,1,0:T(8,128)(2,1)} %all-to-all-done.1.weights), channel_id=1, source_target_pairs={{0,4},{4,0},{1,5},{5,1},{2,6},{6,2},{3,7},{7,3},{8,12},{12,8},{9,1... | collective-permute-start | bytes 6291464 | tf_op jit(solution)/shard_map/ppermute | solution.py:80
  309.3 33.6 %all-to-all-start.2 = ((bf16[32,64,512]{2,1,0:T(8,128)(2,1)}), bf16[32,64,512]{2,1,0:T(8,128)(2,1)S(1)}, u32[]{:S(2)}, u32[]{:S(2)}) async-start(bf16[32,64,512]{2,1,0:T(8,128)(2,1)} %shard_map.241), calls=%async_computation.2 | async-start | bytes 4194304 | tf_op jit(solution)/shard_map/all_to_all | solution.py:110
  326.4 20.7 %collective-permute-start.52 = (bf16[256,1024]{1,0:T(8,128)(2,1)}, bf16[256,1024]{1,0:T(8,128)(2,1)}, u32[]{:S(2)}, u32[]{:S(2)}) collective-permute-start(bf16[256,1024]{1,0:T(8,128)(2,1)} %get-tuple-element.278), channel_id=1, source_target_pairs={{0,96},{4,28},{8,104},{12,4},{16,112},{20,12},{24,120},{28,20},{32... | collective-permute-start | bytes 1572872 | tf_op jit(solution)/shard_map/ppermute | solution.py:72
  329.1 19.2 %collective-permute-start.53 = (bf16[256,1024]{1,0:T(8,128)(2,1)}, bf16[256,1024]{1,0:T(8,128)(2,1)}, u32[]{:S(2)}, u32[]{:S(2)}) collective-permute-start(bf16[256,1024]{1,0:T(8,128)(2,1)} %get-tuple-element.279), channel_id=1, source_target_pairs={{0,32},{4,12},{8,40},{12,20},{16,48},{20,28},{24,56},{28,4},{32,64... | collective-permute-start | bytes 1572872 | tf_op jit(solution)/shard_map/ppermute | solution.py:72
  329.1 28.6 %collective-permute-start.55 = (bf16[384,1024]{1,0:T(8,128)(2,1)}, bf16[384,1024]{1,0:T(8,128)(2,1)}, u32[]{:S(2)}, u32[]{:S(2)}) collective-permute-start(bf16[384,1024]{1,0:T(8,128)(2,1)} %add_convert_fusion.3), channel_id=1, source_target_pairs={{0,1},{1,2},{2,3},{3,0},{4,5},{5,6},{6,7},{7,4},{8,9},{9,10},{10,1... | collective-permute-start | bytes 2359304 | tf_op jit(solution)/shard_map/ppermute | solution.py:60
  351.7 48.0 %all-to-all-start.3 = ((bf16[32,64,512]{2,1,0:T(8,128)(2,1)}), bf16[32,64,512]{2,1,0:T(8,128)(2,1)S(1)}, u32[]{:S(2)}, u32[]{:S(2)}) async-start(bf16[32,64,512]{2,1,0:T(8,128)(2,1)} %get-tuple-element.281), calls=%async_computation.3 | async-start | bytes 4194304 | tf_op jit(solution)/shard_map/all_to_all | solution.py:110
  360.6 21.0 %collective-permute-start.56 = (bf16[384,1024]{1,0:T(8,128)(2,1)}, bf16[384,1024]{1,0:T(8,128)(2,1)S(1)}, u32[]{:S(2)}, u32[]{:S(2)}) collective-permute-start(bf16[384,1024]{1,0:T(8,128)(2,1)} %shard_map.245.own), channel_id=1, source_target_pairs={{0,1},{1,2},{2,3},{3,0},{4,5},{5,6},{6,7},{7,4},{8,9},{9,10},{10,1... | collective-permute-start | bytes 2359304 | tf_op jit(solution)/shard_map/ppermute | solution.py:60
  360.6 21.0 %collective-permute-start.57 = (bf16[384,1024]{1,0:T(8,128)(2,1)}, bf16[384,1024]{1,0:T(8,128)(2,1)S(1)}, u32[]{:S(2)}, u32[]{:S(2)}) collective-permute-start(bf16[384,1024]{1,0:T(8,128)(2,1)} %shard_map.245.own), channel_id=1, source_target_pairs={{0,3},{1,0},{2,1},{3,2},{4,7},{5,4},{6,5},{7,6},{8,11},{9,8},{10,9... | collective-permute-start | bytes 2359304 | tf_op jit(solution)/shard_map/ppermute | solution.py:60
  363.8 26.1 %collective-permute-start.54 = (bf16[256,1024]{1,0:T(8,128)(2,1)S(1)}, bf16[256,1024]{1,0:T(8,128)(2,1)S(1)}, u32[]{:S(2)}, u32[]{:S(2)}) collective-permute-start(bf16[256,1024]{1,0:T(8,128)(2,1)S(1)} %copy-done.34), channel_id=1, source_target_pairs={{0,64},{4,20},{8,72},{12,28},{16,80},{20,4},{24,88},{28,12},{32,96... | collective-permute-start | bytes 1572872 | tf_op jit(solution)/shard_map/ppermute | solution.py:72
  (81 other events, 843.6 us)

commit v5 on v4

--- a/solution.py
+++ b/solution.py
@@ -205,9 +205,15 @@
 
 
 def attend_back_kernel(
-    at, part_0, part_1, part_2a, part_2b, part_3, w_output, query, key, value, mixed, log_total, starts, cosine, sine,
-    grads, out_0, out_1, out_2, out_3, grad_in, grad_query,
+    at, part_0, part_1, part_2a, part_2b, part_3, w_output, query_in, key_in, value_in, mixed_in, logs_in, starts,
+    cosine_in, sine_in, grads, out_0, out_1, out_2, out_3, grad_in, grad_query,
+    query, key, value, mixed, log_total, cosine, sine, sems,
 ):
+    sources = (mixed_in, logs_in, key_in, query_in, value_in, cosine_in, sine_in)
+    kept = (mixed, log_total, key, query, value, cosine, sine)
+    loads = [pltpu.make_async_copy(a, b, sems.at[n]) for n, (a, b) in enumerate(zip(sources, kept))]
+    for load in loads:
+        load.start()
     rows, width = out_0.shape[0], query.shape[1]
     length = rows * SIDE
     heads = width // HEAD_DIM
@@ -219,13 +225,17 @@
     grad_in[low, :] = dot_rows(part_2a[...], w_output[...]).astype(bf16)
     high = pl.ds(pl.multiple_of(far + cut, 16), rows - cut)
     grad_in[high, :] = dot_rows(part_2b[: rows - cut, :], w_output[...]).astype(bf16)
+    loads[0].wait()
     both = grad_in[...].astype(f32) * mixed[...].astype(f32)
     both_hi = both.astype(bf16)
     both_lo = (both - both_hi.astype(f32)).astype(bf16)
     marks = lax.broadcasted_iota(jnp.int32, (8, width), 1) // HEAD_DIM
     marks = (marks == lax.broadcasted_iota(jnp.int32, (8, width), 0)).astype(bf16)
     inner = dot_rows(marks, both_hi) + dot_rows(marks, both_lo)
+    loads[1].wait()
     logs = jnp.transpose(log_total[...])
+    for load in loads[2:]:
+        load.wait()
     head_of = lax.broadcasted_iota(jnp.int32, (rows, width), 1) // HEAD_DIM
     lane = lax.broadcasted_iota(jnp.int32, (rows, LANES), 1)
     for j in range(SIDE):
@@ -452,12 +462,28 @@
             out[depth:, :] = lower.astype(bf16)
 
 
-def fold_kernel(own_lo, own_hi, before_lo, before_hi, after_lo, after_hi, *outs):
+def fold_kernel(own_lo, own_hi, before_lo, before_hi, after_lo, after_hi, *refs):
+    outs, (terms, sums, load_sems, store_sems) = refs[:SIDE], refs[SIDE:]
     rows = outs[0].shape[0]
-    for i, out in enumerate(outs):
-        part = slice(i % 2 * rows, (i % 2 + 1) * rows)
+
+    def load(i, n):
         refs = (own_lo, before_lo, after_lo) if i < 2 else (own_hi, before_hi, after_hi)
-        out[...] = sum(ref[part, :].astype(f32) for ref in refs).astype(bf16)
+        there = refs[n].at[pl.ds(i % 2 * rows, rows), :]
+        return pltpu.make_async_copy(there, terms.at[i, n], load_sems.at[i, n])
+
+    def store(i):
+        return pltpu.make_async_copy(sums.at[i], outs[i], store_sems.at[i])
+
+    for i in range(SIDE):
+        for n in range(3):
+            load(i, n).start()
+    for i in range(SIDE):
+        for n in range(3):
+            load(i, n).wait()
+        sums[i] = sum(terms[i, n].astype(f32) for n in range(3)).astype(bf16)
+        store(i).start()
+    for i in range(SIDE):
+        store(i).wait()
 
 
 def fold_mix_kernel(own, before, after_, *outs):
@@ -803,6 +829,14 @@
         fold_kernel,
         [array((rows + 16, depth), bf16)] * SIDE,
         [column[0], column[1], *from_before, *from_after],
+        specs=[anywhere] * 6,
+        out_specs=[hbm] * SIDE,
+        scratch=[
+            pltpu.VMEM((SIDE, 3, rows + 16, depth), bf16),
+            pltpu.VMEM((SIDE, rows + 16, depth), bf16),
+            pltpu.SemaphoreType.DMA((SIDE, 3)),
+            pltpu.SemaphoreType.DMA((SIDE,)),
+        ],
         flops=2 * 10**9,
     ))
     flat[0], folded[0] = together(flat[0], folded[0])
@@ -849,8 +883,14 @@
             cosine,
             sine,
         ],
-        specs=[smem] + [vmem] * 14,
-        scratch=[pltpu.VMEM((length, width), bf16), pltpu.VMEM((length, width), f32)],
+        specs=[smem] + [vmem] * 6 + [anywhere] * 5 + [vmem] + [anywhere] * 2,
+        scratch=[
+            pltpu.VMEM((length, width), bf16),
+            pltpu.VMEM((length, width), f32),
+            *[pltpu.VMEM((length, width), bf16)] * 4,
+            *[pltpu.VMEM((length, LANES), f32)] * 3,
+            pltpu.SemaphoreType.DMA((7,)),
+        ],
         flops=12 * 10**9,
     )
     grads_in = direct_swap(grads_out, line_shift)

time: 410 us -> 410 us (level)
  no operation moved by 1% of the time
where the time goes in v5:
time: 410 us; the launch traced here: 405 us
  Pallas kernels  151 us (37%)
  waiting for transfers between devices  108 us (26%)
  starting transfers between devices  105 us (26%)
  local copies, waits for them, and re-layouts  20.1 us (5%)
  other arithmetic  19.4 us (5%)
    pallas_call x19, Pallas kernels, call(): pl.pallas_call(kernel, out_shape=out_shapes, in_specs=specs or [whole] *...  151 us
    ppermute x33, waiting for transfers between devices, plane_shift(): return lax.ppermute(values, PLANE, pairs)  60.6 us
    ppermute x33, starting transfers between devices, plane_shift(): return lax.ppermute(values, PLANE, pairs)  53.4 us
    ppermute x24, waiting for transfers between devices, line_shift(): return lax.ppermute(values, 'head', pairs)  32.3 us
    ppermute x24, starting transfers between devices, line_shift(): return lax.ppermute(values, 'head', pairs)  28.6 us
    all_to_all x4, starting transfers between devices, swap_all(): return lax.all_to_all(values, axes, 0, 0, tiled=True)  22 us
    all_to_all x4, waiting for transfers between devices, swap_all(): return lax.all_to_all(values, axes, 0, 0, tiled=True)  14.9 us
    unnamed x97, local copies, waits for them, and re-layouts  13.7 us
  transfers between devices with their start and end apart: 67, of which 25 were waited for; matrix products, arithmetic and copies ran while one was open for 7% of the time, Pallas kernels for 35%

profile of v5, /device:TPU:4, one launch (start us, length us, event | category | flops | bytes accessed | tf_op | source)
XLA Modules:
  0.0 404.7 jit_solution(12705206841550610823)
XLA Ops:
  30.3 4.4 %all-to-all-start = ((bf16[4,128,1024]{2,1,0:T(8,128)(2,1)}), bf16[4,128,1024]{2,1,0:T(8,128)(2,1)S(1)}, u32[]{:S(2)}, u32[]{:S(2)}) async-start(bf16[4,128,1024]{2,1,0:T(8,128)(2,1)} %broadcast_in_dim.28), calls=%async_computation | async-start | bytes 2097152 | tf_op jit(solution)/shard_map/all_to_all | solution.py:110
  34.7 12.3 %shard_map.229 = (bf16[1024,1024]{1,0:T(8,128)(2,1)}, bf16[1024,256]{1,0:T(8,128)(2,1)}, bf16[1024,256]{1,0:T(8,128)(2,1)}, bf16[1024,256]{1,0:T(8,128)(2,1)}, b...) custom-call(s32[4]{0:T(128)} %pad_add_fusion.at, ...), custom_call_target="tpu_custom_call" | custom-call | flops 12000000000 | bytes 9445392 | tf_op jit(solution)/shard_map/pallas_call | solution.py:39
  53.4 3.6 collective-permute-done.9.mixed_1
  66.9 5.7 %collective-permute-done.13 = bf16[256,1024]{1,0:T(8,128)(2,1)S(1)} collective-permute-done((bf16[256,1024]{1,0:T(8,128)(2,1)S(1)}, bf16[256,1024]{1,0:T(8,128)(2,1)S(1)}, u32[]{:S(2)}, u32[]{:S(2)}) %collective-permute-start.13) | collective-permute-done | bytes 524320 | tf_op jit(solution)/shard_map/ppermute | solution.py:72
  76.5 4.7 %collective-permute-done.16 = bf16[256,1024]{1,0:T(8,128)(2,1)S(1)} collective-permute-done((bf16[256,1024]{1,0:T(8,128)(2,1)S(1)}, bf16[256,1024]{1,0:T(8,128)(2,1)S(1)}, u32[]{:S(2)}, u32[]{:S(2)}) %collective-permute-start.16) | collective-permute-done | bytes 524320 | tf_op jit(solution)/shard_map/ppermute | solution.py:72
  92.3 4.4 %all-to-all-start.1 = ((bf16[4,512,512]{2,1,0:T(8,128)(2,1)}), bf16[4,512,512]{2,1,0:T(8,128)(2,1)}, u32[]{:S(2)}, u32[]{:S(2)}) async-start(bf16[4,512,512]{2,1,0:T(8,128)(2,1)} %broadcast_in_dim.52), calls=%async_computation.1 | async-start | bytes 4194304 | tf_op jit(solution)/shard_map/all_to_all | solution.py:110
  105.5 14.4 %shard_map.231 = (bf16[544,1024]{1,0:T(8,128)(2,1)}, bf16[544,1024]{1,0:T(8,128)(2,1)}, f32[32,256]{1,0:T(8,128)}, bf16[1024,1024]{1,0:T(8,128)(2,1)}, bf16[2,38...) custom-call(s32[4]{0:T(128)} %pad_add_fusion.at, ...), custom_call_target="tpu_custom_call" | custom-call | flops 14000000000 | bytes 20742160 | tf_op jit(solution)/shard_map/pallas_call | solution.py:39
  122.5 4.2 %collective-permute-done.26.g_a = bf16[272,1024]{1,0:T(8,128)(2,1)} collective-permute-done((bf16[272,1024]{1,0:T(8,128)(2,1)}, bf16[272,1024]{1,0:T(8,128)(2,1)}, u32[]{:S(2)}, u32[]{:S(2)}) %collective-permute-start.26) | collective-permute-done | bytes 557088 | tf_op jit(solution)/shard_map/ppermute | solution.py:72
  126.7 5.6 %collective-permute-done.25.x_a = bf16[256,1024]{1,0:T(8,128)(2,1)} collective-permute-done((bf16[256,1024]{1,0:T(8,128)(2,1)S(1)}, bf16[256,1024]{1,0:T(8,128)(2,1)}, u32[]{:S(2)}, u32[]{:S(2)}) %collective-permute-start.25) | collective-permute-done | bytes 524320 | tf_op jit(solution)/shard_map/ppermute | solution.py:72
  132.3 14.4 %shard_map.232 = (bf16[544,1024]{1,0:T(8,128)(2,1)}, bf16[544,1024]{1,0:T(8,128)(2,1)}, f32[32,256]{1,0:T(8,128)}, bf16[1024,1024]{1,0:T(8,128)(2,1)}, bf16[2,38...) custom-call(s32[4]{0:T(128)} %pad_add_fusion.at, ...), custom_call_target="tpu_custom_call" | custom-call | flops 14000000000 | bytes 20742160 | tf_op jit(solution)/shard_map/pallas_call | solution.py:39
  150.8 14.3 %shard_map.233 = (bf16[544,1024]{1,0:T(8,128)(2,1)}, bf16[544,1024]{1,0:T(8,128)(2,1)}, f32[32,256]{1,0:T(8,128)}, bf16[1024,1024]{1,0:T(8,128)(2,1)}, bf16[2,38...) custom-call(s32[4]{0:T(128)} %pad_add_fusion.at, ...), custom_call_target="tpu_custom_call" | custom-call | flops 14000000000 | bytes 20742160 | tf_op jit(solution)/shard_map/pallas_call | solution.py:39
  167.5 14.5 %shard_map.234 = (bf16[544,1024]{1,0:T(8,128)(2,1)}, bf16[544,1024]{1,0:T(8,128)(2,1)}, f32[32,256]{1,0:T(8,128)}, bf16[1024,1024]{1,0:T(8,128)(2,1)}, bf16[2,38...) custom-call(s32[4]{0:T(128)} %pad_add_fusion.at, ...), custom_call_target="tpu_custom_call" | custom-call | flops 14000000000 | bytes 20742160 | tf_op jit(solution)/shard_map/pallas_call | solution.py:39
  188.8 9.0 %collective-permute-done.32.after_lo = bf16[544,1024]{1,0:T(8,128)(2,1)S(1)} collective-permute-done((bf16[544,1024]{1,0:T(8,128)(2,1)}, bf16[544,1024]{1,0:T(8,128)(2,1)S(1)}, u32[]{:S(2)}, u32[]{:S(2)}) %collective-permute-start.32) | collective-permute-done | bytes 1114144 | tf_op jit(solution)/shard_map/ppermute | solution.py:72
  197.8 3.9 collective-permute-done.30.before_lo
  201.8 8.0 %collective-permute-done.34.after_hi = bf16[544,1024]{1,0:T(8,128)(2,1)S(1)} collective-permute-done((bf16[544,1024]{1,0:T(8,128)(2,1)S(1)}, bf16[544,1024]{1,0:T(8,128)(2,1)S(1)}, u32[]{:S(2)}, u32[]{:S(2)}) %collective-permute-start.34) | collective-permute-done | bytes 1114144 | tf_op jit(solution)/shard_map/ppermute | solution.py:72
  210.8 4.4 %shard_map.235 = (bf16[272,1024]{1,0:T(8,128)(2,1)}, bf16[272,1024]{1,0:T(8,128)(2,1)}, bf16[272,1024]{1,0:T(8,128)(2,1)}, bf16[272,1024]{1,0:T(8,128)(2,1)}) custom-call(bf16[544,1024]{1,0:T(8,128)(2,1)} %get-tuple-element.183.own_lo, bf16[544,1024]{1,0:T(8,128)(2,1)} %get-tuple-element.184.own_hi, bf16[544,1024]{1,0:T(8,128)(2,1)} %copy-done.30, ...), custom_call_target="tpu_custom_call" | custom-call | flops 2000000000 | bytes 8912896 | tf_op jit(solution)/shard_map/pallas_call | solution.py:39
  218.3 11.0 %shard_map.236.own = bf16[1536,1024]{1,0:T(8,128)(2,1)} custom-call(bf16[2,384,1024]{2,1,0:T(8,128)(2,1)} %get-tuple-element.232.refs_0_, bf16[2,384,1024]{2,1,0:T(8,128)(2,1)} %get-tuple-element.208.refs_1_, bf16[2,384,512]{2,1,0:T(8,128)(2,1)} %get-tuple-element.209.refs_2_, bf16[2,384,1024]{2,1,0:T(8,128)(2,1)} %get-tuple-element.210.refs_3_, ...), custom_call_target="tpu_custom_call" | custom-call | flops 10000000000 | bytes 25165824 | tf_op jit(solution)/shard_map/pallas_call | solution.py:39
  229.3 4.6 %collective-permute-done.37.term_3 = bf16[272,1024]{1,0:T(8,128)(2,1)S(1)} collective-permute-done((bf16[272,1024]{1,0:T(8,128)(2,1)}, bf16[272,1024]{1,0:T(8,128)(2,1)S(1)}, u32[]{:S(2)}, u32[]{:S(2)}) %collective-permute-start.37) | collective-permute-done | bytes 557088 | tf_op jit(solution)/shard_map/ppermute | solution.py:72
  241.3 10.9 %shard_map.238 = bf16[1536,1024]{1,0:T(8,128)(2,1)} custom-call(bf16[2,384,1024]{2,1,0:T(8,128)(2,1)} %get-tuple-element.232.refs_0_, bf16[2,384,1024]{2,1,0:T(8,128)(2,1)} %get-tuple-element.208.refs_1_, bf16[2,384,512]{2,1,0:T(8,128)(2,1)} %get-tuple-element.209.refs_2_, bf16[2,384,1024]{2,1,0:T(8,128)(2,1)} %get-tuple-element.210.refs_3_, ...), custom_call_target="tpu_custom_call" | custom-call | flops 10000000000 | bytes 25165824 | tf_op jit(solution)/shard_map/pallas_call | solution.py:39
  258.3 6.3 %shard_map.239 = (bf16[384,1024]{1,0:T(8,128)(2,1)}, bf16[384,1024]{1,0:T(8,128)(2,1)}, bf16[384,1024]{1,0:T(8,128)(2,1)}, bf16[384,1024]{1,0:T(8,128)(2,1)}) custom-call(s32[4]{0:T(128)} %pad_add_fusion.at, bf16[1536,1024]{1,0:T(8,128)(2,1)} %shard_map.236.own, bf16[1536,1024]{1,0:T(8,128)(2,1)} %collective-permute-done.40.sib), custom_call_target="tpu_custom_call" | custom-call | flops 3000000000 | bytes 9437200 | tf_op jit(solution)/shard_map/pallas_call | solution.py:39
  268.9 13.8 %shard_map.240 = (bf16[1024,512]{1,0:T(8,128)(2,1)}, bf16[256,512]{1,0:T(8,128)(2,1)}, bf16[256,512]{1,0:T(8,128)(2,1)}, bf16[256,512]{1,0:T(8,128)(2,1)}, bf16[256,512]{1,0:T(8,128)(2,1)}) custom-call(s32[4]{0:T(128)} %pad_add_fusion.at, bf16[304,1024]{1,0:T(8,128)(2,1)} %copy-done.2, bf16[304,1024]{1,0:T(8,128)(2,1)} %copy-done.23, ...), custom_call_target="tpu_custom_call" | custom-call | flops 12000000000 | bytes 8785936 | tf_op jit(solution)/shard_map/pallas_call | solution.py:39
  282.7 3.9 add_convert_fusion
  294.7 7.0 %shard_map.241 = bf16[32,64,512]{2,1,0:T(8,128)(2,1)} custom-call(s32[4]{0:T(128)} %pad_add_fusion.at, bf16[1024,1024]{1,0:T(8,128)(2,1)} %get-tuple-element.258.normed, bf16[1024,512]{1,0:T(8,128)(2,1)} %get-tuple-element.259.grads, bf16[1024,256]{1,0:T(8,128)(2,1)} %get-tuple-element.253.mixed_in.mixed, bf16[304,1024]{1,0:T(8,128)(2,1)} %copy-done.2, ...), custom_call_target="tpu_custom_call" | custom-call | flops 6000000000 | bytes 9310224 | tf_op jit(solution)/shard_map/pallas_call | solution.py:39
  303.3 5.2 %collective-permute-done.49.g_3 = bf16[256,512]{1,0:T(8,128)(2,1)S(1)} collective-permute-done((bf16[256,512]{1,0:T(8,128)(2,1)S(1)}, bf16[256,512]{1,0:T(8,128)(2,1)S(1)}, u32[]{:S(2)}, u32[]{:S(2)}) %collective-permute-start.49) | collective-permute-done | bytes 262176 | tf_op jit(solution)/shard_map/ppermute | solution.py:60
  309.2 7.1 %all-to-all-start.2 = ((bf16[32,64,512]{2,1,0:T(8,128)(2,1)}), bf16[32,64,512]{2,1,0:T(8,128)(2,1)S(1)}, u32[]{:S(2)}, u32[]{:S(2)}) async-start(bf16[32,64,512]{2,1,0:T(8,128)(2,1)} %shard_map.241), calls=%async_computation.2 | async-start | bytes 4194304 | tf_op jit(solution)/shard_map/all_to_all | solution.py:110
  316.3 5.6 %shard_map.242 = f32[256,1024]{1,0:T(8,128)} custom-call(s32[4]{0:T(128)} %pad_add_fusion.at, bf16[256,512]{1,0:T(8,128)(2,1)} %get-tuple-element.268.g_0, bf16[256,512]{1,0:T(8,128)(2,1)} %copy-done.43, bf16[256,512]{1,0:T(8,128)(2,1)} %copy-done.44, bf16[256,512]{1,0:T(8,128)(2,1)} %copy-done.45, bf16[4,512,512]{2,1,0:T(8,128)(2,1)} %all-to-all-done.1.weights, ...), custom_call_target="tpu_custom_call" | custom-call | flops 4000000000 | bytes 7868432 | tf_op jit(solution)/shard_map/pallas_call | solution.py:39
  322.0 4.4 %shard_map.243 = (bf16[256,1024]{1,0:T(8,128)(2,1)}, bf16[256,1024]{1,0:T(8,128)(2,1)}, bf16[256,1024]{1,0:T(8,128)(2,1)}, bf16[256,1024]{1,0:T(8,128)(2,1)}) custom-call(bf16[1024,1024]{1,0:T(8,128)(2,1)} %get-tuple-element.274.own, bf16[1024,1024]{1,0:T(8,128)(2,1)} %collective-permute-done.50.before, bf16[1024,1024]{1,0:T(8,128)(2,1)} %collective-permute-done.43.after_), custom_call_target="tpu_custom_call" | custom-call | flops 2000000000 | bytes 8388608 | tf_op jit(solution)/shard_map/pallas_call | solution.py:39
  329.1 13.8 %all-to-all-done.2.parts = bf16[32,64,512]{2,1,0:T(8,128)(2,1)S(1)} async-done(((bf16[32,64,512]{2,1,0:T(8,128)(2,1)}), bf16[32,64,512]{2,1,0:T(8,128)(2,1)S(1)}, u32[]{:S(2)}, u32[]{:S(2)}) %all-to-all-start.2) | async-done | bytes 2097184 | tf_op jit(solution)/shard_map/all_to_all | solution.py:110
  342.9 4.2 %collective-permute-done.52 = bf16[256,1024]{1,0:T(8,128)(2,1)} collective-permute-done((bf16[256,1024]{1,0:T(8,128)(2,1)}, bf16[256,1024]{1,0:T(8,128)(2,1)}, u32[]{:S(2)}, u32[]{:S(2)}) %collective-permute-start.52) | collective-permute-done | bytes 524320 | tf_op jit(solution)/shard_map/ppermute | solution.py:72
  351.6 6.1 %all-to-all-start.3 = ((bf16[32,64,512]{2,1,0:T(8,128)(2,1)}), bf16[32,64,512]{2,1,0:T(8,128)(2,1)S(1)}, u32[]{:S(2)}, u32[]{:S(2)}) async-start(bf16[32,64,512]{2,1,0:T(8,128)(2,1)} %get-tuple-element.281), calls=%async_computation.3 | async-start | bytes 4194304 | tf_op jit(solution)/shard_map/all_to_all | solution.py:110
  366.8 14.8 %collective-permute-done.56.from_before = bf16[384,1024]{1,0:T(8,128)(2,1)S(1)} collective-permute-done((bf16[384,1024]{1,0:T(8,128)(2,1)}, bf16[384,1024]{1,0:T(8,128)(2,1)S(1)}, u32[]{:S(2)}, u32[]{:S(2)}) %collective-permute-start.56) | collective-permute-done | bytes 786464 | tf_op jit(solution)/shard_map/ppermute | solution.py:60
  394.7 4.9 %shard_map.246 = (f32[1,1024,512]{2,1,0:T(8,128)}, f32[1,1024,512]{2,1,0:T(8,128)}, f32[1,512,1024]{2,1,0:T(8,128)}) custom-call(s32[4]{0:T(128)} %pad_add_fusion.at, bf16[384,1024]{1,0:T(8,128)(2,1)} %shard_map.245.own, bf16[384,1024]{1,0:T(8,128)(2,1)} %copy-done.22, bf16[192,1024]{1,0:T(8,128)(2,1)} %copy-done.35, ...), custom_call_target="tpu_custom_call" | custom-call | flops 4000000000 | bytes 9437200 | tf_op jit(solution)/shard_map/pallas_call | solution.py:39
  (248 shorter events, 151.6 us)
Async XLA Ops:
  0.6 18.4 %collective-permute-start = (bf16[256,1024]{1,0:T(8,128)(2,1)}, bf16[256,1024]{1,0:T(8,128)(2,1)S(1)}, u32[]{:S(2)}, u32[]{:S(2)}) collective-permute-start(bf16[256,1024]{1,0:T(8,128)(2,1)} %tokens.3), channel_id=1, source_target_pairs={{0,1},{1,2},{2,3},{3,0},{4,5},{5,6},{6,7},{7,4},{8,9},{9,10},{10,1... | collective-permute-start | bytes 1572872 | tf_op jit(solution)/shard_map/ppermute | solution.py:60
  8.5 17.3 %collective-permute-start.5 = (bf16[272,1024]{1,0:T(8,128)(2,1)}, bf16[272,1024]{1,0:T(8,128)(2,1)S(1)}, u32[]{:S(2)}, u32[]{:S(2)}) collective-permute-start(bf16[272,1024]{1,0:T(8,128)(2,1)} %fusion.1.g_a), channel_id=1, source_target_pairs={{0,64},{4,20},{8,72},{12,28},{16,80},{20,4},{24,88},{28,12},{32,96... | collective-permute-start | bytes 1671176 | tf_op jit(solution)/shard_map/ppermute | solution.py:72
  28.3 23.0 %collective-permute-start.7 = (bf16[816,1024]{1,0:T(8,128)(2,1)}, bf16[816,1024]{1,0:T(8,128)(2,1)}, u32[]{:S(2)}, u32[]{:S(2)}) collective-permute-start(bf16[816,1024]{1,0:T(8,128)(2,1)} %pad_maximum_fusion.g_b), channel_id=1, source_target_pairs={{0,8},{4,36},{8,16},{12,44},{16,24},{20,52},{24,0},{28,60},{32,40}... | collective-permute-start | bytes 5013512 | tf_op jit(solution)/shard_map/ppermute | solution.py:72
  29.5 22.7 %collective-permute-start.8 = (bf16[816,1024]{1,0:T(8,128)(2,1)}, bf16[816,1024]{1,0:T(8,128)(2,1)}, u32[]{:S(2)}, u32[]{:S(2)}) collective-permute-start(bf16[816,1024]{1,0:T(8,128)(2,1)} %pad_maximum_fusion.g_b), channel_id=1, source_target_pairs={{0,24},{4,100},{8,0},{12,108},{16,8},{20,116},{24,16},{28,124},{32... | collective-permute-start | bytes 5013512 | tf_op jit(solution)/shard_map/ppermute | solution.py:72
  30.3 17.8 %all-to-all-start = ((bf16[4,128,1024]{2,1,0:T(8,128)(2,1)}), bf16[4,128,1024]{2,1,0:T(8,128)(2,1)S(1)}, u32[]{:S(2)}, u32[]{:S(2)}) async-start(bf16[4,128,1024]{2,1,0:T(8,128)(2,1)} %broadcast_in_dim.28), calls=%async_computation | async-start | bytes 2097152 | tf_op jit(solution)/shard_map/all_to_all | solution.py:110
  82.1 20.7 %collective-permute-start.21 = (bf16[768,1024]{1,0:T(8,128)(2,1)}, bf16[768,1024]{1,0:T(8,128)(2,1)}, u32[]{:S(2)}, u32[]{:S(2)}) collective-permute-start(bf16[768,1024]{1,0:T(8,128)(2,1)} %constant_dynamic-update-slice_fusion.x_b), channel_id=1, source_target_pairs={{0,24},{4,100},{8,0},{12,108},{16,8},{20,116},{24,16},{28,124},{32... | collective-permute-start | bytes 4718600 | tf_op jit(solution)/shard_map/ppermute | solution.py:72
  86.8 33.2 %collective-permute-start.22 = (bf16[768,1024]{1,0:T(8,128)(2,1)}, bf16[768,1024]{1,0:T(8,128)(2,1)}, u32[]{:S(2)}, u32[]{:S(2)}) collective-permute-start(bf16[768,1024]{1,0:T(8,128)(2,1)} %constant_dynamic-update-slice_fusion.x_b), channel_id=1, source_target_pairs={{0,8},{4,36},{8,16},{12,44},{16,24},{20,52},{24,0},{28,60},{32,40}... | collective-permute-start | bytes 4718600 | tf_op jit(solution)/shard_map/ppermute | solution.py:72
  90.7 31.8 %collective-permute-start.24 = (bf16[816,1024]{1,0:T(8,128)(2,1)}, bf16[816,1024]{1,0:T(8,128)(2,1)}, u32[]{:S(2)}, u32[]{:S(2)}) collective-permute-start(bf16[816,1024]{1,0:T(8,128)(2,1)} %collective-permute-done.8.g_b), channel_id=1, source_target_pairs={{0,24},{4,100},{8,0},{12,108},{16,8},{20,116},{24,16},{28,124},{32... | collective-permute-start | bytes 5013512 | tf_op jit(solution)/shard_map/ppermute | solution.py:72
  92.3 54.4 %all-to-all-start.1 = ((bf16[4,512,512]{2,1,0:T(8,128)(2,1)}), bf16[4,512,512]{2,1,0:T(8,128)(2,1)}, u32[]{:S(2)}, u32[]{:S(2)}) async-start(bf16[4,512,512]{2,1,0:T(8,128)(2,1)} %broadcast_in_dim.52), calls=%async_computation.1 | async-start | bytes 4194304 | tf_op jit(solution)/shard_map/all_to_all | solution.py:110
  96.8 29.9 %collective-permute-start.26 = (bf16[272,1024]{1,0:T(8,128)(2,1)}, bf16[272,1024]{1,0:T(8,128)(2,1)}, u32[]{:S(2)}, u32[]{:S(2)}) collective-permute-start(bf16[272,1024]{1,0:T(8,128)(2,1)} %fusion.1.g_a), channel_id=1, source_target_pairs={{0,24},{4,100},{8,0},{12,108},{16,8},{20,116},{24,16},{28,124},{32... | collective-permute-start | bytes 1671176 | tf_op jit(solution)/shard_map/ppermute | solution.py:72
  98.4 33.9 %collective-permute-start.25 = (bf16[256,1024]{1,0:T(8,128)(2,1)S(1)}, bf16[256,1024]{1,0:T(8,128)(2,1)}, u32[]{:S(2)}, u32[]{:S(2)}) collective-permute-start(bf16[256,1024]{1,0:T(8,128)(2,1)S(1)} %get-tuple-element.175.x_a.inputs), channel_id=1, source_target_pairs={{0,24},{4,100},{8,0},{12,108},{16,8},{20,116},{24,16},{28,124},{32... | collective-permute-start | bytes 1572872 | tf_op jit(solution)/shard_map/ppermute | solution.py:72
  102.8 17.2 %collective-permute-start.23 = (bf16[272,1024]{1,0:T(8,128)(2,1)}, bf16[272,1024]{1,0:T(8,128)(2,1)S(1)}, u32[]{:S(2)}, u32[]{:S(2)}) collective-permute-start(bf16[272,1024]{1,0:T(8,128)(2,1)} %copy-done.32), channel_id=1, source_target_pairs={{0,8},{4,36},{8,16},{12,44},{16,24},{20,52},{24,0},{28,60},{32,40}... | collective-permute-start | bytes 1671176 | tf_op jit(solution)/shard_map/ppermute | solution.py:72
  119.9 29.7 %collective-permute-start.28 = (bf16[768,1024]{1,0:T(8,128)(2,1)}, bf16[768,1024]{1,0:T(8,128)(2,1)S(1)}, u32[]{:S(2)}, u32[]{:S(2)}) collective-permute-start(bf16[768,1024]{1,0:T(8,128)(2,1)} %collective-permute-done.21.x_b), channel_id=1, source_target_pairs={{0,24},{4,100},{8,0},{12,108},{16,8},{20,116},{24,16},{28,124},{32... | collective-permute-start | bytes 4718600 | tf_op jit(solution)/shard_map/ppermute | solution.py:72
  120.0 29.6 %collective-permute-start.27 = (bf16[256,1024]{1,0:T(8,128)(2,1)}, bf16[256,1024]{1,0:T(8,128)(2,1)}, u32[]{:S(2)}, u32[]{:S(2)}) collective-permute-start(bf16[256,1024]{1,0:T(8,128)(2,1)} %collective-permute-done.20.x_a), channel_id=1, source_target_pairs={{0,8},{4,36},{8,16},{12,44},{16,24},{20,52},{24,0},{28,60},{32,40}... | collective-permute-start | bytes 1572872 | tf_op jit(solution)/shard_map/ppermute | solution.py:72
  146.7 42.2 %collective-permute-start.31 = (bf16[544,1024]{1,0:T(8,128)(2,1)}, bf16[544,1024]{1,0:T(8,128)(2,1)}, u32[]{:S(2)}, u32[]{:S(2)}) collective-permute-start(bf16[544,1024]{1,0:T(8,128)(2,1)} %get-tuple-element.198), channel_id=1, source_target_pairs={{0,8},{4,36},{8,16},{12,44},{16,24},{20,52},{24,0},{28,60},{32,40}... | collective-permute-start | bytes 3342344 | tf_op jit(solution)/shard_map/ppermute | solution.py:72
  165.2 18.2 %collective-permute-start.29 = (bf16[544,1024]{1,0:T(8,128)(2,1)}, bf16[544,1024]{1,0:T(8,128)(2,1)}, u32[]{:S(2)}, u32[]{:S(2)}) collective-permute-start(bf16[544,1024]{1,0:T(8,128)(2,1)} %get-tuple-element.197), channel_id=1, source_target_pairs={{0,8},{4,36},{8,16},{12,44},{16,24},{20,52},{24,0},{28,60},{32,40}... | collective-permute-start | bytes 3342344 | tf_op jit(solution)/shard_map/ppermute | solution.py:72
  167.3 18.6 %collective-permute-start.33 = (bf16[544,1024]{1,0:T(8,128)(2,1)}, bf16[544,1024]{1,0:T(8,128)(2,1)S(1)}, u32[]{:S(2)}, u32[]{:S(2)}) collective-permute-start(bf16[544,1024]{1,0:T(8,128)(2,1)} %get-tuple-element.204), channel_id=1, source_target_pairs={{0,24},{4,100},{8,0},{12,108},{16,8},{20,116},{24,16},{28,124},{32... | collective-permute-start | bytes 3342344 | tf_op jit(solution)/shard_map/ppermute | solution.py:72
  186.4 23.3 %collective-permute-start.34 = (bf16[544,1024]{1,0:T(8,128)(2,1)S(1)}, bf16[544,1024]{1,0:T(8,128)(2,1)S(1)}, u32[]{:S(2)}, u32[]{:S(2)}) collective-permute-start(bf16[544,1024]{1,0:T(8,128)(2,1)S(1)} %add_convert_fusion.1), channel_id=1, source_target_pairs={{0,24},{4,100},{8,0},{12,108},{16,8},{20,116},{24,16},{28,124},{32... | collective-permute-start | bytes 3342344 | tf_op jit(solution)/shard_map/ppermute | solution.py:72
  252.3 30.3 %collective-permute-start.44 = (bf16[1024,1024]{1,0:T(8,128)(2,1)}, bf16[1024,1024]{1,0:T(8,128)(2,1)}, u32[]{:S(2)}, u32[]{:S(2)}) collective-permute-start(bf16[1024,1024]{1,0:T(8,128)(2,1)} %get-tuple-element.245), channel_id=1, source_target_pairs={{0,8},{4,36},{8,16},{12,44},{16,24},{20,52},{24,0},{28,60},{32,40}... | collective-permute-start | bytes 6291464 | tf_op jit(solution)/shard_map/ppermute | solution.py:72
  256.1 33.0 %collective-permute-start.43 = (bf16[1024,1024]{1,0:T(8,128)(2,1)}, bf16[1024,1024]{1,0:T(8,128)(2,1)}, u32[]{:S(2)}, u32[]{:S(2)}) collective-permute-start(bf16[1024,1024]{1,0:T(8,128)(2,1)} %get-tuple-element.242), channel_id=1, source_target_pairs={{0,24},{4,100},{8,0},{12,108},{16,8},{20,116},{24,16},{28,124},{32... | collective-permute-start | bytes 6291464 | tf_op jit(solution)/shard_map/ppermute | solution.py:72
  264.6 22.0 %collective-permute-start.41 = (bf16[384,1024]{1,0:T(8,128)(2,1)}, bf16[384,1024]{1,0:T(8,128)(2,1)}, u32[]{:S(2)}, u32[]{:S(2)}) collective-permute-start(bf16[384,1024]{1,0:T(8,128)(2,1)} %get-tuple-element.235), channel_id=1, source_target_pairs={{0,1},{1,2},{2,3},{3,0},{4,5},{5,6},{6,7},{7,4},{8,9},{9,10},{10,1... | collective-permute-start | bytes 2359304 | tf_op jit(solution)/shard_map/ppermute | solution.py:60
  266.5 22.6 %collective-permute-start.42 = (bf16[384,1024]{1,0:T(8,128)(2,1)}, bf16[384,1024]{1,0:T(8,128)(2,1)}, u32[]{:S(2)}, u32[]{:S(2)}) collective-permute-start(bf16[384,1024]{1,0:T(8,128)(2,1)} %get-tuple-element.236), channel_id=1, source_target_pairs={{0,3},{1,0},{2,1},{3,2},{4,7},{5,4},{6,5},{7,6},{8,11},{9,8},{10,9... | collective-permute-start | bytes 2359304 | tf_op jit(solution)/shard_map/ppermute | solution.py:60
  289.1 27.2 %collective-permute-start.50 = (bf16[1024,1024]{1,0:T(8,128)(2,1)}, bf16[1024,1024]{1,0:T(8,128)(2,1)}, u32[]{:S(2)}, u32[]{:S(2)}) collective-permute-start(bf16[1024,1024]{1,0:T(8,128)(2,1)} %add_convert_fusion), channel_id=1, source_target_pairs={{0,8},{4,36},{8,16},{12,44},{16,24},{20,52},{24,0},{28,60},{32,40}... | collective-permute-start | bytes 6291464 | tf_op jit(solution)/shard_map/ppermute | solution.py:72
  292.3 24.0 %collective-permute-start.51 = (bf16[4,512,512]{2,1,0:T(8,128)(2,1)}, bf16[4,512,512]{2,1,0:T(8,128)(2,1)}, u32[]{:S(2)}, u32[]{:S(2)}) collective-permute-start(bf16[4,512,512]{2,1,0:T(8,128)(2,1)} %all-to-all-done.1.weights), channel_id=1, source_target_pairs={{0,4},{4,0},{1,5},{5,1},{2,6},{6,2},{3,7},{7,3},{8,12},{12,8},{9,1... | collective-permute-start | bytes 6291464 | tf_op jit(solution)/shard_map/ppermute | solution.py:80
  309.2 33.7 %all-to-all-start.2 = ((bf16[32,64,512]{2,1,0:T(8,128)(2,1)}), bf16[32,64,512]{2,1,0:T(8,128)(2,1)S(1)}, u32[]{:S(2)}, u32[]{:S(2)}) async-start(bf16[32,64,512]{2,1,0:T(8,128)(2,1)} %shard_map.241), calls=%async_computation.2 | async-start | bytes 4194304 | tf_op jit(solution)/shard_map/all_to_all | solution.py:110
  326.4 20.7 %collective-permute-start.52 = (bf16[256,1024]{1,0:T(8,128)(2,1)}, bf16[256,1024]{1,0:T(8,128)(2,1)}, u32[]{:S(2)}, u32[]{:S(2)}) collective-permute-start(bf16[256,1024]{1,0:T(8,128)(2,1)} %get-tuple-element.278), channel_id=1, source_target_pairs={{0,96},{4,28},{8,104},{12,4},{16,112},{20,12},{24,120},{28,20},{32... | collective-permute-start | bytes 1572872 | tf_op jit(solution)/shard_map/ppermute | solution.py:72
  329.1 19.2 %collective-permute-start.53 = (bf16[256,1024]{1,0:T(8,128)(2,1)}, bf16[256,1024]{1,0:T(8,128)(2,1)}, u32[]{:S(2)}, u32[]{:S(2)}) collective-permute-start(bf16[256,1024]{1,0:T(8,128)(2,1)} %get-tuple-element.279), channel_id=1, source_target_pairs={{0,32},{4,12},{8,40},{12,20},{16,48},{20,28},{24,56},{28,4},{32,64... | collective-permute-start | bytes 1572872 | tf_op jit(solution)/shard_map/ppermute | solution.py:72
  329.1 28.6 %collective-permute-start.55 = (bf16[384,1024]{1,0:T(8,128)(2,1)}, bf16[384,1024]{1,0:T(8,128)(2,1)}, u32[]{:S(2)}, u32[]{:S(2)}) collective-permute-start(bf16[384,1024]{1,0:T(8,128)(2,1)} %add_convert_fusion.3), channel_id=1, source_target_pairs={{0,1},{1,2},{2,3},{3,0},{4,5},{5,6},{6,7},{7,4},{8,9},{9,10},{10,1... | collective-permute-start | bytes 2359304 | tf_op jit(solution)/shard_map/ppermute | solution.py:60
  351.6 48.0 %all-to-all-start.3 = ((bf16[32,64,512]{2,1,0:T(8,128)(2,1)}), bf16[32,64,512]{2,1,0:T(8,128)(2,1)S(1)}, u32[]{:S(2)}, u32[]{:S(2)}) async-start(bf16[32,64,512]{2,1,0:T(8,128)(2,1)} %get-tuple-element.281), calls=%async_computation.3 | async-start | bytes 4194304 | tf_op jit(solution)/shard_map/all_to_all | solution.py:110
  360.6 21.0 %collective-permute-start.56 = (bf16[384,1024]{1,0:T(8,128)(2,1)}, bf16[384,1024]{1,0:T(8,128)(2,1)S(1)}, u32[]{:S(2)}, u32[]{:S(2)}) collective-permute-start(bf16[384,1024]{1,0:T(8,128)(2,1)} %shard_map.245.own), channel_id=1, source_target_pairs={{0,1},{1,2},{2,3},{3,0},{4,5},{5,6},{6,7},{7,4},{8,9},{9,10},{10,1... | collective-permute-start | bytes 2359304 | tf_op jit(solution)/shard_map/ppermute | solution.py:60
  360.6 21.0 %collective-permute-start.57 = (bf16[384,1024]{1,0:T(8,128)(2,1)}, bf16[384,1024]{1,0:T(8,128)(2,1)S(1)}, u32[]{:S(2)}, u32[]{:S(2)}) collective-permute-start(bf16[384,1024]{1,0:T(8,128)(2,1)} %shard_map.245.own), channel_id=1, source_target_pairs={{0,3},{1,0},{2,1},{3,2},{4,7},{5,4},{6,5},{7,6},{8,11},{9,8},{10,9... | collective-permute-start | bytes 2359304 | tf_op jit(solution)/shard_map/ppermute | solution.py:60
  363.8 26.1 %collective-permute-start.54 = (bf16[256,1024]{1,0:T(8,128)(2,1)S(1)}, bf16[256,1024]{1,0:T(8,128)(2,1)S(1)}, u32[]{:S(2)}, u32[]{:S(2)}) collective-permute-start(bf16[256,1024]{1,0:T(8,128)(2,1)S(1)} %copy-done.34), channel_id=1, source_target_pairs={{0,64},{4,20},{8,72},{12,28},{16,80},{20,4},{24,88},{28,12},{32,96... | collective-permute-start | bytes 1572872 | tf_op jit(solution)/shard_map/ppermute | solution.py:72
  (81 other events, 843.6 us)
